TPU v7x, 128 devices: a whole 4x4x4 slice. The times are simulated.
128 devices in a mesh: dp: 16 (over x, y), pipe: 8 (over z, core).
Axes of the slice: x: 4, y: 4, z: 4, core: 2. Of those that a mesh axis runs over, the one named last changes fastest.
Arguments:
- layer_input: bfloat16 [8, 8192, 8192], P('pipe', 'dp')
- value_grad: bfloat16 [8, 8192, 1024], P('pipe', 'dp')
- master_weight: float32 [8, 8192, 1024], P('pipe', 'dp'), may hold values from -0.75 to 0.75
- moment_one: float32 [8, 8192, 1024], P('pipe', 'dp'), may hold values from -1.5 to 1.5
- moment_two: float32 [8, 8192, 1024], P('pipe', 'dp'), may hold values from 0.001 to 0.05
- overflow_flags: int32 [8, 16], P('pipe', 'dp'), may hold values from 0 to 1, as said below
Outputs:
- new_weight: float32 [8, 8192, 1024], P('pipe', 'dp')
- new_moment_one: float32 [8, 8192, 1024], P('pipe', 'dp')
- new_moment_two: float32 [8, 8192, 1024], P('pipe', 'dp')
Inputs may be any that keep to these rules, and one draw needn't show every extreme that they name: `overflow_flags`: 1 marks an overflow; in every draw between one and 4 sections hold a mark, each of them on one or more ranks.
All inputs are finite; a program needn't handle non-finite values.
Results may differ from a plain program's by a relative error of at most 0.0003.
Values may be sent and summed in bfloat16 or wider, within the bound.
No kernel may reach another device: no remote copies, remote signals or barrier semaphores. Data moves between devices by JAX's collectives and lax.ppermute only.
A program may use at most 128 MiB of HBM per device.

v0:
```python
import math

import jax
import jax.numpy as jnp
from jax import lax
from jax.sharding import PartitionSpec as P

D = 8192
KV = 1024


def entering(value, axis, join, neutral):
    count, mine = (lax.axis_size(axis), lax.axis_index(axis))
    pieces = lax.all_gather(value, axis)
    running = jnp.full_like(value, 0) + jnp.asarray(neutral, value.dtype)

    def lap(position, running):
        longer = join(running, pieces[position])
        return jnp.where(position < mine, longer, running)

    return lax.fori_loop(0, count - 1, lap, running)


def broadcast(block, axis, source):
    block = jnp.where(lax.axis_index(axis) == source, block, jnp.zeros_like(block))
    return lax.psum(block, axis)


def add_pair(earlier, later):
    return earlier + later


def per_device(layer_input, value_grad, master_weight, moment_one, moment_two, overflow_flags):
    inputs_local = layer_input[0]
    grads_local = value_grad[0]
    gradient = lax.psum_scatter(
        lax.dot_general(
            inputs_local, grads_local, (((0,), (0,)), ((), ())), preferred_element_type=jnp.float32
        ),
        "dp",
        scatter_dimension=0,
        tiled=True,
    )
    own_squares = jnp.sum(gradient * gradient)
    own_flag = (overflow_flags[0, 0] != 0).astype(jnp.float32)
    section_count = lax.axis_size("pipe")
    section_squares, section_flags = lax.psum((own_squares, own_flag), "dp")
    keep = section_flags == 0.0
    masked = jnp.where(keep, section_squares, jnp.float32(0.0))
    before = entering(masked, "pipe", add_pair, jnp.float32(0.0))
    total = broadcast(before + masked, "pipe", section_count - 1)
    bound = 0.5 * math.sqrt(D * KV * section_count)
    clip = jnp.minimum(jnp.float32(1.0), bound / (jnp.sqrt(total) + 1e-06))
    weight_old = master_weight[0]
    first_old = moment_one[0]
    second_old = moment_two[0]
    scaled = clip * gradient
    first = 0.9 * first_old + 0.1 * scaled
    second = 0.95 * second_old + 0.05 * scaled * scaled
    updated = weight_old - 0.02 * (first / (jnp.sqrt(second) + 1e-08) + 0.1 * weight_old)
    new_weight = jnp.where(keep, updated, weight_old)
    new_first = jnp.where(keep, first, first_old)
    new_second = jnp.where(keep, second, second_old)
    return (new_weight[None], new_first[None], new_second[None])


def solution(mesh):
    placed = (
        P("pipe", "dp", None),
        P("pipe", "dp", None),
        P("pipe", "dp", None),
        P("pipe", "dp", None),
        P("pipe", "dp", None),
        P("pipe", "dp"),
    )
    return jax.shard_map(
        per_device,
        mesh=mesh,
        in_specs=placed,
        out_specs=(P("pipe", "dp", None), P("pipe", "dp", None), P("pipe", "dp", None)),
        check_vma=False,
    )
```

profile of v0, /device:TPU:1, one launch (start us, length us, event | category | flops | bytes accessed | tf_op | source)
XLA Modules:
  0.0 318.6 jit_solution(7808148041896183297)
XLA Ops:
  7.2 0.0 copy-start
  7.2 0.0 reduce-scatter.2.cloned.1.call-start
  7.2 1.2 copy-done
  8.4 18.7 %fusion = f32[8192,1024]{1,0:T(8,128)} fusion(bf16[1,512,8192]{2,1,0:T(8,128)(2,1)} %param.8, bf16[1,512,1024]{2,1,0:T(8,128)(2,1)S(1)} %copy-done), kind=kOutput, calls=%fused_computation | convolution fusion | flops 8589934592 | bytes 42991616 | tf_op jit(solution)/shard_map/dot_general | solution.py:37
  27.1 0.0 copy-start.2
  27.1 0.0 reduce-scatter.2.cloned.1.call-update
  27.8 0.0 copy-done.2
  27.8 0.6 dynamic-slice
  28.4 196.8 %reduce-scatter.2.cloned.1.call-done = f32[512,1024]{1,0:T(8,128)} async-done(((f32[8192,1024]{1,0:T(8,128)}), f32[512,1024]{1,0:T(8,128)}) %reduce-scatter.2.cloned.1.call-update) | async-done | bytes 2097168 | tf_op jit(solution)/shard_map/reduce_scatter | solution.py:36
  225.2 0.0 copy-start.1
  225.2 2.9 multiply_reduce_fusion
  228.1 32.5 %all-reduce.1 = (f32[]{:T(128)}, f32[]{:T(128)}) all-reduce(f32[]{:T(128)} %bitcast.1, f32[]{:T(128)} %multiply_reduce_fusion), channel_id=1, replica_groups=mesh['dp'=16,'pipe'=8] {'dp'}, use_global_device_ids=true, to_apply=%region_0.0 | all-reduce | flops 2 | bytes 16 | tf_op jit(solution)/shard_map/psum | solution.py:47
  261.8 0.7 dynamic-update-slice
  262.5 19.9 %all-reduce = f32[8]{0:T(128)S(1)} all-reduce(f32[8]{0:T(128)S(1)} %dynamic-update-slice), channel_id=1, replica_groups=mesh['dp'=16,'pipe'=8] {'pipe'}, use_global_device_ids=true, to_apply=%add | all-reduce | flops 8 | bytes 64
  282.4 8.1 %while.13 = (s32[]{:T(128)}, f32[]{:T(128)}, s32[]{:T(128)}, f32[8]{0:T(128)S(1)}, s32[]{:T(128)}) while((s32[]{:T(128)}, f32[]{:T(128)}, s32[]{:T(128)}, f32[8]{0:T(128)S(1)}, s32[]{:T(128)}) %tuple.34), condition=%wide.region_5.6_spmd, body=%wide.region_4.5_spmd.sunk | while | flops 5 | bytes 107 | solution.py:21
  282.4 0.6 dynamic_slice.8
  283.6 0.6 dynamic_slice.8
  284.8 0.6 dynamic_slice.8
  285.9 0.6 dynamic_slice.8
  287.1 0.6 dynamic_slice.8
  288.2 0.6 dynamic_slice.8
  289.4 0.6 dynamic_slice.8
  290.6 12.8 %psum.23 = f32[]{:T(128)} all-reduce(f32[]{:T(128)S(6)} %select_n.37), channel_id=1, replica_groups=mesh['dp'=16,'pipe'=8] {'pipe'}, use_global_device_ids=true, to_apply=%region_6.7 | all-reduce | flops 1 | bytes 8 | tf_op jit(solution)/shard_map/psum | solution.py:26
  304.1 0.0 copy-done.1
  304.2 7.5 %fusion.4 = (f32[1,512,1024]{2,1,0:T(8,128)}, f32[1,512,1024]{2,1,0:T(8,128)}, f32[1,512,1024]{2,1,0:T(8,128)}) fusion(f32[1,512,1024]{2,1,0:T(8,128)} %param.12, f32[512,1024]{1,0:T(8,128)S(1)} %copy-done.1, f32[]{:T(128)S(6)} %min_shard_map.3, pred[]{:T(512)S(6)} %eq.6, f32[1,512,1024]{2,1,0:T(8,128)} %param.11, f32[1,512,1024]{2,1,0:T(8,128)} %param.10), kind=kLoop, calls=%fused_computation.8 | loop fusion | flops 8912896 | bytes 14680069 | tf_op jit(solution)/shard_map/broadcast_in_dim | solution.py:64
  (1 shorter events, 0.0 us)
Async XLA Ops:
  7.2 1.2 copy-start
  7.2 218.0 %reduce-scatter.2.cloned.1.call-start = ((), (), s32[]{:S(2)}) async-start(), calls=%async_computation.1 | async-start | bytes 35651584 | tf_op jit(solution)/shard_map/reduce_scatter | solution.py:36
  27.1 0.7 copy-start.2
  225.2 79.0 %copy-start.1 = (f32[512,1024]{1,0:T(8,128)S(1)}, f32[512,1024]{1,0:T(8,128)}, u32[]{:S(2)}) copy-start(f32[512,1024]{1,0:T(8,128)} %reduce-scatter.2.cloned.1.call-done) | copy-start | bytes 6291460
Sparse Core Ops, SparseCore 0:
  27.3 197.8 reduce-scatter.1
where the time goes:
time: 319 us
  waiting for transfers between devices  197 us (62%)
  blocking collectives  65.2 us (20%)
  matrix products  18.7 us (6%)
  between operations  16.7 us (5%)
  other arithmetic  10.4 us (3%)
  local copies, waits for them, and re-layouts  6.52 us (2%)
  loops' own time  4.08 us (1%)
    reduce_scatter x1, waiting for transfers between devices, per_device(): lax.psum_scatter(lax.dot_general(inputs_local, grads_local, (((0,), (0,))...  197 us
    psum x1, blocking collectives, per_device(): section_squares, section_flags = lax.psum((own_squares, own_flag), 'dp')  32.5 us
    unnamed x1, blocking collectives  19.9 us
    dot_general x1, matrix products, per_device(): lax.dot_general(inputs_local, grads_local, (((0,), (0,)), ((), ())), pref...  18.7 us
    psum x1, blocking collectives, broadcast(): return lax.psum(block, axis)  12.8 us
    broadcast_in_dim x1, other arithmetic, per_device(): return (new_weight[None], new_first[None], new_second[None])  7.55 us
  transfers between devices with their start and end apart: 1, of which 1 were waited for; matrix products, arithmetic and copies ran while one was open for 0% of the time, Pallas kernels for 0%

commit v1 on v0

v1 whole, which is shorter than its diff:
```python
import functools
import math

import jax
import jax.numpy as jnp
from jax import lax
from jax.experimental import pallas as pl
from jax.experimental.pallas import tpu as pltpu
from jax.sharding import PartitionSpec as P

D = 8192
KV = 1024
RANKS = 16
DEVICES = 128
PIPE = 8
TOK = 512
OWN = 512
COLS = 256
VARIANTS = 4
STEP = 128
KERNEL_VMEM = 14 << 20
UPDATE_VMEM = 60 << 20
TOP_POWER = 29.9985
SCALE_ROWS = 16

XA, XB, YA, YB = 4, 12, 1, 3
ORDERS = ((YA, YB, XB, XA), (YB, YA, XA, XB), (XA, XB, YB, YA), (XB, XA, YA, YB))
PAIRS = ((2, 3), (0, 1))


TRANSPOSED = (((0,), (0,)), ((), ()))


def masks_of(order, step):
    base = {0: order[0] ^ order[1], 1: order[0], 2: order[1], 3: 0}[step]
    return [base, base ^ order[3], base ^ order[2], base ^ order[2] ^ order[3]]


def decode(codes, scale):
    wide = codes.astype(jnp.float32)
    return wide * jnp.abs(wide) * scale


def scale_of(step_code):
    power = step_code * (1.0 / 64.0) - TOP_POWER
    return jnp.exp2(power), jnp.exp2(-power)


def columns_of(me_ref, mask):
    block = jnp.bitwise_xor(me_ref[0], mask)
    return pl.ds(pl.multiple_of(block * OWN, OWN), OWN)


def scales_of(received):
    return [
        scale_of(r[r.shape[0] - SCALE_ROWS :, :].astype(jnp.float32)[:1])[0]
        for r in received
    ]


def pieces(rows, body, start):
    def some(i, carry):
        return body(pl.multiple_of(i * STEP, STEP), carry)

    return lax.fori_loop(0, rows // STEP, some, start)


def largest_of(total):
    return jnp.max(jnp.abs(total), axis=0, keepdims=True)


def add_received(source, first, received, rows, sums):
    scales = scales_of([r for r, _ in received])

    def body(at, largest):
        total = source[pl.ds(first + at, STEP), :]
        for (r, begin), scale in zip(received, scales):
            total = total + decode(r[pl.ds(begin + at, STEP), :], scale)
        sums[pl.ds(at, STEP), :] = total
        return jnp.maximum(largest, largest_of(total))

    return pieces(rows, body, jnp.zeros((1, COLS), jnp.float32))


def encode(largest, sums, cols, blocks, out_ref):
    step_code = jnp.ceil(jnp.log2(jnp.maximum(largest, 1e-37)) * 64.0)
    step_code = jnp.clip(step_code, -90.0 * 64.0, 128.0 * 64.0)
    factor = scale_of(step_code)[1]
    rows = len(blocks) * OWN
    out_ref[rows : rows + SCALE_ROWS, :] = (
        jnp.broadcast_to(step_code, (SCALE_ROWS, COLS)).astype(jnp.int32).astype(jnp.int16)
    )
    for slot, block in enumerate(blocks):

        def body(at, _):
            scaled = sums[pl.ds(pl.multiple_of(block * OWN + at, STEP), STEP), cols] * factor
            rooted = scaled * lax.rsqrt(jnp.maximum(jnp.abs(scaled), 1e-12))
            whole = jnp.round(rooted).astype(jnp.int32)
            out_ref[pl.ds(slot * OWN + at, STEP), :] = whole.astype(jnp.int16)
            return 0

        pieces(OWN, body, 0)


def product(x_ref, me_ref, masks, g):
    x = jnp.concatenate([x_ref[0, :, columns_of(me_ref, mask)] for mask in masks], axis=1)
    return lax.dot_general(x, g, TRANSPOSED, preferred_element_type=jnp.float32)


def first_kernel(pair, me_ref, x_ref, g_ref, after_ref, *refs):
    outs, sums = refs[:2], refs[2]
    variants = PAIRS[pair]
    if pair == 0:
        total = lax.dot_general(
            x_ref[:, : 4 * OWN],
            x_ref[:, 4 * OWN :],
            TRANSPOSED,
            preferred_element_type=jnp.float32,
        )
        place = {XA ^ XB ^ y: jnp.bitwise_and(jnp.bitwise_xor(me_ref[0], y), 3) for y in range(4)}
    else:
        masks = masks_of(ORDERS[variants[0]], 0)
        cols = slice(variants[0] * COLS, (variants[1] + 1) * COLS)
        total = product(x_ref, me_ref, masks, g_ref[0, :, cols])
        place = {mask: slot for slot, mask in enumerate(masks)}
    sums[...] = total
    largest = largest_of(total)
    for half, v in enumerate(variants):
        cols = slice(half * COLS, (half + 1) * COLS)
        blocks = [place[mask] for mask in masks_of(ORDERS[v], 0)]
        encode(largest[:, cols], sums, cols, blocks, outs[half])


def mid_kernel(step, has, me_ref, x_ref, g_ref, *refs):
    received = refs[1 : 1 + VARIANTS * has]
    outs = refs[1 + VARIANTS * has :][:VARIANTS]
    sums = refs[-1]
    for v in range(VARIANTS):
        masks = masks_of(ORDERS[v], step)
        total = product(x_ref, me_ref, masks, g_ref[0, :, v * COLS : (v + 1) * COLS])
        into = outs[v] if step == 3 else sums
        into[...] = total
        largest = largest_of(total)
        if has:
            largest = add_received(into, 0, [(received[v], 0)], 4 * OWN, into)
        if step != 3:
            encode(largest, sums, slice(0, COLS), range(4), outs[v])


def late_kernel(count, arrivals, p_ref, *refs):
    received, out, sums = refs[:arrivals], refs[arrivals], refs[arrivals + 1]
    first = count * OWN
    largest = add_received(
        p_ref, first, [(r, first) for r in received], count * OWN, sums
    )
    encode(largest, sums, slice(0, COLS), range(count), out)


def finish_kernel(*refs):
    flag_ref = refs[0]
    grad_hbm, report_hbm, grad_ref, report_ref, sems = refs[-5:]
    copies = []
    acc = jnp.zeros((8, 128), jnp.float32)
    for v in range(VARIANTS):
        p_ref, *received = refs[1 + 4 * v : 5 + 4 * v]
        scales = scales_of(received)

        def body(at, acc):
            total = p_ref[pl.ds(at, STEP), :]
            for r, scale in zip(received, scales):
                total = total + decode(r[pl.ds(at, STEP), :], scale)
            grad_ref[pl.ds(at, STEP), v * COLS : (v + 1) * COLS] = total
            squared = total * total
            squared = squared[:, :128] + squared[:, 128:]
            return acc + jnp.sum(squared.reshape(STEP // 8, 8, 128), axis=0)

        acc = pieces(OWN, body, acc)
        cols = slice(v * COLS, (v + 1) * COLS)
        copies.append(
            pltpu.make_async_copy(grad_ref.at[:, cols], grad_hbm.at[:, cols], sems.at[v])
        )
        copies[-1].start()
    marked = jnp.where(flag_ref[0, 0] != 0, 1.0, 0.0)
    acc = acc + pltpu.roll(acc, 64, axis=1)
    lane = lax.broadcasted_iota(jnp.int32, (8, 128), 1)
    acc = jnp.where(lane < 64, jnp.sum(acc, axis=0, keepdims=True), marked)
    report_ref[...] = jnp.broadcast_to(acc[:1][None], (DEVICES, 1, 128))
    copies.append(pltpu.make_async_copy(report_ref, report_hbm, sems.at[VARIANTS]))
    copies[-1].start()
    for copy in copies:
        copy.wait()


WHOLE = pl.BlockSpec(memory_space=pltpu.VMEM)
LEFT = pl.BlockSpec(memory_space=pl.ANY)
FAR = pl.BlockSpec(memory_space=pltpu.HBM)
SCALAR = pl.BlockSpec(memory_space=pltpu.SMEM)


def coded(blocks):
    return jax.ShapeDtypeStruct((blocks * OWN + SCALE_ROWS, COLS), jnp.int16)


def partial(blocks):
    return jax.ShapeDtypeStruct((blocks * OWN, COLS), jnp.float32)


def cost(blocks, dots, arrivals):
    values = blocks * OWN * COLS
    return pl.CostEstimate(
        flops=2 * TOK * values * dots,
        bytes_accessed=values * (4 + 2 * arrivals),
        transcendentals=values,
    )


def kernel_call(body, name, ins, outs, scratch, estimate, out_spec=WHOLE):
    return pl.pallas_call(
        body,
        out_shape=outs,
        in_specs=ins,
        out_specs=[out_spec] * len(outs),
        scratch_shapes=scratch,
        compiler_params=pltpu.CompilerParams(vmem_limit_bytes=KERNEL_VMEM),
        cost_estimate=estimate,
        name=name,
    )


def first(pair, me, x, g, after):
    return kernel_call(
        functools.partial(first_kernel, pair),
        f"first_{pair}",
        [SCALAR, WHOLE, WHOLE if pair else LEFT, LEFT],
        [coded(4)] * 2,
        [pltpu.VMEM((4 * OWN, 2 * COLS), jnp.float32)],
        cost(8, 1, 1),
    )(me, x, g, after)


def mid(step, me, x, g, after, received):
    return kernel_call(
        functools.partial(mid_kernel, step, 1 if received else 0),
        f"mid_{step}",
        [SCALAR, WHOLE, WHOLE, LEFT] + [WHOLE] * len(received),
        [partial(4) if step == 3 else coded(4)] * VARIANTS,
        [pltpu.VMEM((4 * OWN, COLS), jnp.float32)],
        cost(4 * VARIANTS, 1, 1),
    )(me, x, g, after, *received)


def late(count, v, p, received):
    [code] = kernel_call(
        functools.partial(late_kernel, count, len(received)),
        f"late_{count}_{v}",
        [WHOLE] * (1 + len(received)),
        [coded(count)],
        [pltpu.VMEM((count * OWN, COLS), jnp.float32)],
        cost(count, 0, len(received)),
    )(p, *received)
    return code


def finish(flag, held):
    outs = [
        jax.ShapeDtypeStruct((OWN, KV), jnp.float32),
        jax.ShapeDtypeStruct((DEVICES, 1, 128), jnp.float32),
    ]
    return kernel_call(
        finish_kernel,
        "finish",
        [SCALAR] + [WHOLE] * len(held),
        outs,
        [pltpu.VMEM(o.shape, o.dtype) for o in outs] + [pltpu.SemaphoreType.DMA((VARIANTS + 1,))],
        cost(VARIANTS, 0, 3),
        out_spec=FAR,
    )(flag, *held)


UPDATE_ROWS = 128


def update_kernel(bound, pipe_ref, reports, w_ref, m1_ref, m2_ref, g_ref, *refs):
    new_w, new_m1, new_m2, clip_ref, own_ref = refs

    @pl.when(pl.program_id(0) == 0)
    def _():
        lane = lax.broadcasted_iota(jnp.int32, (1, 128), 1)
        total = jnp.zeros((1, 128), jnp.float32)
        own = jnp.zeros((1, 128), jnp.float32)
        for section in range(PIPE):
            report = functools.reduce(
                jnp.add, [reports[rank * PIPE + section] for rank in range(RANKS)]
            )
            marks = pltpu.roll(report, 64, axis=1)
            total = total + jnp.where((lane < 64) & (marks == 0.0), report, 0.0)
            own = jnp.where(pipe_ref[0] == section, marks, own)
        total = jnp.sum(total, keepdims=True)
        clip = jnp.minimum(1.0, bound / (jnp.sqrt(total) + 1e-06))
        clip_ref[...] = jnp.broadcast_to(clip, (8, 128))
        own_ref[...] = jnp.broadcast_to(own[:1, :1], (8, 128))

    clip = clip_ref[:1, :1]
    keep = own_ref[:1, :1] == 0.0
    w, first_old, second_old = w_ref[0], m1_ref[0], m2_ref[0]
    scaled = clip * g_ref[...]
    first = 0.9 * first_old + 0.1 * scaled
    second = 0.95 * second_old + 0.05 * scaled * scaled
    updated = w - 0.02 * (first / (jnp.sqrt(second) + 1e-08) + 0.1 * w)
    new_w[0] = jnp.where(keep, updated, w)
    new_m1[0] = jnp.where(keep, first, first_old)
    new_m2[0] = jnp.where(keep, second, second_old)


def update(pipe, reports, w, m1, m2, grad, bound):
    block = pl.BlockSpec((1, UPDATE_ROWS, KV), lambda i: (0, i, 0))
    shape = jax.ShapeDtypeStruct((1, OWN, KV), jnp.float32)
    return pl.pallas_call(
        functools.partial(update_kernel, bound),
        grid=(OWN // UPDATE_ROWS,),
        out_shape=[shape] * 3,
        in_specs=[SCALAR, WHOLE, block, block, block]
        + [pl.BlockSpec((UPDATE_ROWS, KV), lambda i: (i, 0))],
        out_specs=[block] * 3,
        scratch_shapes=[pltpu.VMEM((8, 128), jnp.float32)] * 2,
        compiler_params=pltpu.CompilerParams(vmem_limit_bytes=UPDATE_VMEM),
        name="update",
    )(pipe, reports, w, m1, m2, grad)


def swap(value, axis, count, mask):
    return lax.ppermute(value, axis, [(i, i ^ mask) for i in range(count)])


def per_device(layer_input, value_grad, master_weight, moment_one, moment_two, overflow_flags):
    me = lax.axis_index("dp").astype(jnp.int32).reshape(1)
    every = range(VARIANTS)

    def cross(codes, bit):
        return [swap(codes[v], "dp", RANKS, ORDERS[v][bit]) for v in every]

    x, g = layer_input, value_grad
    far = lax.bitwise_xor(lax.axis_index("dp") // 4, 2) * (4 * OWN)
    some = jnp.concatenate(
        [
            lax.dynamic_slice(layer_input[0], (0, far), (TOK, 4 * OWN)),
            value_grad[0, :, PAIRS[0][0] * COLS : (PAIRS[0][1] + 1) * COLS],
        ],
        axis=1,
    )
    codes = first(0, me, some, me, me)
    codes = first(1, me, x, g, codes[-1]) + codes
    zero = cross(codes, 0)
    codes = mid(1, me, x, g, codes[-1], [])
    one = cross(codes, 0)
    codes = mid(2, me, x, g, codes[-1], zero)
    two = cross(codes, 1)
    kept = mid(3, me, x, g, codes[-1], one)
    three = cross([late(2, v, kept[v], [two[v]]) for v in every], 2)
    four = cross([late(1, v, kept[v], [two[v], three[v]]) for v in every], 3)
    held = [a for v in every for a in (kept[v], two[v], three[v], four[v])]
    grad, report = finish(overflow_flags, held)
    reports = lax.all_to_all(report, ("dp", "pipe"), 0, 0)
    bound = 0.5 * math.sqrt(D * KV * PIPE)
    pipe = lax.axis_index("pipe").astype(jnp.int32).reshape(1)
    return tuple(update(pipe, reports, master_weight, moment_one, moment_two, grad, bound))


def solution(mesh):
    placed = P("pipe", "dp", None)
    return jax.shard_map(
        per_device,
        mesh=mesh,
        in_specs=(placed,) * 5 + (P("pipe", "dp"),),
        out_specs=(placed,) * 3,
        check_vma=False,
    )
```

time: 319 us -> 141 us (0.44)
  waiting for transfers between devices: 197 us -> 52.2 us
  blocking collectives: 65.2 us -> 0 us
  Pallas kernels: 0 us -> 44.8 us
  starting transfers between devices: 0.04 us -> 37.6 us
  matrix products: 18.7 us -> 0 us
  between operations: 16.7 us -> 1.52 us
  other arithmetic: 10.4 us -> 0.19 us
  loops' own time: 4.08 us -> 0 us
    reduce_scatter x1 -> x0, waiting for transfers between devices: 197 us -> none  [per_device(): lax.psum_scatter(lax.dot_general(inputs_local, grads_local, (((0,), (0,))...]
    psum x2 -> x0, blocking collectives: 45.3 us -> none  [the longest x1 32.5 us: per_device(): section_squares, section_flags = lax.psum((own_squares, own_flag), 'dp')]
    pallas_call x0 -> x15, Pallas kernels: none -> 44.8 us  [the longest x3 24.7 us: mid(): kernel_call(functools.partial(mid_kernel, step, 1 if received else 0), f'...]
    ppermute x0 -> x20, waiting for transfers between devices: none -> 42.9 us  [swap(): return lax.ppermute(value, axis, [(i, i ^ mask) for i in range(count)])]
    ppermute x0 -> x20, starting transfers between devices: none -> 24.8 us  [swap(): return lax.ppermute(value, axis, [(i, i ^ mask) for i in range(count)])]
    unnamed x1 -> x0, blocking collectives: 19.9 us -> none
    dot_general x1 -> x0, matrix products: 18.7 us -> none  [per_device(): lax.dot_general(inputs_local, grads_local, (((0,), (0,)), ((), ())), pref...]
    all_to_all x0 -> x1, starting transfers between devices: none -> 12.9 us  [per_device(): reports = lax.all_to_all(report, ('dp', 'pipe'), 0, 0)]
  transfers between devices with their start and end apart: 1 -> 21, of which waited for: 1 -> 13; matrix products, arithmetic and copies ran while one was open for 0% -> 0% of each run, Pallas kernels for 0% -> 22%
where the time goes in v1:
time: 141 us
  waiting for transfers between devices  52.2 us (37%)
  Pallas kernels  44.8 us (32%)
  starting transfers between devices  37.6 us (27%)
  local copies, waits for them, and re-layouts  4.86 us (3%)
  between operations  1.52 us (1%)
    ppermute x20, waiting for transfers between devices, swap(): return lax.ppermute(value, axis, [(i, i ^ mask) for i in range(count)])  42.9 us
    ppermute x20, starting transfers between devices, swap(): return lax.ppermute(value, axis, [(i, i ^ mask) for i in range(count)])  24.8 us
    pallas_call x3, Pallas kernels, mid(): kernel_call(functools.partial(mid_kernel, step, 1 if received else 0), f'...  24.7 us
    all_to_all x1, starting transfers between devices, per_device(): reports = lax.all_to_all(report, ('dp', 'pipe'), 0, 0)  12.9 us
    all_to_all x1, waiting for transfers between devices, per_device(): reports = lax.all_to_all(report, ('dp', 'pipe'), 0, 0)  9.28 us
    pallas_call x1, Pallas kernels, update(): pl.pallas_call(functools.partial(update_kernel, bound), grid=(OWN // UPDA...  7.93 us
    pallas_call x2, Pallas kernels, first(): kernel_call(functools.partial(first_kernel, pair), f'first_{pair}', [SCAL...  5.12 us
    pallas_call x8, Pallas kernels, late(): kernel_call(functools.partial(late_kernel, count, len(received)), f'late_...  4.46 us
  transfers between devices with their start and end apart: 21, of which 13 were waited for; matrix products, arithmetic and copies ran while one was open for 0% of the time, Pallas kernels for 22%

profile of v1, /device:TPU:1, one launch (start us, length us, event | category | flops | bytes accessed | tf_op | source)
XLA Modules:
  0.0 141.2 jit_solution(12440419663862700524)
XLA Ops:
  1.7 1.8 %dynamic-slice_bitcast_fusion = bf16[512,2048]{1,0:T(8,128)(2,1)S(1)} fusion(bf16[1,512,8192]{2,1,0:T(8,128)(2,1)} %x_ref.7, s32[]{:T(128)S(6)} %select_n.9), kind=kLoop, calls=%fused_computation.1 | loop fusion | bytes 4194308 | tf_op jit(solution)/shard_map/dynamic_slice | solution.py:346
  3.8 2.6 %first_0.1 = (s16[2064,256]{1,0:T(8,128)(2,1)S(1)}, s16[2064,256]{1,0:T(8,128)(2,1)S(1)}) custom-call(s32[1]{0:T(128)} %bitcast.1.me_ref.g_ref.after_ref, bf16[512,2560]{1,0:T(8,128)(2,1)S(1)} %pad_maximum_fusion.x_ref, s32[1]{0:T(128)} %bitcast.1.me_ref.g_ref.after_ref, s32[1]{0:T(128)} %bitcast.1.me_ref.g_ref.after_ref), custom_call_target="tpu_custom_call" | custom-call | flops 1073741824 | bytes 6291456 | tf_op jit(solution)/shard_map/first_0/pallas_call | solution.py:231
  6.4 2.1 %collective-permute-start.2 = (s16[2064,256]{1,0:T(8,128)(2,1)S(1)}, s16[2064,256]{1,0:T(8,128)(2,1)S(1)}, u32[]{:S(2)}, u32[]{:S(2)}) collective-permute-start(s16[2064,256]{1,0:T(8,128)(2,1)S(1)} %get-tuple-element.25), channel_id=1, source_target_pairs={{0,32},{8,40},{16,48},{24,56},{32,0},{40,8},{48,16},{56,24},{64,96... | collective-permute-start | bytes 3170312 | tf_op jit(solution)/shard_map/ppermute | solution.py:332
  8.5 1.8 %collective-permute-start.3 = (s16[2064,256]{1,0:T(8,128)(2,1)S(1)}, s16[2064,256]{1,0:T(8,128)(2,1)S(1)}, u32[]{:S(2)}, u32[]{:S(2)}) collective-permute-start(s16[2064,256]{1,0:T(8,128)(2,1)S(1)} %get-tuple-element.21.refs_0_.after_ref), channel_id=1, source_target_pairs={{0,96},{8,104},{16,112},{24,120},{32,64},{40,72},{48,80},{56,88},{... | collective-permute-start | bytes 3170312 | tf_op jit(solution)/shard_map/ppermute | solution.py:332
  10.3 2.6 %first_1.1 = (s16[2064,256]{1,0:T(8,128)(2,1)S(1)}, s16[2064,256]{1,0:T(8,128)(2,1)S(1)}) custom-call(s32[1]{0:T(128)} %bitcast.1.me_ref.g_ref.after_ref, bf16[1,512,8192]{2,1,0:T(8,128)(2,1)S(1)} %copy-done, bf16[1,512,1024]{2,1,0:T(8,128)(2,1)S(1)} %copy-done.1, s16[2064,256]{1,0:T(8,128)(2,1)S(1)} %get-tuple-element.21.refs_0_.after_ref), custom_call_target="tpu_custom_call" | custom-call | flops 1073741824 | bytes 6291456 | tf_op jit(solution)/shard_map/first_1/pallas_call | solution.py:231
  12.9 1.4 collective-permute-start
  14.2 1.9 %collective-permute-start.1 = (s16[2064,256]{1,0:T(8,128)(2,1)S(1)}, s16[2064,256]{1,0:T(8,128)(2,1)S(1)}, u32[]{:S(2)}, u32[]{:S(2)}) collective-permute-start(s16[2064,256]{1,0:T(8,128)(2,1)S(1)} %get-tuple-element.24), channel_id=1, source_target_pairs={{0,24},{8,16},{16,8},{24,0},{32,56},{40,48},{48,40},{56,32},{64,88... | collective-permute-start | bytes 3170312 | tf_op jit(solution)/shard_map/ppermute | solution.py:332
  16.1 7.6 %mid_1.1 = (s16[2064,256]{1,0:T(8,128)(2,1)S(1)}, s16[2064,256]{1,0:T(8,128)(2,1)S(1)}, s16[2064,256]{1,0:T(8,128)(2,1)S(1)}, s16[2064,256]{1,0:T(8,128)(2,1)S(1)}) custom-call(s32[1]{0:T(128)} %bitcast.1.me_ref.g_ref.after_ref, bf16[1,512,8192]{2,1,0:T(8,128)(2,1)S(1)} %copy-done, bf16[1,512,1024]{2,1,0:T(8,128)(2,1)S(1)} %copy-done.1, ...), custom_call_target="tpu_custom_call" | custom-call | flops 2147483648 | bytes 12582912 | tf_op jit(solution)/shard_map/mid_1/pallas_call | solution.py:242
  24.2 6.8 %collective-permute-done.2.refs_3_ = s16[2064,256]{1,0:T(8,128)(2,1)S(1)} collective-permute-done((s16[2064,256]{1,0:T(8,128)(2,1)S(1)}, s16[2064,256]{1,0:T(8,128)(2,1)S(1)}, u32[]{:S(2)}, u32[]{:S(2)}) %collective-permute-start.2) | collective-permute-done | bytes 1056800 | tf_op jit(solution)/shard_map/ppermute | solution.py:332
  31.0 3.2 %collective-permute-start.5 = (s16[2064,256]{1,0:T(8,128)(2,1)S(1)}, s16[2064,256]{1,0:T(8,128)(2,1)S(1)}, u32[]{:S(2)}, u32[]{:S(2)}) collective-permute-start(s16[2064,256]{1,0:T(8,128)(2,1)S(1)} %get-tuple-element.28), channel_id=1, source_target_pairs={{0,24},{8,16},{16,8},{24,0},{32,56},{40,48},{48,40},{56,32},{64,88... | collective-permute-start | bytes 3170312 | tf_op jit(solution)/shard_map/ppermute | solution.py:332
  34.2 1.2 collective-permute-start.6
  35.4 1.1 collective-permute-done.refs_1_
  37.4 1.4 collective-permute-done.1.refs_2_
  38.8 10.1 %mid_2.1 = (s16[2064,256]{1,0:T(8,128)(2,1)S(1)}, s16[2064,256]{1,0:T(8,128)(2,1)S(1)}, s16[2064,256]{1,0:T(8,128)(2,1)S(1)}, s16[2064,256]{1,0:T(8,128)(2,1)S(1)}) custom-call(s32[1]{0:T(128)} %bitcast.1.me_ref.g_ref.after_ref, bf16[1,512,8192]{2,1,0:T(8,128)(2,1)S(1)} %copy-done, bf16[1,512,1024]{2,1,0:T(8,128)(2,1)S(1)} %copy-done.1, ...), custom_call_target="tpu_custom_call" | custom-call | flops 2147483648 | bytes 12582912 | tf_op jit(solution)/shard_map/mid_2/pallas_call | solution.py:242
  49.3 9.9 %collective-permute-done.4.refs_1_ = s16[2064,256]{1,0:T(8,128)(2,1)S(1)} collective-permute-done((s16[2064,256]{1,0:T(8,128)(2,1)S(1)}, s16[2064,256]{1,0:T(8,128)(2,1)S(1)}, u32[]{:S(2)}, u32[]{:S(2)}) %collective-permute-start.4) | collective-permute-done | bytes 1056800 | tf_op jit(solution)/shard_map/ppermute | solution.py:332
  60.0 1.4 collective-permute-done.5.refs_2_
  61.4 1.9 %collective-permute-start.8 = (s16[2064,256]{1,0:T(8,128)(2,1)S(1)}, s16[2064,256]{1,0:T(8,128)(2,1)S(1)}, u32[]{:S(2)}, u32[]{:S(2)}) collective-permute-start(s16[2064,256]{1,0:T(8,128)(2,1)S(1)} %get-tuple-element.31), channel_id=1, source_target_pairs={{0,24},{8,16},{16,8},{24,0},{32,56},{40,48},{48,40},{56,32},{64,88... | collective-permute-start | bytes 3170312 | tf_op jit(solution)/shard_map/ppermute | solution.py:332
  63.3 6.9 %mid_3.1 = (f32[2048,256]{1,0:T(8,128)S(1)}, f32[2048,256]{1,0:T(8,128)S(1)}, f32[2048,256]{1,0:T(8,128)S(1)}, f32[2048,256]{1,0:T(8,128)S(1)}) custom-call(s32[1]{0:T(128)} %bitcast.1.me_ref.g_ref.after_ref, bf16[1,512,8192]{2,1,0:T(8,128)(2,1)S(1)} %copy-done, bf16[1,512,1024]{2,1,0:T(8,128)(2,1)S(1)} %copy-done.1, ...), custom_call_target="tpu_custom_call" | custom-call | flops 2147483648 | bytes 12582912 | tf_op jit(solution)/shard_map/mid_3/pallas_call | solution.py:242
  70.3 9.6 %collective-permute-done.17.refs_0_.refs_14_ = s16[2064,256]{1,0:T(8,128)(2,1)S(1)} collective-permute-done((s16[2064,256]{1,0:T(8,128)(2,1)S(1)}, s16[2064,256]{1,0:T(8,128)(2,1)S(1)}, u32[]{:S(2)}, u32[]{:S(2)}) %collective-permute-start.17) | collective-permute-done | bytes 1056800 | tf_op jit(solution)/shard_map/ppermute | solution.py:332
  81.2 1.8 %collective-permute-done.14.refs_0_.refs_10_ = s16[2064,256]{1,0:T(8,128)(2,1)S(1)} collective-permute-done((s16[2064,256]{1,0:T(8,128)(2,1)S(1)}, s16[2064,256]{1,0:T(8,128)(2,1)S(1)}, u32[]{:S(2)}, u32[]{:S(2)}) %collective-permute-start.14) | collective-permute-done | bytes 1056800 | tf_op jit(solution)/shard_map/ppermute | solution.py:332
  83.7 2.8 %collective-permute-start.15 = (s16[1040,256]{1,0:T(8,128)(2,1)S(1)}, s16[1040,256]{1,0:T(8,128)(2,1)S(1)}, u32[]{:S(2)}, u32[]{:S(2)}) collective-permute-start(s16[1040,256]{1,0:T(8,128)(2,1)S(1)} %late_2_2.1), channel_id=1, source_target_pairs={{0,24},{8,16},{16,8},{24,0},{32,56},{40,48},{48,40},{56,32},{64,88... | collective-permute-start | bytes 1597448 | tf_op jit(solution)/shard_map/ppermute | solution.py:332
  88.0 1.2 collective-permute-start.9
  89.2 6.0 %collective-permute-done.18.refs_1_.refs_15_ = s16[1040,256]{1,0:T(8,128)(2,1)S(1)} collective-permute-done((s16[1040,256]{1,0:T(8,128)(2,1)S(1)}, s16[1040,256]{1,0:T(8,128)(2,1)S(1)}, u32[]{:S(2)}, u32[]{:S(2)}) %collective-permute-start.18) | collective-permute-done | bytes 532512 | tf_op jit(solution)/shard_map/ppermute | solution.py:332
  95.6 2.0 %collective-permute-start.19 = (s16[528,256]{1,0:T(8,128)(2,1)S(1)}, s16[528,256]{1,0:T(8,128)(2,1)S(1)}, u32[]{:S(2)}, u32[]{:S(2)}) collective-permute-start(s16[528,256]{1,0:T(8,128)(2,1)S(1)} %late_1_3.1), channel_id=1, source_target_pairs={{0,24},{8,16},{16,8},{24,0},{32,56},{40,48},{48,40},{56,32},{64,88... | collective-permute-start | bytes 811016 | tf_op jit(solution)/shard_map/ppermute | solution.py:332
  98.7 1.6 %collective-permute-start.13 = (s16[528,256]{1,0:T(8,128)(2,1)S(1)}, s16[528,256]{1,0:T(8,128)(2,1)S(1)}, u32[]{:S(2)}, u32[]{:S(2)}) collective-permute-start(s16[528,256]{1,0:T(8,128)(2,1)S(1)} %late_1_1.1), channel_id=1, source_target_pairs={{0,96},{8,104},{16,112},{24,120},{32,64},{40,72},{48,80},{56,88},{... | collective-permute-start | bytes 811016 | tf_op jit(solution)/shard_map/ppermute | solution.py:332
  102.5 1.3 collective-permute-done.16.refs_12_
  103.8 2.6 %collective-permute-done.13.refs_8_ = s16[528,256]{1,0:T(8,128)(2,1)S(1)} collective-permute-done((s16[528,256]{1,0:T(8,128)(2,1)S(1)}, s16[528,256]{1,0:T(8,128)(2,1)S(1)}, u32[]{:S(2)}, u32[]{:S(2)}) %collective-permute-start.13) | collective-permute-done | bytes 270368 | tf_op jit(solution)/shard_map/ppermute | solution.py:332
  106.5 2.6 %finish.1 = (f32[512,1024]{1,0:T(8,128)S(1)}, f32[128,1,128]{2,1,0:T(1,128)}) custom-call(s32[1,1]{1,0:T(1,128)S(6)} %copy.9.refs_0_, f32[2048,256]{1,0:T(8,128)S(1)} %get-tuple-element.30.p_ref.refs_1_, s16[2064,256]{1,0:T(8,128)(2,1)S(1)} %collective-permute-done.8.refs_0_.refs_2_, s16[1040,256]{1,0:T(8,128)(2,1)S(1)} %collective-permute-done.9.refs_1_.refs_3_, ...), custom_call_target="tpu_custom_call" | custom-call | bytes 5242880 | tf_op jit(solution)/shard_map/finish/pallas_call | solution.py:269
  109.1 1.3 copy-done.2
  110.5 12.9 %all-to-all-start = ((f32[128,1,128]{2,1,0:T(1,128)}), f32[128,1,128]{2,1,0:T(1,128)S(1)}, u32[]{:S(2)}, u32[]{:S(2)}) async-start(f32[128,1,128]{2,1,0:T(1,128)} %get-tuple-element.37), calls=%async_computation | async-start | bytes 131072 | tf_op jit(solution)/shard_map/all_to_all | solution.py:363
  123.3 9.3 %all-to-all-done.reports = f32[128,1,128]{2,1,0:T(1,128)S(1)} async-done(((f32[128,1,128]{2,1,0:T(1,128)}), f32[128,1,128]{2,1,0:T(1,128)S(1)}, u32[]{:S(2)}, u32[]{:S(2)}) %all-to-all-start) | async-done | bytes 65568 | tf_op jit(solution)/shard_map/all_to_all | solution.py:363
  133.2 7.9 %update.1 = (f32[1,512,1024]{2,1,0:T(8,128)}, f32[1,512,1024]{2,1,0:T(8,128)}, f32[1,512,1024]{2,1,0:T(8,128)}) custom-call(s32[1]{0:T(128)} %bitcast.pipe_ref, f32[128,1,128]{2,1,0:T(1,128)} %copy-done.3, f32[1,512,1024]{2,1,0:T(8,128)} %w_ref.1, f32[1,512,1024]{2,1,0:T(8,128)} %m1_ref.1, f32[1,512,1024]{2,1,0:T(8,128)} %m2_ref.1, f32[512,1024]{1,0:T(8,128)} %copy-done.2), custom_call_target="tpu_custom_call" | custom-call | tf_op jit(solution)/shard_map/update/pallas_call | solution.py:318
  (36 shorter events, 11.1 us)
Async XLA Ops:
  1.7 8.6 %copy-start.1 = (bf16[1,512,1024]{2,1,0:T(8,128)(2,1)S(1)}, bf16[1,512,1024]{2,1,0:T(8,128)(2,1)}, u32[]{:S(2)}) copy-start(bf16[1,512,1024]{2,1,0:T(8,128)(2,1)} %g_ref.7) | copy-start | bytes 3145732
  3.6 6.7 %copy-start = (bf16[1,512,8192]{2,1,0:T(8,128)(2,1)S(1)}, bf16[1,512,8192]{2,1,0:T(8,128)(2,1)}, u32[]{:S(2)}) copy-start(bf16[1,512,8192]{2,1,0:T(8,128)(2,1)} %x_ref.7) | copy-start | bytes 25165828
  6.4 24.7 %collective-permute-start.2 = (s16[2064,256]{1,0:T(8,128)(2,1)S(1)}, s16[2064,256]{1,0:T(8,128)(2,1)S(1)}, u32[]{:S(2)}, u32[]{:S(2)}) collective-permute-start(s16[2064,256]{1,0:T(8,128)(2,1)S(1)} %get-tuple-element.25), channel_id=1, source_target_pairs={{0,32},{8,40},{16,48},{24,56},{32,0},{40,8},{48,16},{56,24},{64,96... | collective-permute-start | bytes 3170312 | tf_op jit(solution)/shard_map/ppermute | solution.py:332
  8.5 25.7 %collective-permute-start.3 = (s16[2064,256]{1,0:T(8,128)(2,1)S(1)}, s16[2064,256]{1,0:T(8,128)(2,1)S(1)}, u32[]{:S(2)}, u32[]{:S(2)}) collective-permute-start(s16[2064,256]{1,0:T(8,128)(2,1)S(1)} %get-tuple-element.21.refs_0_.after_ref), channel_id=1, source_target_pairs={{0,96},{8,104},{16,112},{24,120},{32,64},{40,72},{48,80},{56,88},{... | collective-permute-start | bytes 3170312 | tf_op jit(solution)/shard_map/ppermute | solution.py:332
  12.9 23.7 %collective-permute-start = (s16[2064,256]{1,0:T(8,128)(2,1)S(1)}, s16[2064,256]{1,0:T(8,128)(2,1)S(1)}, u32[]{:S(2)}, u32[]{:S(2)}) collective-permute-start(s16[2064,256]{1,0:T(8,128)(2,1)S(1)} %get-tuple-element.23), channel_id=1, source_target_pairs={{0,8},{8,0},{16,24},{24,16},{32,40},{40,32},{48,56},{56,48},{64,72... | collective-permute-start | bytes 3170312 | tf_op jit(solution)/shard_map/ppermute | solution.py:332
  14.2 24.5 %collective-permute-start.1 = (s16[2064,256]{1,0:T(8,128)(2,1)S(1)}, s16[2064,256]{1,0:T(8,128)(2,1)S(1)}, u32[]{:S(2)}, u32[]{:S(2)}) collective-permute-start(s16[2064,256]{1,0:T(8,128)(2,1)S(1)} %get-tuple-element.24), channel_id=1, source_target_pairs={{0,24},{8,16},{16,8},{24,0},{32,56},{40,48},{48,40},{56,32},{64,88... | collective-permute-start | bytes 3170312 | tf_op jit(solution)/shard_map/ppermute | solution.py:332
  23.7 35.5 %collective-permute-start.4 = (s16[2064,256]{1,0:T(8,128)(2,1)S(1)}, s16[2064,256]{1,0:T(8,128)(2,1)S(1)}, u32[]{:S(2)}, u32[]{:S(2)}) collective-permute-start(s16[2064,256]{1,0:T(8,128)(2,1)S(1)} %get-tuple-element.27), channel_id=1, source_target_pairs={{0,8},{8,0},{16,24},{24,16},{32,40},{40,32},{48,56},{56,48},{64,72... | collective-permute-start | bytes 3170312 | tf_op jit(solution)/shard_map/ppermute | solution.py:332
  31.0 30.4 %collective-permute-start.5 = (s16[2064,256]{1,0:T(8,128)(2,1)S(1)}, s16[2064,256]{1,0:T(8,128)(2,1)S(1)}, u32[]{:S(2)}, u32[]{:S(2)}) collective-permute-start(s16[2064,256]{1,0:T(8,128)(2,1)S(1)} %get-tuple-element.28), channel_id=1, source_target_pairs={{0,24},{8,16},{16,8},{24,0},{32,56},{40,48},{48,40},{56,32},{64,88... | collective-permute-start | bytes 3170312 | tf_op jit(solution)/shard_map/ppermute | solution.py:332
  34.2 27.2 %collective-permute-start.6 = (s16[2064,256]{1,0:T(8,128)(2,1)S(1)}, s16[2064,256]{1,0:T(8,128)(2,1)S(1)}, u32[]{:S(2)}, u32[]{:S(2)}) collective-permute-start(s16[2064,256]{1,0:T(8,128)(2,1)S(1)} %get-tuple-element.29), channel_id=1, source_target_pairs={{0,32},{8,40},{16,48},{24,56},{32,0},{40,8},{48,16},{56,24},{64,96... | collective-permute-start | bytes 3170312 | tf_op jit(solution)/shard_map/ppermute | solution.py:332
  36.5 26.8 %collective-permute-start.7 = (s16[2064,256]{1,0:T(8,128)(2,1)S(1)}, s16[2064,256]{1,0:T(8,128)(2,1)S(1)}, u32[]{:S(2)}, u32[]{:S(2)}) collective-permute-start(s16[2064,256]{1,0:T(8,128)(2,1)S(1)} %get-tuple-element.22.refs_0_), channel_id=1, source_target_pairs={{0,96},{8,104},{16,112},{24,120},{32,64},{40,72},{48,80},{56,88},{... | collective-permute-start | bytes 3170312 | tf_op jit(solution)/shard_map/ppermute | solution.py:332
  48.9 30.9 %collective-permute-start.17 = (s16[2064,256]{1,0:T(8,128)(2,1)S(1)}, s16[2064,256]{1,0:T(8,128)(2,1)S(1)}, u32[]{:S(2)}, u32[]{:S(2)}) collective-permute-start(s16[2064,256]{1,0:T(8,128)(2,1)S(1)} %get-tuple-element.26.refs_0_), channel_id=1, source_target_pairs={{0,32},{8,40},{16,48},{24,56},{32,0},{40,8},{48,16},{56,24},{64,96... | collective-permute-start | bytes 3170312 | tf_op jit(solution)/shard_map/ppermute | solution.py:332
  59.2 23.9 %collective-permute-start.14 = (s16[2064,256]{1,0:T(8,128)(2,1)S(1)}, s16[2064,256]{1,0:T(8,128)(2,1)S(1)}, u32[]{:S(2)}, u32[]{:S(2)}) collective-permute-start(s16[2064,256]{1,0:T(8,128)(2,1)S(1)} %get-tuple-element.35), channel_id=1, source_target_pairs={{0,96},{8,104},{16,112},{24,120},{32,64},{40,72},{48,80},{56,88},{... | collective-permute-start | bytes 3170312 | tf_op jit(solution)/shard_map/ppermute | solution.py:332
  61.4 25.2 %collective-permute-start.11 = (s16[2064,256]{1,0:T(8,128)(2,1)S(1)}, s16[2064,256]{1,0:T(8,128)(2,1)S(1)}, u32[]{:S(2)}, u32[]{:S(2)}) collective-permute-start(s16[2064,256]{1,0:T(8,128)(2,1)S(1)} %get-tuple-element.33), channel_id=1, source_target_pairs={{0,8},{8,0},{16,24},{24,16},{32,40},{40,32},{48,56},{56,48},{64,72... | collective-permute-start | bytes 3170312 | tf_op jit(solution)/shard_map/ppermute | solution.py:332
  61.4 25.9 %collective-permute-start.8 = (s16[2064,256]{1,0:T(8,128)(2,1)S(1)}, s16[2064,256]{1,0:T(8,128)(2,1)S(1)}, u32[]{:S(2)}, u32[]{:S(2)}) collective-permute-start(s16[2064,256]{1,0:T(8,128)(2,1)S(1)} %get-tuple-element.31), channel_id=1, source_target_pairs={{0,24},{8,16},{16,8},{24,0},{32,56},{40,48},{48,40},{56,32},{64,88... | collective-permute-start | bytes 3170312 | tf_op jit(solution)/shard_map/ppermute | solution.py:332
  80.5 14.7 %collective-permute-start.18 = (s16[1040,256]{1,0:T(8,128)(2,1)S(1)}, s16[1040,256]{1,0:T(8,128)(2,1)S(1)}, u32[]{:S(2)}, u32[]{:S(2)}) collective-permute-start(s16[1040,256]{1,0:T(8,128)(2,1)S(1)} %late_2_3.1), channel_id=1, source_target_pairs={{0,8},{8,0},{16,24},{24,16},{32,40},{40,32},{48,56},{56,48},{64,72... | collective-permute-start | bytes 1597448 | tf_op jit(solution)/shard_map/ppermute | solution.py:332
  83.7 13.9 %collective-permute-start.15 = (s16[1040,256]{1,0:T(8,128)(2,1)S(1)}, s16[1040,256]{1,0:T(8,128)(2,1)S(1)}, u32[]{:S(2)}, u32[]{:S(2)}) collective-permute-start(s16[1040,256]{1,0:T(8,128)(2,1)S(1)} %late_2_2.1), channel_id=1, source_target_pairs={{0,24},{8,16},{16,8},{24,0},{32,56},{40,48},{48,40},{56,32},{64,88... | collective-permute-start | bytes 1597448 | tf_op jit(solution)/shard_map/ppermute | solution.py:332
  87.2 11.0 %collective-permute-start.12 = (s16[1040,256]{1,0:T(8,128)(2,1)S(1)}, s16[1040,256]{1,0:T(8,128)(2,1)S(1)}, u32[]{:S(2)}, u32[]{:S(2)}) collective-permute-start(s16[1040,256]{1,0:T(8,128)(2,1)S(1)} %late_2_1.1), channel_id=1, source_target_pairs={{0,32},{8,40},{16,48},{24,56},{32,0},{40,8},{48,16},{56,24},{64,96... | collective-permute-start | bytes 1597448 | tf_op jit(solution)/shard_map/ppermute | solution.py:332
  88.0 12.3 %collective-permute-start.9 = (s16[1040,256]{1,0:T(8,128)(2,1)S(1)}, s16[1040,256]{1,0:T(8,128)(2,1)S(1)}, u32[]{:S(2)}, u32[]{:S(2)}) collective-permute-start(s16[1040,256]{1,0:T(8,128)(2,1)S(1)} %late_2_0.1), channel_id=1, source_target_pairs={{0,96},{8,104},{16,112},{24,120},{32,64},{40,72},{48,80},{56,88},{... | collective-permute-start | bytes 1597448 | tf_op jit(solution)/shard_map/ppermute | solution.py:332
  95.6 6.9 %collective-permute-start.19 = (s16[528,256]{1,0:T(8,128)(2,1)S(1)}, s16[528,256]{1,0:T(8,128)(2,1)S(1)}, u32[]{:S(2)}, u32[]{:S(2)}) collective-permute-start(s16[528,256]{1,0:T(8,128)(2,1)S(1)} %late_1_3.1), channel_id=1, source_target_pairs={{0,24},{8,16},{16,8},{24,0},{32,56},{40,48},{48,40},{56,32},{64,88... | collective-permute-start | bytes 811016 | tf_op jit(solution)/shard_map/ppermute | solution.py:332
  98.1 5.7 %collective-permute-start.16 = (s16[528,256]{1,0:T(8,128)(2,1)S(1)}, s16[528,256]{1,0:T(8,128)(2,1)S(1)}, u32[]{:S(2)}, u32[]{:S(2)}) collective-permute-start(s16[528,256]{1,0:T(8,128)(2,1)S(1)} %late_1_2.1), channel_id=1, source_target_pairs={{0,8},{8,0},{16,24},{24,16},{32,40},{40,32},{48,56},{56,48},{64,72... | collective-permute-start | bytes 811016 | tf_op jit(solution)/shard_map/ppermute | solution.py:332
  98.7 7.7 %collective-permute-start.13 = (s16[528,256]{1,0:T(8,128)(2,1)S(1)}, s16[528,256]{1,0:T(8,128)(2,1)S(1)}, u32[]{:S(2)}, u32[]{:S(2)}) collective-permute-start(s16[528,256]{1,0:T(8,128)(2,1)S(1)} %late_1_1.1), channel_id=1, source_target_pairs={{0,96},{8,104},{16,112},{24,120},{32,64},{40,72},{48,80},{56,88},{... | collective-permute-start | bytes 811016 | tf_op jit(solution)/shard_map/ppermute | solution.py:332
  100.8 5.7 %collective-permute-start.10 = (s16[528,256]{1,0:T(8,128)(2,1)S(1)}, s16[528,256]{1,0:T(8,128)(2,1)S(1)}, u32[]{:S(2)}, u32[]{:S(2)}) collective-permute-start(s16[528,256]{1,0:T(8,128)(2,1)S(1)} %late_1_0.1), channel_id=1, source_target_pairs={{0,32},{8,40},{16,48},{24,56},{32,0},{40,8},{48,16},{56,24},{64,96... | collective-permute-start | bytes 811016 | tf_op jit(solution)/shard_map/ppermute | solution.py:332
  109.1 1.3 copy-start.2
  110.5 22.2 %all-to-all-start = ((f32[128,1,128]{2,1,0:T(1,128)}), f32[128,1,128]{2,1,0:T(1,128)S(1)}, u32[]{:S(2)}, u32[]{:S(2)}) async-start(f32[128,1,128]{2,1,0:T(1,128)} %get-tuple-element.37), calls=%async_computation | async-start | bytes 131072 | tf_op jit(solution)/shard_map/all_to_all | solution.py:363
  132.6 0.6 copy-start.3

commit v2 on v1

--- a/solution.py
+++ b/solution.py
@@ -12,21 +12,23 @@
 KV = 1024
 RANKS = 16
 DEVICES = 128
+FAR_ROWS = 12288
 PIPE = 8
 TOK = 512
 OWN = 512
 COLS = 256
 VARIANTS = 4
-STEP = 128
+STEP = 512
 KERNEL_VMEM = 14 << 20
+HEAD_VMEM = 121 << 19
 UPDATE_VMEM = 60 << 20
 TOP_POWER = 29.9985
 SCALE_ROWS = 16
 
 XA, XB, YA, YB = 4, 12, 1, 3
-ORDERS = ((YA, YB, XB, XA), (YB, YA, XA, XB), (XA, XB, YB, YA), (XB, XA, YA, YB))
-PAIRS = ((2, 3), (0, 1))
-
+ORDERS = ((XA, XB, YB, YA), (YA, YB, XB, XA), (YB, YA, XA, XB), (XB, XA, YA, YB))
+RAW, CODED = (0, 1), (2, 3)
+SHARES = ((0, 128, 0, 1024), (128, 128, 0, 1024), (256, 256, 0, 512), (256, 256, 512, 512))
 
 TRANSPOSED = (((0,), (0,)), ((), ()))
 
@@ -46,9 +48,10 @@
     return jnp.exp2(power), jnp.exp2(-power)
 
 
-def columns_of(me_ref, mask):
+def columns_of(me_ref, mask, v):
     block = jnp.bitwise_xor(me_ref[0], mask)
-    return pl.ds(pl.multiple_of(block * OWN, OWN), OWN)
+    first, rows = SHARES[v][:2]
+    return pl.ds(pl.multiple_of(block * OWN + first, 128), rows)
 
 
 def scales_of(received):
@@ -82,69 +85,91 @@
     return pieces(rows, body, jnp.zeros((1, COLS), jnp.float32))
 
 
-def encode(largest, sums, cols, blocks, out_ref):
+def encode(largest, sums, blocks, out_ref):
     step_code = jnp.ceil(jnp.log2(jnp.maximum(largest, 1e-37)) * 64.0)
     step_code = jnp.clip(step_code, -90.0 * 64.0, 128.0 * 64.0)
     factor = scale_of(step_code)[1]
-    rows = len(blocks) * OWN
+    rows = blocks * OWN
     out_ref[rows : rows + SCALE_ROWS, :] = (
         jnp.broadcast_to(step_code, (SCALE_ROWS, COLS)).astype(jnp.int32).astype(jnp.int16)
     )
-    for slot, block in enumerate(blocks):
-
-        def body(at, _):
-            scaled = sums[pl.ds(pl.multiple_of(block * OWN + at, STEP), STEP), cols] * factor
-            rooted = scaled * lax.rsqrt(jnp.maximum(jnp.abs(scaled), 1e-12))
-            whole = jnp.round(rooted).astype(jnp.int32)
-            out_ref[pl.ds(slot * OWN + at, STEP), :] = whole.astype(jnp.int16)
-            return 0
-
-        pieces(OWN, body, 0)
-
-
-def product(x_ref, me_ref, masks, g):
-    x = jnp.concatenate([x_ref[0, :, columns_of(me_ref, mask)] for mask in masks], axis=1)
-    return lax.dot_general(x, g, TRANSPOSED, preferred_element_type=jnp.float32)
-
-
-def first_kernel(pair, me_ref, x_ref, g_ref, after_ref, *refs):
-    outs, sums = refs[:2], refs[2]
-    variants = PAIRS[pair]
-    if pair == 0:
-        total = lax.dot_general(
-            x_ref[:, : 4 * OWN],
-            x_ref[:, 4 * OWN :],
-            TRANSPOSED,
-            preferred_element_type=jnp.float32,
+
+    def body(at, _):
+        scaled = sums[pl.ds(at, STEP), :] * factor
+        rooted = scaled * lax.rsqrt(jnp.maximum(jnp.abs(scaled), 1e-12))
+        out_ref[pl.ds(at, STEP), :] = jnp.round(rooted).astype(jnp.int32).astype(jnp.int16)
+        return 0
+
+    pieces(rows, body, 0)
+
+
+def multiply(v, x, g, into):
+    _, rows, _, cols = SHARES[v]
+    total = lax.dot_general(x, g, TRANSPOSED, preferred_element_type=jnp.float32)
+    largest = jnp.zeros((1, COLS), jnp.float32)
+    for group in range(cols // COLS):
+        part = total[:, group * COLS : (group + 1) * COLS]
+        largest = jnp.maximum(largest, largest_of(part))
+        for slot in range(4):
+            at = slot * OWN + group * rows
+            into[at : at + rows, :] = part[slot * rows : (slot + 1) * rows, :]
+    return largest
+
+
+def head_kernel(me_ref, x_hbm, g_hbm, *refs):
+    outs, (x_buf, g_buf, sums, sems) = refs[: len(CODED)], refs[len(CODED) :]
+    copies = []
+    for i, v in enumerate(CODED):
+        _, rows, first, cols = SHARES[v]
+        at = (slice(None), slice(first, first + cols))
+        copies.append(
+            [pltpu.make_async_copy(g_hbm.at[0, *at], g_buf.at[*at], sems.at[i, 4])]
+            + [
+                pltpu.make_async_copy(
+                    x_hbm.at[0, :, columns_of(me_ref, mask, v)],
+                    x_buf.at[i, :, slot * rows : (slot + 1) * rows],
+                    sems.at[i, slot],
+                )
+                for slot, mask in enumerate(masks_of(ORDERS[v], 0))
+            ]
         )
-        place = {XA ^ XB ^ y: jnp.bitwise_and(jnp.bitwise_xor(me_ref[0], y), 3) for y in range(4)}
-    else:
-        masks = masks_of(ORDERS[variants[0]], 0)
-        cols = slice(variants[0] * COLS, (variants[1] + 1) * COLS)
-        total = product(x_ref, me_ref, masks, g_ref[0, :, cols])
-        place = {mask: slot for slot, mask in enumerate(masks)}
-    sums[...] = total
-    largest = largest_of(total)
-    for half, v in enumerate(variants):
-        cols = slice(half * COLS, (half + 1) * COLS)
-        blocks = [place[mask] for mask in masks_of(ORDERS[v], 0)]
-        encode(largest[:, cols], sums, cols, blocks, outs[half])
-
-
-def mid_kernel(step, has, me_ref, x_ref, g_ref, *refs):
-    received = refs[1 : 1 + VARIANTS * has]
-    outs = refs[1 + VARIANTS * has :][:VARIANTS]
-    sums = refs[-1]
-    for v in range(VARIANTS):
-        masks = masks_of(ORDERS[v], step)
-        total = product(x_ref, me_ref, masks, g_ref[0, :, v * COLS : (v + 1) * COLS])
-        into = outs[v] if step == 3 else sums
-        into[...] = total
-        largest = largest_of(total)
-        if has:
-            largest = add_received(into, 0, [(received[v], 0)], 4 * OWN, into)
+        for copy in copies[-1]:
+            copy.start()
+    for i, v in enumerate(CODED):
+        _, _, first, cols = SHARES[v]
+        for copy in copies[i]:
+            copy.wait()
+        largest = multiply(v, x_buf[i], g_buf[:, first : first + cols], sums)
+        encode(largest, sums, 4, outs[i])
+
+
+def work_kernel(step, variants, unread, me_ref, x_ref, g_ref, *refs):
+    refs, arrived = list(refs)[unread:], []
+    for v in variants:
+        count = 0 if step < 2 else 2 if v in RAW else 1
+        arrived.append([refs.pop(0) for _ in range(count)])
+    outs, sums = refs[:-1], refs[-1]
+    for v, there, out in zip(variants, arrived, outs):
+        _, rows, first, cols = SHARES[v]
+        x = [x_ref[0, :, columns_of(me_ref, mask, v)] for mask in masks_of(ORDERS[v], step)]
+        x, g = jnp.concatenate(x, axis=1), g_ref[0, :, first : first + cols]
+        if v in RAW:
+            half = slice(4 * rows * (step - 2), 4 * rows * (step - 1))
+            x = jnp.concatenate([x, there[1][:, half]], axis=0)
+            g = jnp.concatenate([g, there[0][...]], axis=0)
+        into = out if step == 3 else sums
+        largest = multiply(v, x, g, into)
+        if step >= 2 and v in CODED:
+            largest = add_received(into, 0, [(there[0], 0)], 4 * OWN, into)
         if step != 3:
-            encode(largest, sums, slice(0, COLS), range(4), outs[v])
+            encode(largest, sums, 4, out)
+
+
+def gather_kernel(me_ref, x_ref, after_ref, *outs):
+    for v, out in zip(RAW, outs):
+        masks = masks_of(ORDERS[v], 0) + masks_of(ORDERS[v], 1)
+        for slot, mask in enumerate(masks):
+            out[:, slot * 128 : (slot + 1) * 128] = x_ref[0, :, columns_of(me_ref, mask, v)]
 
 
 def late_kernel(count, arrivals, p_ref, *refs):
@@ -153,7 +178,7 @@
     largest = add_received(
         p_ref, first, [(r, first) for r in received], count * OWN, sums
     )
-    encode(largest, sums, slice(0, COLS), range(count), out)
+    encode(largest, sums, count, out)
 
 
 def finish_kernel(*refs):
@@ -164,21 +189,19 @@
     for v in range(VARIANTS):
         p_ref, *received = refs[1 + 4 * v : 5 + 4 * v]
         scales = scales_of(received)
-
-        def body(at, acc):
-            total = p_ref[pl.ds(at, STEP), :]
+        first, rows, left, cols = SHARES[v]
+        for group in range(cols // COLS):
+            at = slice(group * rows, (group + 1) * rows)
+            total = p_ref[at, :]
             for r, scale in zip(received, scales):
-                total = total + decode(r[pl.ds(at, STEP), :], scale)
-            grad_ref[pl.ds(at, STEP), v * COLS : (v + 1) * COLS] = total
+                total = total + decode(r[at, :], scale)
+            begin = left + group * COLS
+            grad_ref[first : first + rows, begin : begin + COLS] = total
             squared = total * total
             squared = squared[:, :128] + squared[:, 128:]
-            return acc + jnp.sum(squared.reshape(STEP // 8, 8, 128), axis=0)
-
-        acc = pieces(OWN, body, acc)
-        cols = slice(v * COLS, (v + 1) * COLS)
-        copies.append(
-            pltpu.make_async_copy(grad_ref.at[:, cols], grad_hbm.at[:, cols], sems.at[v])
-        )
+            acc = acc + jnp.sum(squared.reshape(rows // 8, 8, 128), axis=0)
+        at = (slice(first, first + rows), slice(left, left + cols))
+        copies.append(pltpu.make_async_copy(grad_ref.at[at], grad_hbm.at[at], sems.at[v]))
         copies[-1].start()
     marked = jnp.where(flag_ref[0, 0] != 0, 1.0, 0.0)
     acc = acc + pltpu.roll(acc, 64, axis=1)
@@ -214,39 +237,58 @@
     )
 
 
-def kernel_call(body, name, ins, outs, scratch, estimate, out_spec=WHOLE):
+def kernel_call(body, name, ins, outs, scratch, estimate, out_specs=None, vmem=KERNEL_VMEM):
     return pl.pallas_call(
         body,
         out_shape=outs,
         in_specs=ins,
-        out_specs=[out_spec] * len(outs),
+        out_specs=out_specs or [WHOLE] * len(outs),
         scratch_shapes=scratch,
-        compiler_params=pltpu.CompilerParams(vmem_limit_bytes=KERNEL_VMEM),
+        compiler_params=pltpu.CompilerParams(vmem_limit_bytes=vmem),
         cost_estimate=estimate,
         name=name,
     )
 
 
-def first(pair, me, x, g, after):
+def head(me, x, g):
+    rows = SHARES[CODED[0]][1]
     return kernel_call(
-        functools.partial(first_kernel, pair),
-        f"first_{pair}",
-        [SCALAR, WHOLE, WHOLE if pair else LEFT, LEFT],
-        [coded(4)] * 2,
-        [pltpu.VMEM((4 * OWN, 2 * COLS), jnp.float32)],
+        head_kernel,
+        "head",
+        [SCALAR, FAR, FAR],
+        [coded(4)] * len(CODED),
+        [
+            pltpu.VMEM((len(CODED), TOK, 4 * rows), jnp.bfloat16),
+            pltpu.VMEM((TOK, KV), jnp.bfloat16),
+            pltpu.VMEM((4 * OWN, COLS), jnp.float32),
+            pltpu.SemaphoreType.DMA((len(CODED), 5)),
+        ],
         cost(8, 1, 1),
-    )(me, x, g, after)
-
-
-def mid(step, me, x, g, after, received):
+        vmem=HEAD_VMEM,
+    )(me, x, g)
+
+
+def work(step, variants, me, x, g, after, arrived):
+    after = after if isinstance(after, list) else [after]
     return kernel_call(
-        functools.partial(mid_kernel, step, 1 if received else 0),
-        f"mid_{step}",
-        [SCALAR, WHOLE, WHOLE, LEFT] + [WHOLE] * len(received),
-        [partial(4) if step == 3 else coded(4)] * VARIANTS,
+        functools.partial(work_kernel, step, variants, len(after)),
+        f"work_{step}_{variants[0]}",
+        [SCALAR, WHOLE, WHOLE] + [LEFT] * len(after) + [WHOLE] * len(arrived),
+        [partial(4) if step == 3 else coded(4)] * len(variants),
         [pltpu.VMEM((4 * OWN, COLS), jnp.float32)],
-        cost(4 * VARIANTS, 1, 1),
-    )(me, x, g, after, *received)
+        cost(4 * len(variants), 1, 1),
+    )(me, x, g, *after, *arrived)
+
+
+def gather(me, x, after):
+    return kernel_call(
+        gather_kernel,
+        "gather",
+        [SCALAR, WHOLE, LEFT],
+        [jax.ShapeDtypeStruct((TOK, 8 * 128), jnp.bfloat16)] * 2,
+        [],
+        cost(4, 0, 1),
+    )(me, x, after)
 
 
 def late(count, v, p, received):
@@ -262,18 +304,18 @@
 
 
 def finish(flag, held):
-    outs = [
-        jax.ShapeDtypeStruct((OWN, KV), jnp.float32),
-        jax.ShapeDtypeStruct((DEVICES, 1, 128), jnp.float32),
-    ]
+    grad = jax.ShapeDtypeStruct((OWN, KV), jnp.float32)
+    report = jax.ShapeDtypeStruct((DEVICES, 1, 128), jnp.float32)
+    far = jax.ShapeDtypeStruct((FAR_ROWS, KV), jnp.float32)
     return kernel_call(
         finish_kernel,
         "finish",
         [SCALAR] + [WHOLE] * len(held),
-        outs,
-        [pltpu.VMEM(o.shape, o.dtype) for o in outs] + [pltpu.SemaphoreType.DMA((VARIANTS + 1,))],
+        [far, report],
+        [pltpu.VMEM(o.shape, o.dtype) for o in (grad, report)]
+        + [pltpu.SemaphoreType.DMA((VARIANTS + 1,))],
         cost(VARIANTS, 0, 3),
-        out_spec=FAR,
+        [FAR] * 2,
     )(flag, *held)
 
 
@@ -336,28 +378,33 @@
     me = lax.axis_index("dp").astype(jnp.int32).reshape(1)
     every = range(VARIANTS)
 
-    def cross(codes, bit):
-        return [swap(codes[v], "dp", RANKS, ORDERS[v][bit]) for v in every]
+    def cross(value, v, bit):
+        return swap(value, "dp", RANKS, ORDERS[v][bit])
 
     x, g = layer_input, value_grad
-    far = lax.bitwise_xor(lax.axis_index("dp") // 4, 2) * (4 * OWN)
-    some = jnp.concatenate(
-        [
-            lax.dynamic_slice(layer_input[0], (0, far), (TOK, 4 * OWN)),
-            value_grad[0, :, PAIRS[0][0] * COLS : (PAIRS[0][1] + 1) * COLS],
-        ],
-        axis=1,
-    )
-    codes = first(0, me, some, me, me)
-    codes = first(1, me, x, g, codes[-1]) + codes
-    zero = cross(codes, 0)
-    codes = mid(1, me, x, g, codes[-1], [])
-    one = cross(codes, 0)
-    codes = mid(2, me, x, g, codes[-1], zero)
-    two = cross(codes, 1)
-    kept = mid(3, me, x, g, codes[-1], one)
-    three = cross([late(2, v, kept[v], [two[v]]) for v in every], 2)
-    four = cross([late(1, v, kept[v], [two[v], three[v]]) for v in every], 3)
+    zero, one, two = ([None] * VARIANTS for _ in range(3))
+    for v in RAW:
+        zero[v] = cross(g[0], v, 0)
+    codes = head(me, x, g)
+    for v, code in zip(CODED, codes):
+        zero[v] = cross(code, v, 0)
+    after = codes[-1]
+    sent = list(gather(me, x, after))
+    after = [sent[-1]] + [zero[v] for v in RAW]
+    sent += work(1, CODED, me, x, g, after, [])
+    for v in every:
+        one[v] = cross(sent[v], v, 0)
+    after = sent[-1]
+    arrived = {v: [zero[v], one[v]] for v in RAW} | {v: [zero[v]] for v in CODED}
+    for variants in (CODED, RAW):
+        codes = work(2, variants, me, x, g, after, [a for v in variants for a in arrived[v]])
+        for v, code in zip(variants, codes):
+            two[v] = cross(code, v, 1)
+        after = codes[-1]
+    arrived |= {v: [one[v]] for v in CODED}
+    kept = work(3, tuple(every), me, x, g, after, [a for v in every for a in arrived[v]])
+    three = [cross(late(2, v, kept[v], [two[v]]), v, 2) for v in every]
+    four = [cross(late(1, v, kept[v], [two[v], three[v]]), v, 3) for v in every]
     held = [a for v in every for a in (kept[v], two[v], three[v], four[v])]
     grad, report = finish(overflow_flags, held)
     reports = lax.all_to_all(report, ("dp", "pipe"), 0, 0)

time: 141 us -> 136 us (0.965)
  Pallas kernels: 44.8 us -> 34.5 us
  starting transfers between devices: 37.6 us -> 45 us
  waiting for transfers between devices: 52.2 us -> 49.8 us
    pallas_call x6 -> x7, Pallas kernels: 32.4 us -> 22.9 us  [the longest x4 14.2 us: work(): kernel_call(functools.partial(work_kernel, step, variants, len(after)), f...]
    all_to_all x1, starting transfers between devices: 12.9 us -> 16.9 us  [per_device(): reports = lax.all_to_all(report, ('dp', 'pipe'), 0, 0)]
    ppermute x20, starting transfers between devices: 24.8 us -> 28.1 us  [swap(): return lax.ppermute(value, axis, [(i, i ^ mask) for i in range(count)])]
    unnamed x8, local copies, waits for them, and re-layouts: 1.96 us -> 5.25 us
    ppermute x20, waiting for transfers between devices: 42.9 us -> 40.5 us  [swap(): return lax.ppermute(value, axis, [(i, i ^ mask) for i in range(count)])]
    dynamic_slice x1 -> x0, local copies, waits for them, and re-layouts: 1.82 us -> none  [per_device(): lax.dynamic_slice(layer_input[0], (0, far), (TOK, 4 * OWN))]
  transfers between devices with their start and end apart: 21 -> 21, of which waited for: 13 -> 13; matrix products, arithmetic and copies ran while one was open for 0% -> 0% of each run, Pallas kernels for 22% -> 17%
where the time goes in v2:
time: 136 us
  waiting for transfers between devices  49.8 us (37%)
  starting transfers between devices  45 us (33%)
  Pallas kernels  34.5 us (25%)
  local copies, waits for them, and re-layouts  5.25 us (4%)
  between operations  1.44 us (1%)
    ppermute x20, waiting for transfers between devices, swap(): return lax.ppermute(value, axis, [(i, i ^ mask) for i in range(count)])  40.5 us
    ppermute x20, starting transfers between devices, swap(): return lax.ppermute(value, axis, [(i, i ^ mask) for i in range(count)])  28.1 us
    all_to_all x1, starting transfers between devices, per_device(): reports = lax.all_to_all(report, ('dp', 'pipe'), 0, 0)  16.9 us
    pallas_call x4, Pallas kernels, work(): kernel_call(functools.partial(work_kernel, step, variants, len(after)), f...  14.2 us
    all_to_all x1, waiting for transfers between devices, per_device(): reports = lax.all_to_all(report, ('dp', 'pipe'), 0, 0)  9.28 us
    pallas_call x1, Pallas kernels, update(): pl.pallas_call(functools.partial(update_kernel, bound), grid=(OWN // UPDA...  7.93 us
    unnamed x8, local copies, waits for them, and re-layouts  5.25 us
    pallas_call x1, Pallas kernels, head(): kernel_call(head_kernel, 'head', [SCALAR, FAR, FAR], [coded(4)] * len(COD...  5.16 us
  transfers between devices with their start and end apart: 21, of which 13 were waited for; matrix products, arithmetic and copies ran while one was open for 0% of the time, Pallas kernels for 17%

profile of v2, /device:TPU:1, one launch (start us, length us, event | category | flops | bytes accessed | tf_op | source)
XLA Modules:
  0.0 136.0 jit_solution(13892312999453026272)
XLA Ops:
  0.6 2.2 %collective-permute-start.1 = (bf16[512,1024]{1,0:T(8,128)(2,1)}, bf16[512,1024]{1,0:T(8,128)(2,1)S(1)}, u32[]{:S(2)}, u32[]{:S(2)}) collective-permute-start(bf16[512,1024]{1,0:T(8,128)(2,1)} %bitcast.3), channel_id=1, source_target_pairs={{0,8},{8,0},{16,24},{24,16},{32,40},{40,32},{48,56},{56,48},{64,72... | collective-permute-start | bytes 3145736 | tf_op jit(solution)/shard_map/ppermute | solution.py:374
  2.8 1.2 collective-permute-start
  4.0 5.2 %head.1 = (s16[2064,256]{1,0:T(8,128)(2,1)}, s16[2064,256]{1,0:T(8,128)(2,1)}) custom-call(s32[1]{0:T(128)} %bitcast.1.me_ref, bf16[1,512,8192]{2,1,0:T(8,128)(2,1)} %x_ref.9, bf16[1,512,1024]{2,1,0:T(8,128)(2,1)} %g_ref.7), custom_call_target="tpu_custom_call" | custom-call | flops 1073741824 | bytes 6291456 | tf_op jit(solution)/shard_map/head/pallas_call | solution.py:255
  9.2 2.0 %collective-permute-start.2 = (s16[2064,256]{1,0:T(8,128)(2,1)}, s16[2064,256]{1,0:T(8,128)(2,1)S(1)}, u32[]{:S(2)}, u32[]{:S(2)}) collective-permute-start(s16[2064,256]{1,0:T(8,128)(2,1)} %get-tuple-element.22), channel_id=1, source_target_pairs={{0,24},{8,16},{16,8},{24,0},{32,56},{40,48},{48,40},{56,32},{64,88... | collective-permute-start | bytes 3170312 | tf_op jit(solution)/shard_map/ppermute | solution.py:374
  11.2 1.8 %collective-permute-start.3 = (s16[2064,256]{1,0:T(8,128)(2,1)}, s16[2064,256]{1,0:T(8,128)(2,1)S(1)}, u32[]{:S(2)}, u32[]{:S(2)}) collective-permute-start(s16[2064,256]{1,0:T(8,128)(2,1)} %get-tuple-element.19.after_ref), channel_id=1, source_target_pairs={{0,96},{8,104},{16,112},{24,120},{32,64},{40,72},{48,80},{56,88},{... | collective-permute-start | bytes 3170312 | tf_op jit(solution)/shard_map/ppermute | solution.py:374
  13.0 3.4 %copy-done = bf16[1,512,8192]{2,1,0:T(8,128)(2,1)S(1)} copy-done((bf16[1,512,8192]{2,1,0:T(8,128)(2,1)S(1)}, bf16[1,512,8192]{2,1,0:T(8,128)(2,1)}, u32[]{:S(2)}) %copy-start) | copy-done | bytes 8388632
  16.4 1.2 copy-done.2
  18.6 6.9 %collective-permute-done.1.refs_2_.refs_3_ = bf16[512,1024]{1,0:T(8,128)(2,1)S(1)} collective-permute-done((bf16[512,1024]{1,0:T(8,128)(2,1)}, bf16[512,1024]{1,0:T(8,128)(2,1)S(1)}, u32[]{:S(2)}, u32[]{:S(2)}) %collective-permute-start.1) | collective-permute-done | bytes 1048608 | tf_op jit(solution)/shard_map/ppermute | solution.py:374
  25.5 1.6 %collective-permute-start.5 = (bf16[512,1024]{1,0:T(8,128)(2,1)S(1)}, bf16[512,1024]{1,0:T(8,128)(2,1)S(1)}, u32[]{:S(2)}, u32[]{:S(2)}) collective-permute-start(bf16[512,1024]{1,0:T(8,128)(2,1)S(1)} %get-tuple-element.20.refs_0_), channel_id=1, source_target_pairs={{0,8},{8,0},{16,24},{24,16},{32,40},{40,32},{48,56},{56,48},{64,72... | collective-permute-start | bytes 3145736 | tf_op jit(solution)/shard_map/ppermute | solution.py:374
  27.1 2.5 %work_1_2.1 = (s16[2064,256]{1,0:T(8,128)(2,1)S(1)}, s16[2064,256]{1,0:T(8,128)(2,1)S(1)}) custom-call(s32[1]{0:T(128)} %bitcast.1.me_ref, bf16[1,512,8192]{2,1,0:T(8,128)(2,1)S(1)} %copy-done, bf16[1,512,1024]{2,1,0:T(8,128)(2,1)S(1)} %copy-done.1, bf16[512,1024]{1,0:T(8,128)(2,1)S(1)} %get-tuple-element.20.refs_0_, ...), custom_call_target="tpu_custom_call" | custom-call | flops 1073741824 | bytes 6291456 | tf_op jit(solution)/shard_map/work_1_2/pallas_call | solution.py:273
  29.6 1.9 %collective-permute-start.6 = (s16[2064,256]{1,0:T(8,128)(2,1)S(1)}, s16[2064,256]{1,0:T(8,128)(2,1)S(1)}, u32[]{:S(2)}, u32[]{:S(2)}) collective-permute-start(s16[2064,256]{1,0:T(8,128)(2,1)S(1)} %get-tuple-element.26), channel_id=1, source_target_pairs={{0,24},{8,16},{16,8},{24,0},{32,56},{40,48},{48,40},{56,32},{64,88... | collective-permute-start | bytes 3170312 | tf_op jit(solution)/shard_map/ppermute | solution.py:374
  31.6 2.7 %collective-permute-done.2.refs_1_ = s16[2064,256]{1,0:T(8,128)(2,1)S(1)} collective-permute-done((s16[2064,256]{1,0:T(8,128)(2,1)}, s16[2064,256]{1,0:T(8,128)(2,1)S(1)}, u32[]{:S(2)}, u32[]{:S(2)}) %collective-permute-start.2) | collective-permute-done | bytes 1056800 | tf_op jit(solution)/shard_map/ppermute | solution.py:374
  34.3 1.8 %collective-permute-start.7 = (s16[2064,256]{1,0:T(8,128)(2,1)S(1)}, s16[2064,256]{1,0:T(8,128)(2,1)S(1)}, u32[]{:S(2)}, u32[]{:S(2)}) collective-permute-start(s16[2064,256]{1,0:T(8,128)(2,1)S(1)} %get-tuple-element.21.refs_0_), channel_id=1, source_target_pairs={{0,96},{8,104},{16,112},{24,120},{32,64},{40,72},{48,80},{56,88},{... | collective-permute-start | bytes 3170312 | tf_op jit(solution)/shard_map/ppermute | solution.py:374
  36.1 3.5 %work_2_2.1 = (s16[2064,256]{1,0:T(8,128)(2,1)S(1)}, s16[2064,256]{1,0:T(8,128)(2,1)S(1)}) custom-call(s32[1]{0:T(128)} %bitcast.1.me_ref, bf16[1,512,8192]{2,1,0:T(8,128)(2,1)S(1)} %copy-done, bf16[1,512,1024]{2,1,0:T(8,128)(2,1)S(1)} %copy-done.1, s16[2064,256]{1,0:T(8,128)(2,1)S(1)} %get-tuple-element.21.refs_0_, ...), custom_call_target="tpu_custom_call" | custom-call | flops 1073741824 | bytes 6291456 | tf_op jit(solution)/shard_map/work_2_2/pallas_call | solution.py:273
  39.9 9.3 %collective-permute-done.4.refs_2_ = bf16[512,1024]{1,0:T(8,128)(2,1)S(1)} collective-permute-done((bf16[512,1024]{1,0:T(8,128)(2,1)S(1)}, bf16[512,1024]{1,0:T(8,128)(2,1)S(1)}, u32[]{:S(2)}, u32[]{:S(2)}) %collective-permute-start.4) | collective-permute-done | bytes 1048608 | tf_op jit(solution)/shard_map/ppermute | solution.py:374
  49.2 1.2 collective-permute-start.17
  50.4 3.6 %work_2_0.1 = (s16[2064,256]{1,0:T(8,128)(2,1)S(1)}, s16[2064,256]{1,0:T(8,128)(2,1)S(1)}) custom-call(s32[1]{0:T(128)} %bitcast.1.me_ref, bf16[1,512,8192]{2,1,0:T(8,128)(2,1)S(1)} %copy-done, bf16[1,512,1024]{2,1,0:T(8,128)(2,1)S(1)} %copy-done.1, s16[2064,256]{1,0:T(8,128)(2,1)S(1)} %get-tuple-element.23.refs_0_, ...), custom_call_target="tpu_custom_call" | custom-call | flops 1073741824 | bytes 6291456 | tf_op jit(solution)/shard_map/work_2_0/pallas_call | solution.py:273
  54.0 2.0 %collective-permute-start.11 = (s16[2064,256]{1,0:T(8,128)(2,1)S(1)}, s16[2064,256]{1,0:T(8,128)(2,1)S(1)}, u32[]{:S(2)}, u32[]{:S(2)}) collective-permute-start(s16[2064,256]{1,0:T(8,128)(2,1)S(1)} %get-tuple-element.25.refs_0_), channel_id=1, source_target_pairs={{0,24},{8,16},{16,8},{24,0},{32,56},{40,48},{48,40},{56,32},{64,88... | collective-permute-start | bytes 3170312 | tf_op jit(solution)/shard_map/ppermute | solution.py:374
  57.0 1.8 %collective-permute-start.8 = (s16[2064,256]{1,0:T(8,128)(2,1)S(1)}, s16[2064,256]{1,0:T(8,128)(2,1)S(1)}, u32[]{:S(2)}, u32[]{:S(2)}) collective-permute-start(s16[2064,256]{1,0:T(8,128)(2,1)S(1)} %get-tuple-element.28), channel_id=1, source_target_pairs={{0,96},{8,104},{16,112},{24,120},{32,64},{40,72},{48,80},{56,88},{... | collective-permute-start | bytes 3170312 | tf_op jit(solution)/shard_map/ppermute | solution.py:374
  58.8 4.6 %work_3_0.1 = (f32[2048,256]{1,0:T(8,128)S(1)}, f32[2048,256]{1,0:T(8,128)S(1)}, f32[2048,256]{1,0:T(8,128)S(1)}, f32[2048,256]{1,0:T(8,128)S(1)}) custom-call(s32[1]{0:T(128)} %bitcast.1.me_ref, bf16[1,512,8192]{2,1,0:T(8,128)(2,1)S(1)} %copy-done, bf16[1,512,1024]{2,1,0:T(8,128)(2,1)S(1)} %copy-done.1, s16[2064,256]{1,0:T(8,128)(2,1)S(1)} %get-tuple-element.25.refs_0_, ...), custom_call_target="tpu_custom_call" | custom-call | flops 2147483648 | bytes 12582912 | tf_op jit(solution)/shard_map/work_3_0/pallas_call | solution.py:273
  63.4 8.8 %collective-permute-done.17.refs_0_.refs_14_ = s16[2064,256]{1,0:T(8,128)(2,1)S(1)} collective-permute-done((s16[2064,256]{1,0:T(8,128)(2,1)S(1)}, s16[2064,256]{1,0:T(8,128)(2,1)S(1)}, u32[]{:S(2)}, u32[]{:S(2)}) %collective-permute-start.17) | collective-permute-done | bytes 1056800 | tf_op jit(solution)/shard_map/ppermute | solution.py:374
  73.4 1.4 collective-permute-start.15
  74.8 3.9 %collective-permute-done.11.refs_0_.refs_6_ = s16[2064,256]{1,0:T(8,128)(2,1)S(1)} collective-permute-done((s16[2064,256]{1,0:T(8,128)(2,1)S(1)}, s16[2064,256]{1,0:T(8,128)(2,1)S(1)}, u32[]{:S(2)}, u32[]{:S(2)}) %collective-permute-start.11) | collective-permute-done | bytes 1056800 | tf_op jit(solution)/shard_map/ppermute | solution.py:374
  80.8 1.9 %collective-permute-start.9 = (s16[1040,256]{1,0:T(8,128)(2,1)S(1)}, s16[1040,256]{1,0:T(8,128)(2,1)S(1)}, u32[]{:S(2)}, u32[]{:S(2)}) collective-permute-start(s16[1040,256]{1,0:T(8,128)(2,1)S(1)} %late_2_0.1), channel_id=1, source_target_pairs={{0,24},{8,16},{16,8},{24,0},{32,56},{40,48},{48,40},{56,32},{64,88... | collective-permute-start | bytes 1597448 | tf_op jit(solution)/shard_map/ppermute | solution.py:374
  84.0 2.0 %collective-permute-start.19 = (s16[528,256]{1,0:T(8,128)(2,1)S(1)}, s16[528,256]{1,0:T(8,128)(2,1)S(1)}, u32[]{:S(2)}, u32[]{:S(2)}) collective-permute-start(s16[528,256]{1,0:T(8,128)(2,1)S(1)} %late_1_3.1), channel_id=1, source_target_pairs={{0,24},{8,16},{16,8},{24,0},{32,56},{40,48},{48,40},{56,32},{64,88... | collective-permute-start | bytes 811016 | tf_op jit(solution)/shard_map/ppermute | solution.py:374
  86.4 2.6 %collective-permute-start.16 = (s16[528,256]{1,0:T(8,128)(2,1)S(1)}, s16[528,256]{1,0:T(8,128)(2,1)S(1)}, u32[]{:S(2)}, u32[]{:S(2)}) collective-permute-start(s16[528,256]{1,0:T(8,128)(2,1)S(1)} %late_1_2.1), channel_id=1, source_target_pairs={{0,96},{8,104},{16,112},{24,120},{32,64},{40,72},{48,80},{56,88},{... | collective-permute-start | bytes 811016 | tf_op jit(solution)/shard_map/ppermute | solution.py:374
  89.0 2.7 %collective-permute-done.12.refs_1_.refs_7_ = s16[1040,256]{1,0:T(8,128)(2,1)S(1)} collective-permute-done((s16[1040,256]{1,0:T(8,128)(2,1)S(1)}, s16[1040,256]{1,0:T(8,128)(2,1)S(1)}, u32[]{:S(2)}, u32[]{:S(2)}) %collective-permute-start.12) | collective-permute-done | bytes 532512 | tf_op jit(solution)/shard_map/ppermute | solution.py:374
  94.0 3.4 %collective-permute-done.19.refs_16_ = s16[528,256]{1,0:T(8,128)(2,1)S(1)} collective-permute-done((s16[528,256]{1,0:T(8,128)(2,1)S(1)}, s16[528,256]{1,0:T(8,128)(2,1)S(1)}, u32[]{:S(2)}, u32[]{:S(2)}) %collective-permute-start.19) | collective-permute-done | bytes 270368 | tf_op jit(solution)/shard_map/ppermute | solution.py:374
  98.3 2.9 %finish.1 = (f32[12288,1024]{1,0:T(8,128)}, f32[128,1,128]{2,1,0:T(1,128)}) custom-call(s32[1,1]{1,0:T(1,128)S(6)} %copy.9.refs_0_, f32[2048,256]{1,0:T(8,128)S(1)} %get-tuple-element.27.p_ref.refs_1_, s16[2064,256]{1,0:T(8,128)(2,1)S(1)} %collective-permute-done.8.refs_0_.refs_2_, s16[1040,256]{1,0:T(8,128)(2,1)S(1)} %collective-permute-done.9.refs_1_.refs_3_, ...), custom_call_target="tpu_custom_call" | custom-call | bytes 5242880 | tf_op jit(solution)/shard_map/finish/pallas_call | solution.py:310
  101.2 16.9 %all-to-all-start = ((f32[128,1,128]{2,1,0:T(1,128)}), f32[128,1,128]{2,1,0:T(1,128)S(1)}, u32[]{:S(2)}, u32[]{:S(2)}) async-start(f32[128,1,128]{2,1,0:T(1,128)} %get-tuple-element.33), calls=%async_computation | async-start | bytes 131072 | tf_op jit(solution)/shard_map/all_to_all | solution.py:410
  118.1 9.3 %all-to-all-done.reports = f32[128,1,128]{2,1,0:T(1,128)S(1)} async-done(((f32[128,1,128]{2,1,0:T(1,128)}), f32[128,1,128]{2,1,0:T(1,128)S(1)}, u32[]{:S(2)}, u32[]{:S(2)}) %all-to-all-start) | async-done | bytes 65568 | tf_op jit(solution)/shard_map/all_to_all | solution.py:410
  128.0 7.9 %update.1 = (f32[1,512,1024]{2,1,0:T(8,128)}, f32[1,512,1024]{2,1,0:T(8,128)}, f32[1,512,1024]{2,1,0:T(8,128)}) custom-call(s32[1]{0:T(128)} %bitcast.pipe_ref, f32[128,1,128]{2,1,0:T(1,128)} %copy-done.3, f32[1,512,1024]{2,1,0:T(8,128)} %w_ref.1, f32[1,512,1024]{2,1,0:T(8,128)} %m1_ref.1, f32[1,512,1024]{2,1,0:T(8,128)} %m2_ref.1, ...), custom_call_target="tpu_custom_call" | custom-call | tf_op jit(solution)/shard_map/update/pallas_call | solution.py:360
  (34 shorter events, 10.3 us)
Async XLA Ops:
  0.6 24.9 %collective-permute-start.1 = (bf16[512,1024]{1,0:T(8,128)(2,1)}, bf16[512,1024]{1,0:T(8,128)(2,1)S(1)}, u32[]{:S(2)}, u32[]{:S(2)}) collective-permute-start(bf16[512,1024]{1,0:T(8,128)(2,1)} %bitcast.3), channel_id=1, source_target_pairs={{0,8},{8,0},{16,24},{24,16},{32,40},{40,32},{48,56},{56,48},{64,72... | collective-permute-start | bytes 3145736 | tf_op jit(solution)/shard_map/ppermute | solution.py:374
  2.8 24.2 %collective-permute-start = (bf16[512,1024]{1,0:T(8,128)(2,1)}, bf16[512,1024]{1,0:T(8,128)(2,1)S(1)}, u32[]{:S(2)}, u32[]{:S(2)}) collective-permute-start(bf16[512,1024]{1,0:T(8,128)(2,1)} %bitcast.4), channel_id=1, source_target_pairs={{0,32},{8,40},{16,48},{24,56},{32,0},{40,8},{48,16},{56,24},{64,96... | collective-permute-start | bytes 3145736 | tf_op jit(solution)/shard_map/ppermute | solution.py:374
  9.2 25.1 %collective-permute-start.2 = (s16[2064,256]{1,0:T(8,128)(2,1)}, s16[2064,256]{1,0:T(8,128)(2,1)S(1)}, u32[]{:S(2)}, u32[]{:S(2)}) collective-permute-start(s16[2064,256]{1,0:T(8,128)(2,1)} %get-tuple-element.22), channel_id=1, source_target_pairs={{0,24},{8,16},{16,8},{24,0},{32,56},{40,48},{48,40},{56,32},{64,88... | collective-permute-start | bytes 3170312 | tf_op jit(solution)/shard_map/ppermute | solution.py:374
  11.2 24.9 %collective-permute-start.3 = (s16[2064,256]{1,0:T(8,128)(2,1)}, s16[2064,256]{1,0:T(8,128)(2,1)S(1)}, u32[]{:S(2)}, u32[]{:S(2)}) collective-permute-start(s16[2064,256]{1,0:T(8,128)(2,1)} %get-tuple-element.19.after_ref), channel_id=1, source_target_pairs={{0,96},{8,104},{16,112},{24,120},{32,64},{40,72},{48,80},{56,88},{... | collective-permute-start | bytes 3170312 | tf_op jit(solution)/shard_map/ppermute | solution.py:374
  13.0 3.4 %copy-start = (bf16[1,512,8192]{2,1,0:T(8,128)(2,1)S(1)}, bf16[1,512,8192]{2,1,0:T(8,128)(2,1)}, u32[]{:S(2)}) copy-start(bf16[1,512,8192]{2,1,0:T(8,128)(2,1)} %x_ref.9) | copy-start | bytes 25165828
  16.4 1.2 copy-start.2
  17.6 9.5 %copy-start.1 = (bf16[1,512,1024]{2,1,0:T(8,128)(2,1)S(1)}, bf16[1,512,1024]{2,1,0:T(8,128)(2,1)}, u32[]{:S(2)}) copy-start(bf16[1,512,1024]{2,1,0:T(8,128)(2,1)} %g_ref.7) | copy-start | bytes 3145732
  18.2 31.0 %collective-permute-start.4 = (bf16[512,1024]{1,0:T(8,128)(2,1)S(1)}, bf16[512,1024]{1,0:T(8,128)(2,1)S(1)}, u32[]{:S(2)}, u32[]{:S(2)}) collective-permute-start(bf16[512,1024]{1,0:T(8,128)(2,1)S(1)} %get-tuple-element.24), channel_id=1, source_target_pairs={{0,32},{8,40},{16,48},{24,56},{32,0},{40,8},{48,16},{56,24},{64,96... | collective-permute-start | bytes 3145736 | tf_op jit(solution)/shard_map/ppermute | solution.py:374
  25.5 24.9 %collective-permute-start.5 = (bf16[512,1024]{1,0:T(8,128)(2,1)S(1)}, bf16[512,1024]{1,0:T(8,128)(2,1)S(1)}, u32[]{:S(2)}, u32[]{:S(2)}) collective-permute-start(bf16[512,1024]{1,0:T(8,128)(2,1)S(1)} %get-tuple-element.20.refs_0_), channel_id=1, source_target_pairs={{0,8},{8,0},{16,24},{24,16},{32,40},{40,32},{48,56},{56,48},{64,72... | collective-permute-start | bytes 3145736 | tf_op jit(solution)/shard_map/ppermute | solution.py:374
  29.6 27.3 %collective-permute-start.6 = (s16[2064,256]{1,0:T(8,128)(2,1)S(1)}, s16[2064,256]{1,0:T(8,128)(2,1)S(1)}, u32[]{:S(2)}, u32[]{:S(2)}) collective-permute-start(s16[2064,256]{1,0:T(8,128)(2,1)S(1)} %get-tuple-element.26), channel_id=1, source_target_pairs={{0,24},{8,16},{16,8},{24,0},{32,56},{40,48},{48,40},{56,32},{64,88... | collective-permute-start | bytes 3170312 | tf_op jit(solution)/shard_map/ppermute | solution.py:374
  34.3 24.5 %collective-permute-start.7 = (s16[2064,256]{1,0:T(8,128)(2,1)S(1)}, s16[2064,256]{1,0:T(8,128)(2,1)S(1)}, u32[]{:S(2)}, u32[]{:S(2)}) collective-permute-start(s16[2064,256]{1,0:T(8,128)(2,1)S(1)} %get-tuple-element.21.refs_0_), channel_id=1, source_target_pairs={{0,96},{8,104},{16,112},{24,120},{32,64},{40,72},{48,80},{56,88},{... | collective-permute-start | bytes 3170312 | tf_op jit(solution)/shard_map/ppermute | solution.py:374
  39.7 33.2 %collective-permute-start.14 = (s16[2064,256]{1,0:T(8,128)(2,1)S(1)}, s16[2064,256]{1,0:T(8,128)(2,1)S(1)}, u32[]{:S(2)}, u32[]{:S(2)}) collective-permute-start(s16[2064,256]{1,0:T(8,128)(2,1)S(1)} %get-tuple-element.31), channel_id=1, source_target_pairs={{0,8},{8,0},{16,24},{24,16},{32,40},{40,32},{48,56},{56,48},{64,72... | collective-permute-start | bytes 3170312 | tf_op jit(solution)/shard_map/ppermute | solution.py:374
  49.2 23.0 %collective-permute-start.17 = (s16[2064,256]{1,0:T(8,128)(2,1)S(1)}, s16[2064,256]{1,0:T(8,128)(2,1)S(1)}, u32[]{:S(2)}, u32[]{:S(2)}) collective-permute-start(s16[2064,256]{1,0:T(8,128)(2,1)S(1)} %get-tuple-element.23.refs_0_), channel_id=1, source_target_pairs={{0,32},{8,40},{16,48},{24,56},{32,0},{40,8},{48,16},{56,24},{64,96... | collective-permute-start | bytes 3170312 | tf_op jit(solution)/shard_map/ppermute | solution.py:374
  54.0 24.7 %collective-permute-start.11 = (s16[2064,256]{1,0:T(8,128)(2,1)S(1)}, s16[2064,256]{1,0:T(8,128)(2,1)S(1)}, u32[]{:S(2)}, u32[]{:S(2)}) collective-permute-start(s16[2064,256]{1,0:T(8,128)(2,1)S(1)} %get-tuple-element.25.refs_0_), channel_id=1, source_target_pairs={{0,24},{8,16},{16,8},{24,0},{32,56},{40,48},{48,40},{56,32},{64,88... | collective-permute-start | bytes 3170312 | tf_op jit(solution)/shard_map/ppermute | solution.py:374
  57.0 23.3 %collective-permute-start.8 = (s16[2064,256]{1,0:T(8,128)(2,1)S(1)}, s16[2064,256]{1,0:T(8,128)(2,1)S(1)}, u32[]{:S(2)}, u32[]{:S(2)}) collective-permute-start(s16[2064,256]{1,0:T(8,128)(2,1)S(1)} %get-tuple-element.28), channel_id=1, source_target_pairs={{0,96},{8,104},{16,112},{24,120},{32,64},{40,72},{48,80},{56,88},{... | collective-permute-start | bytes 3170312 | tf_op jit(solution)/shard_map/ppermute | solution.py:374
  72.7 10.9 %collective-permute-start.18 = (s16[1040,256]{1,0:T(8,128)(2,1)S(1)}, s16[1040,256]{1,0:T(8,128)(2,1)S(1)}, u32[]{:S(2)}, u32[]{:S(2)}) collective-permute-start(s16[1040,256]{1,0:T(8,128)(2,1)S(1)} %late_2_3.1), channel_id=1, source_target_pairs={{0,8},{8,0},{16,24},{24,16},{32,40},{40,32},{48,56},{56,48},{64,72... | collective-permute-start | bytes 1597448 | tf_op jit(solution)/shard_map/ppermute | solution.py:374
  73.4 12.6 %collective-permute-start.15 = (s16[1040,256]{1,0:T(8,128)(2,1)S(1)}, s16[1040,256]{1,0:T(8,128)(2,1)S(1)}, u32[]{:S(2)}, u32[]{:S(2)}) collective-permute-start(s16[1040,256]{1,0:T(8,128)(2,1)S(1)} %late_2_2.1), channel_id=1, source_target_pairs={{0,32},{8,40},{16,48},{24,56},{32,0},{40,8},{48,16},{56,24},{64,96... | collective-permute-start | bytes 1597448 | tf_op jit(solution)/shard_map/ppermute | solution.py:374
  79.2 12.4 %collective-permute-start.12 = (s16[1040,256]{1,0:T(8,128)(2,1)S(1)}, s16[1040,256]{1,0:T(8,128)(2,1)S(1)}, u32[]{:S(2)}, u32[]{:S(2)}) collective-permute-start(s16[1040,256]{1,0:T(8,128)(2,1)S(1)} %late_2_1.1), channel_id=1, source_target_pairs={{0,96},{8,104},{16,112},{24,120},{32,64},{40,72},{48,80},{56,88},{... | collective-permute-start | bytes 1597448 | tf_op jit(solution)/shard_map/ppermute | solution.py:374
  80.8 11.3 %collective-permute-start.9 = (s16[1040,256]{1,0:T(8,128)(2,1)S(1)}, s16[1040,256]{1,0:T(8,128)(2,1)S(1)}, u32[]{:S(2)}, u32[]{:S(2)}) collective-permute-start(s16[1040,256]{1,0:T(8,128)(2,1)S(1)} %late_2_0.1), channel_id=1, source_target_pairs={{0,24},{8,16},{16,8},{24,0},{32,56},{40,48},{48,40},{56,32},{64,88... | collective-permute-start | bytes 1597448 | tf_op jit(solution)/shard_map/ppermute | solution.py:374
  84.0 13.3 %collective-permute-start.19 = (s16[528,256]{1,0:T(8,128)(2,1)S(1)}, s16[528,256]{1,0:T(8,128)(2,1)S(1)}, u32[]{:S(2)}, u32[]{:S(2)}) collective-permute-start(s16[528,256]{1,0:T(8,128)(2,1)S(1)} %late_1_3.1), channel_id=1, source_target_pairs={{0,24},{8,16},{16,8},{24,0},{32,56},{40,48},{48,40},{56,32},{64,88... | collective-permute-start | bytes 811016 | tf_op jit(solution)/shard_map/ppermute | solution.py:374
  86.4 11.0 %collective-permute-start.16 = (s16[528,256]{1,0:T(8,128)(2,1)S(1)}, s16[528,256]{1,0:T(8,128)(2,1)S(1)}, u32[]{:S(2)}, u32[]{:S(2)}) collective-permute-start(s16[528,256]{1,0:T(8,128)(2,1)S(1)} %late_1_2.1), channel_id=1, source_target_pairs={{0,96},{8,104},{16,112},{24,120},{32,64},{40,72},{48,80},{56,88},{... | collective-permute-start | bytes 811016 | tf_op jit(solution)/shard_map/ppermute | solution.py:374
  92.1 5.7 %collective-permute-start.13 = (s16[528,256]{1,0:T(8,128)(2,1)S(1)}, s16[528,256]{1,0:T(8,128)(2,1)S(1)}, u32[]{:S(2)}, u32[]{:S(2)}) collective-permute-start(s16[528,256]{1,0:T(8,128)(2,1)S(1)} %late_1_1.1), channel_id=1, source_target_pairs={{0,32},{8,40},{16,48},{24,56},{32,0},{40,8},{48,16},{56,24},{64,96... | collective-permute-start | bytes 811016 | tf_op jit(solution)/shard_map/ppermute | solution.py:374
  92.6 5.7 %collective-permute-start.10 = (s16[528,256]{1,0:T(8,128)(2,1)S(1)}, s16[528,256]{1,0:T(8,128)(2,1)S(1)}, u32[]{:S(2)}, u32[]{:S(2)}) collective-permute-start(s16[528,256]{1,0:T(8,128)(2,1)S(1)} %late_1_0.1), channel_id=1, source_target_pairs={{0,8},{8,0},{16,24},{24,16},{32,40},{40,32},{48,56},{56,48},{64,72... | collective-permute-start | bytes 811016 | tf_op jit(solution)/shard_map/ppermute | solution.py:374
  101.2 26.2 %all-to-all-start = ((f32[128,1,128]{2,1,0:T(1,128)}), f32[128,1,128]{2,1,0:T(1,128)S(1)}, u32[]{:S(2)}, u32[]{:S(2)}) async-start(f32[128,1,128]{2,1,0:T(1,128)} %get-tuple-element.33), calls=%async_computation | async-start | bytes 131072 | tf_op jit(solution)/shard_map/all_to_all | solution.py:410
  127.4 0.6 copy-start.3

commit v3 on v2

--- a/solution.py
+++ b/solution.py
@@ -20,22 +20,28 @@
 VARIANTS = 4
 STEP = 512
 KERNEL_VMEM = 14 << 20
-HEAD_VMEM = 121 << 19
+HEAD_VMEM = 57 << 20
 UPDATE_VMEM = 60 << 20
 TOP_POWER = 29.9985
 SCALE_ROWS = 16
 
 XA, XB, YA, YB = 4, 12, 1, 3
-ORDERS = ((XA, XB, YB, YA), (YA, YB, XB, XA), (YB, YA, XA, XB), (XB, XA, YA, YB))
+ORDERS = (
+    ((XA, XB, YB, YA), (YA, YB, XB, XA), (YB, YA, XA, XB), (XB, XA, YA, YB)),
+    ((XB, XA, YA, YB), (YB, YA, XA, XB), (YA, YB, XB, XA), (XA, XB, YB, YA)),
+)
 RAW, CODED = (0, 1), (2, 3)
 SHARES = ((0, 128, 0, 1024), (128, 128, 0, 1024), (256, 256, 0, 512), (256, 256, 512, 512))
 
 TRANSPOSED = (((0,), (0,)), ((), ()))
 
 
-def masks_of(order, step):
-    base = {0: order[0] ^ order[1], 1: order[0], 2: order[1], 3: 0}[step]
-    return [base, base ^ order[3], base ^ order[2], base ^ order[2] ^ order[3]]
+def masks_of(v, step):
+    masks = []
+    for order in (orders[v] for orders in ORDERS):
+        base = {0: order[0] ^ order[1], 1: order[0], 2: order[1], 3: 0}[step]
+        masks.append([base, base ^ order[3], base ^ order[2], base ^ order[2] ^ order[3]])
+    return list(zip(*masks))
 
 
 def decode(codes, scale):
@@ -49,7 +55,7 @@
 
 
 def columns_of(me_ref, mask, v):
-    block = jnp.bitwise_xor(me_ref[0], mask)
+    block = jnp.bitwise_xor(me_ref[0], jnp.where(me_ref[1] == 0, *mask))
     first, rows = SHARES[v][:2]
     return pl.ds(pl.multiple_of(block * OWN + first, 128), rows)
 
@@ -117,8 +123,8 @@
 
 
 def head_kernel(me_ref, x_hbm, g_hbm, *refs):
-    outs, (x_buf, g_buf, sums, sems) = refs[: len(CODED)], refs[len(CODED) :]
-    copies = []
+    outs, raw, (x_buf, g_buf, sums, sems, raw_sems) = refs[:2], refs[2:4], refs[4:]
+    copies, raw_copies = [], []
     for i, v in enumerate(CODED):
         _, rows, first, cols = SHARES[v]
         at = (slice(None), slice(first, first + cols))
@@ -130,17 +136,29 @@
                     x_buf.at[i, :, slot * rows : (slot + 1) * rows],
                     sems.at[i, slot],
                 )
-                for slot, mask in enumerate(masks_of(ORDERS[v], 0))
+                for slot, mask in enumerate(masks_of(v, 0))
             ]
         )
         for copy in copies[-1]:
             copy.start()
+    for i, v in enumerate(RAW):
+        for slot, mask in enumerate(masks_of(v, 0) + masks_of(v, 1)):
+            raw_copies.append(
+                pltpu.make_async_copy(
+                    x_hbm.at[0, :, columns_of(me_ref, mask, v)],
+                    raw[i].at[:, slot * 128 : (slot + 1) * 128],
+                    raw_sems.at[i, slot],
+                )
+            )
+            raw_copies[-1].start()
     for i, v in enumerate(CODED):
         _, _, first, cols = SHARES[v]
         for copy in copies[i]:
             copy.wait()
         largest = multiply(v, x_buf[i], g_buf[:, first : first + cols], sums)
         encode(largest, sums, 4, outs[i])
+    for copy in raw_copies:
+        copy.wait()
 
 
 def work_kernel(step, variants, unread, me_ref, x_ref, g_ref, *refs):
@@ -151,7 +169,7 @@
     outs, sums = refs[:-1], refs[-1]
     for v, there, out in zip(variants, arrived, outs):
         _, rows, first, cols = SHARES[v]
-        x = [x_ref[0, :, columns_of(me_ref, mask, v)] for mask in masks_of(ORDERS[v], step)]
+        x = [x_ref[0, :, columns_of(me_ref, mask, v)] for mask in masks_of(v, step)]
         x, g = jnp.concatenate(x, axis=1), g_ref[0, :, first : first + cols]
         if v in RAW:
             half = slice(4 * rows * (step - 2), 4 * rows * (step - 1))
@@ -165,13 +183,6 @@
             encode(largest, sums, 4, out)
 
 
-def gather_kernel(me_ref, x_ref, after_ref, *outs):
-    for v, out in zip(RAW, outs):
-        masks = masks_of(ORDERS[v], 0) + masks_of(ORDERS[v], 1)
-        for slot, mask in enumerate(masks):
-            out[:, slot * 128 : (slot + 1) * 128] = x_ref[0, :, columns_of(me_ref, mask, v)]
-
-
 def late_kernel(count, arrivals, p_ref, *refs):
     received, out, sums = refs[:arrivals], refs[arrivals], refs[arrivals + 1]
     first = count * OWN
@@ -181,13 +192,23 @@
     encode(largest, sums, count, out)
 
 
+def sum_kernel(*refs):
+    outs = refs[3 * VARIANTS :]
+    for v, out in enumerate(outs):
+        p_ref, *received = refs[3 * v : 3 * v + 3]
+        total = p_ref[:OWN, :]
+        for r, scale in zip(received, scales_of(received)):
+            total = total + decode(r[:OWN, :], scale)
+        out[...] = total
+
+
 def finish_kernel(*refs):
     flag_ref = refs[0]
     grad_hbm, report_hbm, grad_ref, report_ref, sems = refs[-5:]
     copies = []
     acc = jnp.zeros((8, 128), jnp.float32)
     for v in range(VARIANTS):
-        p_ref, *received = refs[1 + 4 * v : 5 + 4 * v]
+        p_ref, *received = refs[1 + 2 * v : 3 + 2 * v]
         scales = scales_of(received)
         first, rows, left, cols = SHARES[v]
         for group in range(cols // COLS):
@@ -256,12 +277,13 @@
         head_kernel,
         "head",
         [SCALAR, FAR, FAR],
-        [coded(4)] * len(CODED),
+        [coded(4)] * len(CODED) + [jax.ShapeDtypeStruct((TOK, 8 * 128), jnp.bfloat16)] * len(RAW),
         [
             pltpu.VMEM((len(CODED), TOK, 4 * rows), jnp.bfloat16),
             pltpu.VMEM((TOK, KV), jnp.bfloat16),
             pltpu.VMEM((4 * OWN, COLS), jnp.float32),
             pltpu.SemaphoreType.DMA((len(CODED), 5)),
+            pltpu.SemaphoreType.DMA((len(RAW), 8)),
         ],
         cost(8, 1, 1),
         vmem=HEAD_VMEM,
@@ -280,17 +302,6 @@
     )(me, x, g, *after, *arrived)
 
 
-def gather(me, x, after):
-    return kernel_call(
-        gather_kernel,
-        "gather",
-        [SCALAR, WHOLE, LEFT],
-        [jax.ShapeDtypeStruct((TOK, 8 * 128), jnp.bfloat16)] * 2,
-        [],
-        cost(4, 0, 1),
-    )(me, x, after)
-
-
 def late(count, v, p, received):
     [code] = kernel_call(
         functools.partial(late_kernel, count, len(received)),
@@ -301,6 +312,17 @@
         cost(count, 0, len(received)),
     )(p, *received)
     return code
+
+
+def sum_own(held):
+    return kernel_call(
+        sum_kernel,
+        "sum",
+        [WHOLE] * len(held),
+        [partial(1)] * VARIANTS,
+        [],
+        cost(VARIANTS, 0, 2),
+    )(*held)
 
 
 def finish(flag, held):
@@ -319,7 +341,7 @@
     )(flag, *held)
 
 
-UPDATE_ROWS = 128
+UPDATE_ROWS = 256
 
 
 def update_kernel(bound, pipe_ref, reports, w_ref, m1_ref, m2_ref, g_ref, *refs):
@@ -348,7 +370,8 @@
     scaled = clip * g_ref[...]
     first = 0.9 * first_old + 0.1 * scaled
     second = 0.95 * second_old + 0.05 * scaled * scaled
-    updated = w - 0.02 * (first / (jnp.sqrt(second) + 1e-08) + 0.1 * w)
+    root = second * lax.rsqrt(second)
+    updated = w - 0.02 * (first / (root + 1e-08) + 0.1 * w)
     new_w[0] = jnp.where(keep, updated, w)
     new_m1[0] = jnp.where(keep, first, first_old)
     new_m2[0] = jnp.where(keep, second, second_old)
@@ -370,28 +393,30 @@
     )(pipe, reports, w, m1, m2, grad)
 
 
-def swap(value, axis, count, mask):
-    return lax.ppermute(value, axis, [(i, i ^ mask) for i in range(count)])
+def swap(value, masks):
+    pairs = []
+    for rank in range(RANKS):
+        for pipe in range(PIPE):
+            pairs.append((rank * PIPE + pipe, (rank ^ masks[pipe % 2]) * PIPE + pipe))
+    return lax.ppermute(value, ("dp", "pipe"), pairs)
 
 
 def per_device(layer_input, value_grad, master_weight, moment_one, moment_two, overflow_flags):
-    me = lax.axis_index("dp").astype(jnp.int32).reshape(1)
+    rank, core = lax.axis_index("dp"), lax.axis_index("pipe") % 2
+    me = jnp.stack([rank, core]).astype(jnp.int32)
     every = range(VARIANTS)
 
     def cross(value, v, bit):
-        return swap(value, "dp", RANKS, ORDERS[v][bit])
+        return swap(value, [orders[v][bit] for orders in ORDERS])
 
     x, g = layer_input, value_grad
     zero, one, two = ([None] * VARIANTS for _ in range(3))
     for v in RAW:
         zero[v] = cross(g[0], v, 0)
-    codes = head(me, x, g)
+    *codes, raw_0, raw_1 = head(me, x, g)
     for v, code in zip(CODED, codes):
         zero[v] = cross(code, v, 0)
-    after = codes[-1]
-    sent = list(gather(me, x, after))
-    after = [sent[-1]] + [zero[v] for v in RAW]
-    sent += work(1, CODED, me, x, g, after, [])
+    sent = [raw_0, raw_1, *work(1, CODED, me, x, g, [zero[v] for v in RAW], [])]
     for v in every:
         one[v] = cross(sent[v], v, 0)
     after = sent[-1]
@@ -405,7 +430,8 @@
     kept = work(3, tuple(every), me, x, g, after, [a for v in every for a in arrived[v]])
     three = [cross(late(2, v, kept[v], [two[v]]), v, 2) for v in every]
     four = [cross(late(1, v, kept[v], [two[v], three[v]]), v, 3) for v in every]
-    held = [a for v in every for a in (kept[v], two[v], three[v], four[v])]
+    own = sum_own([a for v in every for a in (kept[v], two[v], three[v])])
+    held = [a for v in every for a in (own[v], four[v])]
     grad, report = finish(overflow_flags, held)
     reports = lax.all_to_all(report, ("dp", "pipe"), 0, 0)
     bound = 0.5 * math.sqrt(D * KV * PIPE)

time: 136 us -> 126 us (0.926)
  starting transfers between devices: 45 us -> 23.5 us
  blocking collectives: 0 us -> 18.9 us
  waiting for transfers between devices: 49.8 us -> 40.8 us
  Pallas kernels: 34.5 us -> 37.4 us
  local copies, waits for them, and re-layouts: 5.25 us -> 3.39 us
    all_to_all x0 -> x1, blocking collectives: none -> 18.9 us  [per_device(): reports = lax.all_to_all(report, ('dp', 'pipe'), 0, 0)]
    all_to_all x1 -> x0, starting transfers between devices: 16.9 us -> none  [per_device(): reports = lax.all_to_all(report, ('dp', 'pipe'), 0, 0)]
    all_to_all x1 -> x0, waiting for transfers between devices: 9.28 us -> none  [per_device(): reports = lax.all_to_all(report, ('dp', 'pipe'), 0, 0)]
    ppermute x20, starting transfers between devices: 28.1 us -> 23.5 us  [swap(): return lax.ppermute(value, ('dp', 'pipe'), pairs)]
    pallas_call x1, Pallas kernels: 5.16 us -> 7.48 us  [head(): kernel_call(head_kernel, 'head', [SCALAR, FAR, FAR], [coded(4)] * len(COD...]
    pallas_call x4, Pallas kernels: 14.2 us -> 16.3 us  [work(): kernel_call(functools.partial(work_kernel, step, variants, len(after)), f...]
    unnamed x8 -> x6, local copies, waits for them, and re-layouts: 5.25 us -> 3.39 us
  transfers between devices with their start and end apart: 21 -> 20, of which waited for: 13 -> 13; matrix products, arithmetic and copies ran while one was open for 0% -> 0% of each run, Pallas kernels for 17% -> 22%
where the time goes in v3:
time: 126 us
  waiting for transfers between devices  40.8 us (32%)
  Pallas kernels  37.4 us (30%)
  starting transfers between devices  23.5 us (19%)
  blocking collectives  18.9 us (15%)
  local copies, waits for them, and re-layouts  3.39 us (3%)
  between operations  1.46 us (1%)
    ppermute x20, waiting for transfers between devices, swap(): return lax.ppermute(value, ('dp', 'pipe'), pairs)  40.8 us
    ppermute x20, starting transfers between devices, swap(): return lax.ppermute(value, ('dp', 'pipe'), pairs)  23.5 us
    all_to_all x1, blocking collectives, per_device(): reports = lax.all_to_all(report, ('dp', 'pipe'), 0, 0)  18.9 us
    pallas_call x4, Pallas kernels, work(): kernel_call(functools.partial(work_kernel, step, variants, len(after)), f...  16.3 us
    pallas_call x1, Pallas kernels, head(): kernel_call(head_kernel, 'head', [SCALAR, FAR, FAR], [coded(4)] * len(COD...  7.48 us
    pallas_call x1, Pallas kernels, update(): pl.pallas_call(functools.partial(update_kernel, bound), grid=(OWN // UPDA...  7.22 us
    pallas_call x8, Pallas kernels, late(): kernel_call(functools.partial(late_kernel, count, len(received)), f'late_...  3.71 us
    unnamed x6, local copies, waits for them, and re-layouts  3.39 us
  transfers between devices with their start and end apart: 20, of which 13 were waited for; matrix products, arithmetic and copies ran while one was open for 0% of the time, Pallas kernels for 22%

profile of v3, /device:TPU:1, one launch (start us, length us, event | category | flops | bytes accessed | tf_op | source)
XLA Modules:
  0.0 126.0 jit_solution(14954763388436628909)
XLA Ops:
  0.6 3.6 %collective-permute-start.1 = (bf16[512,1024]{1,0:T(8,128)(2,1)}, bf16[512,1024]{1,0:T(8,128)(2,1)S(1)}, u32[]{:S(2)}, u32[]{:S(2)}) collective-permute-start(bf16[512,1024]{1,0:T(8,128)(2,1)} %bitcast.4), channel_id=1, source_target_pairs={{0,8},{1,25},{2,10},{3,27},{4,12},{5,29},{6,14},{7,31},{8,0},{9,17... | collective-permute-start | bytes 3145736 | tf_op jit(solution)/shard_map/ppermute | solution.py:401
  4.3 2.5 %collective-permute-start = (bf16[512,1024]{1,0:T(8,128)(2,1)}, bf16[512,1024]{1,0:T(8,128)(2,1)S(1)}, u32[]{:S(2)}, u32[]{:S(2)}) collective-permute-start(bf16[512,1024]{1,0:T(8,128)(2,1)} %bitcast.5), channel_id=1, source_target_pairs={{0,32},{1,97},{2,34},{3,99},{4,36},{5,101},{6,38},{7,103},{8,40},{... | collective-permute-start | bytes 3145736 | tf_op jit(solution)/shard_map/ppermute | solution.py:401
  6.8 0.6 pad_add_fusion.me_ref
  7.3 7.5 %head.1 = (s16[2064,256]{1,0:T(8,128)(2,1)}, s16[2064,256]{1,0:T(8,128)(2,1)}, bf16[512,1024]{1,0:T(8,128)(2,1)}, bf16[512,1024]{1,0:T(8,128)(2,1)}) custom-call(s32[2]{0:T(128)} %pad_add_fusion.me_ref, bf16[1,512,8192]{2,1,0:T(8,128)(2,1)} %x_ref.7, bf16[1,512,1024]{2,1,0:T(8,128)(2,1)} %g_ref.7), custom_call_target="tpu_custom_call" | custom-call | flops 1073741824 | bytes 6291456 | tf_op jit(solution)/shard_map/head/pallas_call | solution.py:276
  15.0 0.8 collective-permute-start.4
  15.8 0.9 collective-permute-done.1.refs_1_.refs_3_
  16.7 2.7 %collective-permute-start.5 = (bf16[512,1024]{1,0:T(8,128)(2,1)}, bf16[512,1024]{1,0:T(8,128)(2,1)S(1)}, u32[]{:S(2)}, u32[]{:S(2)}) collective-permute-start(bf16[512,1024]{1,0:T(8,128)(2,1)} %get-tuple-element.28), channel_id=1, source_target_pairs={{0,8},{1,25},{2,10},{3,27},{4,12},{5,29},{6,14},{7,31},{8,0},{9,17... | collective-permute-start | bytes 3145736 | tf_op jit(solution)/shard_map/ppermute | solution.py:401
  19.6 3.4 %copy-done = bf16[1,512,8192]{2,1,0:T(8,128)(2,1)S(1)} copy-done((bf16[1,512,8192]{2,1,0:T(8,128)(2,1)S(1)}, bf16[1,512,8192]{2,1,0:T(8,128)(2,1)}, u32[]{:S(2)}) %copy-start) | copy-done | bytes 8388632
  23.0 3.1 %work_1_2.1 = (s16[2064,256]{1,0:T(8,128)(2,1)S(1)}, s16[2064,256]{1,0:T(8,128)(2,1)S(1)}) custom-call(s32[2]{0:T(128)S(1)} %copy-done.2, bf16[1,512,8192]{2,1,0:T(8,128)(2,1)S(1)} %copy-done, bf16[1,512,1024]{2,1,0:T(8,128)(2,1)S(1)} %copy-done.1, bf16[512,1024]{1,0:T(8,128)(2,1)S(1)} %collective-permute-done.refs_0_.refs_1_, ...), custom_call_target="tpu_custom_call" | custom-call | flops 1073741824 | bytes 6291456 | tf_op jit(solution)/shard_map/work_1_2/pallas_call | solution.py:295
  26.2 10.4 %collective-permute-done.2.refs_1_ = s16[2064,256]{1,0:T(8,128)(2,1)S(1)} collective-permute-done((s16[2064,256]{1,0:T(8,128)(2,1)}, s16[2064,256]{1,0:T(8,128)(2,1)S(1)}, u32[]{:S(2)}, u32[]{:S(2)}) %collective-permute-start.2) | collective-permute-done | bytes 1056800 | tf_op jit(solution)/shard_map/ppermute | solution.py:401
  36.5 1.8 %collective-permute-done.3.refs_2_ = s16[2064,256]{1,0:T(8,128)(2,1)S(1)} collective-permute-done((s16[2064,256]{1,0:T(8,128)(2,1)}, s16[2064,256]{1,0:T(8,128)(2,1)S(1)}, u32[]{:S(2)}, u32[]{:S(2)}) %collective-permute-start.3) | collective-permute-done | bytes 1056800 | tf_op jit(solution)/shard_map/ppermute | solution.py:401
  38.3 4.0 %work_2_2.1 = (s16[2064,256]{1,0:T(8,128)(2,1)S(1)}, s16[2064,256]{1,0:T(8,128)(2,1)S(1)}) custom-call(s32[2]{0:T(128)S(1)} %copy-done.2, bf16[1,512,8192]{2,1,0:T(8,128)(2,1)S(1)} %copy-done, bf16[1,512,1024]{2,1,0:T(8,128)(2,1)S(1)} %copy-done.1, s16[2064,256]{1,0:T(8,128)(2,1)S(1)} %get-tuple-element.23.refs_0_, ...), custom_call_target="tpu_custom_call" | custom-call | flops 1073741824 | bytes 6291456 | tf_op jit(solution)/shard_map/work_2_2/pallas_call | solution.py:295
  42.3 2.9 %collective-permute-start.12 = (s16[2064,256]{1,0:T(8,128)(2,1)S(1)}, s16[2064,256]{1,0:T(8,128)(2,1)S(1)}, u32[]{:S(2)}, u32[]{:S(2)}) collective-permute-start(s16[2064,256]{1,0:T(8,128)(2,1)S(1)} %get-tuple-element.35), channel_id=1, source_target_pairs={{0,8},{1,25},{2,10},{3,27},{4,12},{5,29},{6,14},{7,31},{8,0},{9,17... | collective-permute-start | bytes 3170312 | tf_op jit(solution)/shard_map/ppermute | solution.py:401
  45.5 4.1 %work_2_0.1 = (s16[2064,256]{1,0:T(8,128)(2,1)S(1)}, s16[2064,256]{1,0:T(8,128)(2,1)S(1)}) custom-call(s32[2]{0:T(128)S(1)} %copy-done.2, bf16[1,512,8192]{2,1,0:T(8,128)(2,1)S(1)} %copy-done, bf16[1,512,1024]{2,1,0:T(8,128)(2,1)S(1)} %copy-done.1, s16[2064,256]{1,0:T(8,128)(2,1)S(1)} %get-tuple-element.26.refs_0_, ...), custom_call_target="tpu_custom_call" | custom-call | flops 1073741824 | bytes 6291456 | tf_op jit(solution)/shard_map/work_2_0/pallas_call | solution.py:295
  49.7 1.0 collective-permute-start.10
  50.7 2.8 %collective-permute-done.6.refs_5_ = s16[2064,256]{1,0:T(8,128)(2,1)S(1)} collective-permute-done((s16[2064,256]{1,0:T(8,128)(2,1)S(1)}, s16[2064,256]{1,0:T(8,128)(2,1)S(1)}, u32[]{:S(2)}, u32[]{:S(2)}) %collective-permute-start.6) | collective-permute-done | bytes 1056800 | tf_op jit(solution)/shard_map/ppermute | solution.py:401
  53.5 1.2 collective-permute-start.8
  54.7 5.1 %work_3_0.1 = (f32[2048,256]{1,0:T(8,128)S(1)}, f32[2048,256]{1,0:T(8,128)S(1)}, f32[2048,256]{1,0:T(8,128)S(1)}, f32[2048,256]{1,0:T(8,128)S(1)}) custom-call(s32[2]{0:T(128)S(1)} %copy-done.2, bf16[1,512,8192]{2,1,0:T(8,128)(2,1)S(1)} %copy-done, bf16[1,512,1024]{2,1,0:T(8,128)(2,1)S(1)} %copy-done.1, s16[2064,256]{1,0:T(8,128)(2,1)S(1)} %get-tuple-element.29.refs_0_, ...), custom_call_target="tpu_custom_call" | custom-call | flops 2147483648 | bytes 12582912 | tf_op jit(solution)/shard_map/work_3_0/pallas_call | solution.py:295
  59.8 8.7 %collective-permute-done.14.refs_0_.refs_10_ = s16[2064,256]{1,0:T(8,128)(2,1)S(1)} collective-permute-done((s16[2064,256]{1,0:T(8,128)(2,1)S(1)}, s16[2064,256]{1,0:T(8,128)(2,1)S(1)}, u32[]{:S(2)}, u32[]{:S(2)}) %collective-permute-start.14) | collective-permute-done | bytes 1056800 | tf_op jit(solution)/shard_map/ppermute | solution.py:401
  69.8 2.4 %collective-permute-start.13 = (s16[1040,256]{1,0:T(8,128)(2,1)S(1)}, s16[1040,256]{1,0:T(8,128)(2,1)S(1)}, u32[]{:S(2)}, u32[]{:S(2)}) collective-permute-start(s16[1040,256]{1,0:T(8,128)(2,1)S(1)} %late_2_2.1), channel_id=1, source_target_pairs={{0,32},{1,97},{2,34},{3,99},{4,36},{5,101},{6,38},{7,103},{8,40},{... | collective-permute-start | bytes 1597448 | tf_op jit(solution)/shard_map/ppermute | solution.py:401
  72.2 2.2 %collective-permute-done.10.refs_0_.refs_4_ = s16[2064,256]{1,0:T(8,128)(2,1)S(1)} collective-permute-done((s16[2064,256]{1,0:T(8,128)(2,1)S(1)}, s16[2064,256]{1,0:T(8,128)(2,1)S(1)}, u32[]{:S(2)}, u32[]{:S(2)}) %collective-permute-start.10) | collective-permute-done | bytes 1056800 | tf_op jit(solution)/shard_map/ppermute | solution.py:401
  75.7 1.4 %collective-permute-start.9 = (s16[1040,256]{1,0:T(8,128)(2,1)S(1)}, s16[1040,256]{1,0:T(8,128)(2,1)S(1)}, u32[]{:S(2)}, u32[]{:S(2)}) collective-permute-start(s16[1040,256]{1,0:T(8,128)(2,1)S(1)} %late_2_0.1), channel_id=1, source_target_pairs={{0,24},{1,9},{2,26},{3,11},{4,28},{5,13},{6,30},{7,15},{8,16},{9,1... | collective-permute-start | bytes 1597448 | tf_op jit(solution)/shard_map/ppermute | solution.py:401
  77.1 2.9 %collective-permute-done.15.refs_11_.refs_1_ = s16[1040,256]{1,0:T(8,128)(2,1)S(1)} collective-permute-done((s16[1040,256]{1,0:T(8,128)(2,1)S(1)}, s16[1040,256]{1,0:T(8,128)(2,1)S(1)}, u32[]{:S(2)}, u32[]{:S(2)}) %collective-permute-start.15) | collective-permute-done | bytes 532512 | tf_op jit(solution)/shard_map/ppermute | solution.py:401
  80.5 2.2 %collective-permute-done.13.refs_8_.refs_1_ = s16[1040,256]{1,0:T(8,128)(2,1)S(1)} collective-permute-done((s16[1040,256]{1,0:T(8,128)(2,1)S(1)}, s16[1040,256]{1,0:T(8,128)(2,1)S(1)}, u32[]{:S(2)}, u32[]{:S(2)}) %collective-permute-start.13) | collective-permute-done | bytes 532512 | tf_op jit(solution)/shard_map/ppermute | solution.py:401
  83.2 5.0 %collective-permute-done.11.refs_5_.refs_1_ = s16[1040,256]{1,0:T(8,128)(2,1)S(1)} collective-permute-done((s16[1040,256]{1,0:T(8,128)(2,1)S(1)}, s16[1040,256]{1,0:T(8,128)(2,1)S(1)}, u32[]{:S(2)}, u32[]{:S(2)}) %collective-permute-start.11) | collective-permute-done | bytes 532512 | tf_op jit(solution)/shard_map/ppermute | solution.py:401
  88.6 2.2 %collective-permute-start.17 = (s16[528,256]{1,0:T(8,128)(2,1)S(1)}, s16[528,256]{1,0:T(8,128)(2,1)S(1)}, u32[]{:S(2)}, u32[]{:S(2)}) collective-permute-start(s16[528,256]{1,0:T(8,128)(2,1)S(1)} %late_1_1.1), channel_id=1, source_target_pairs={{0,32},{1,97},{2,34},{3,99},{4,36},{5,101},{6,38},{7,103},{8,40},{... | collective-permute-start | bytes 811016 | tf_op jit(solution)/shard_map/ppermute | solution.py:401
  91.2 1.8 %collective-permute-start.16 = (s16[528,256]{1,0:T(8,128)(2,1)S(1)}, s16[528,256]{1,0:T(8,128)(2,1)S(1)}, u32[]{:S(2)}, u32[]{:S(2)}) collective-permute-start(s16[528,256]{1,0:T(8,128)(2,1)S(1)} %late_1_0.1), channel_id=1, source_target_pairs={{0,8},{1,25},{2,10},{3,27},{4,12},{5,29},{6,14},{7,31},{8,0},{9,17... | collective-permute-start | bytes 811016 | tf_op jit(solution)/shard_map/ppermute | solution.py:401
  93.6 0.8 sum.1
  94.5 3.3 %collective-permute-done.17.refs_4_ = s16[528,256]{1,0:T(8,128)(2,1)S(1)} collective-permute-done((s16[528,256]{1,0:T(8,128)(2,1)S(1)}, s16[528,256]{1,0:T(8,128)(2,1)S(1)}, u32[]{:S(2)}, u32[]{:S(2)}) %collective-permute-start.17) | collective-permute-done | bytes 270368 | tf_op jit(solution)/shard_map/ppermute | solution.py:401
  98.1 1.9 %finish.1 = (f32[12288,1024]{1,0:T(8,128)}, f32[128,1,128]{2,1,0:T(1,128)S(1)}) custom-call(s32[1,1]{1,0:T(1,128)S(6)} %copy.9.refs_0_, f32[512,256]{1,0:T(8,128)S(1)} %get-tuple-element.37.refs_1_, s16[528,256]{1,0:T(8,128)(2,1)S(1)} %collective-permute-done.16.refs_2_, f32[512,256]{1,0:T(8,128)S(1)} %get-tuple-element.38.refs_3_, ...), custom_call_target="tpu_custom_call" | custom-call | bytes 5242880 | tf_op jit(solution)/shard_map/finish/pallas_call | solution.py:332
  99.9 18.9 %all_to_all.5.reports = f32[128,1,128]{2,1,0:T(1,128)} all-to-all(f32[128,1,128]{2,1,0:T(1,128)S(1)} %get-tuple-element.41), channel_id=1, replica_groups=mesh['dp'=16,'pipe'=8] {'dp','pipe'}, dimensions={0} | all-to-all | bytes 131072 | tf_op jit(solution)/shard_map/all_to_all | solution.py:436
  118.8 7.2 %update.1 = (f32[1,512,1024]{2,1,0:T(8,128)}, f32[1,512,1024]{2,1,0:T(8,128)}, f32[1,512,1024]{2,1,0:T(8,128)}) custom-call(s32[1]{0:T(128)} %bitcast.pipe_ref, f32[128,1,128]{2,1,0:T(1,128)} %all_to_all.5.reports, f32[1,512,1024]{2,1,0:T(8,128)} %w_ref.1, f32[1,512,1024]{2,1,0:T(8,128)} %m1_ref.1, f32[1,512,1024]{2,1,0:T(8,128)} %m2_ref.1, ...), custom_call_target="tpu_custom_call" | custom-call | tf_op jit(solution)/shard_map/update/pallas_call | solution.py:383
  (32 shorter events, 5.5 us)
Async XLA Ops:
  0.6 16.0 %collective-permute-start.1 = (bf16[512,1024]{1,0:T(8,128)(2,1)}, bf16[512,1024]{1,0:T(8,128)(2,1)S(1)}, u32[]{:S(2)}, u32[]{:S(2)}) collective-permute-start(bf16[512,1024]{1,0:T(8,128)(2,1)} %bitcast.4), channel_id=1, source_target_pairs={{0,8},{1,25},{2,10},{3,27},{4,12},{5,29},{6,14},{7,31},{8,0},{9,17... | collective-permute-start | bytes 3145736 | tf_op jit(solution)/shard_map/ppermute | solution.py:401
  4.3 15.4 %collective-permute-start = (bf16[512,1024]{1,0:T(8,128)(2,1)}, bf16[512,1024]{1,0:T(8,128)(2,1)S(1)}, u32[]{:S(2)}, u32[]{:S(2)}) collective-permute-start(bf16[512,1024]{1,0:T(8,128)(2,1)} %bitcast.5), channel_id=1, source_target_pairs={{0,32},{1,97},{2,34},{3,99},{4,36},{5,101},{6,38},{7,103},{8,40},{... | collective-permute-start | bytes 3145736 | tf_op jit(solution)/shard_map/ppermute | solution.py:401
  7.3 12.3 %copy-start.1 = (bf16[1,512,1024]{2,1,0:T(8,128)(2,1)S(1)}, bf16[1,512,1024]{2,1,0:T(8,128)(2,1)}, u32[]{:S(2)}) copy-start(bf16[1,512,1024]{2,1,0:T(8,128)(2,1)} %g_ref.7) | copy-start | bytes 3145732
  7.3 12.3 %copy-start.2 = (s32[2]{0:T(128)S(1)}, s32[2]{0:T(128)}, u32[]{:S(2)}) copy-start(s32[2]{0:T(128)} %pad_add_fusion.me_ref) | copy-start | bytes 28
  14.8 21.7 %collective-permute-start.2 = (s16[2064,256]{1,0:T(8,128)(2,1)}, s16[2064,256]{1,0:T(8,128)(2,1)S(1)}, u32[]{:S(2)}, u32[]{:S(2)}) collective-permute-start(s16[2064,256]{1,0:T(8,128)(2,1)} %get-tuple-element.24), channel_id=1, source_target_pairs={{0,24},{1,9},{2,26},{3,11},{4,28},{5,13},{6,30},{7,15},{8,16},{9,1... | collective-permute-start | bytes 3170312 | tf_op jit(solution)/shard_map/ppermute | solution.py:401
  14.9 23.4 %collective-permute-start.3 = (s16[2064,256]{1,0:T(8,128)(2,1)}, s16[2064,256]{1,0:T(8,128)(2,1)S(1)}, u32[]{:S(2)}, u32[]{:S(2)}) collective-permute-start(s16[2064,256]{1,0:T(8,128)(2,1)} %get-tuple-element.25), channel_id=1, source_target_pairs={{0,96},{1,33},{2,98},{3,35},{4,100},{5,37},{6,102},{7,39},{8,104},... | collective-permute-start | bytes 3170312 | tf_op jit(solution)/shard_map/ppermute | solution.py:401
  15.0 30.3 %collective-permute-start.4 = (bf16[512,1024]{1,0:T(8,128)(2,1)}, bf16[512,1024]{1,0:T(8,128)(2,1)S(1)}, u32[]{:S(2)}, u32[]{:S(2)}) collective-permute-start(bf16[512,1024]{1,0:T(8,128)(2,1)} %get-tuple-element.27), channel_id=1, source_target_pairs={{0,32},{1,97},{2,34},{3,99},{4,36},{5,101},{6,38},{7,103},{8,40},{... | collective-permute-start | bytes 3145736 | tf_op jit(solution)/shard_map/ppermute | solution.py:401
  16.7 28.8 %collective-permute-start.5 = (bf16[512,1024]{1,0:T(8,128)(2,1)}, bf16[512,1024]{1,0:T(8,128)(2,1)S(1)}, u32[]{:S(2)}, u32[]{:S(2)}) collective-permute-start(bf16[512,1024]{1,0:T(8,128)(2,1)} %get-tuple-element.28), channel_id=1, source_target_pairs={{0,8},{1,25},{2,10},{3,27},{4,12},{5,29},{6,14},{7,31},{8,0},{9,17... | collective-permute-start | bytes 3145736 | tf_op jit(solution)/shard_map/ppermute | solution.py:401
  19.6 3.4 %copy-start = (bf16[1,512,8192]{2,1,0:T(8,128)(2,1)S(1)}, bf16[1,512,8192]{2,1,0:T(8,128)(2,1)}, u32[]{:S(2)}) copy-start(bf16[1,512,8192]{2,1,0:T(8,128)(2,1)} %x_ref.7) | copy-start | bytes 25165828
  26.1 27.4 %collective-permute-start.6 = (s16[2064,256]{1,0:T(8,128)(2,1)S(1)}, s16[2064,256]{1,0:T(8,128)(2,1)S(1)}, u32[]{:S(2)}, u32[]{:S(2)}) collective-permute-start(s16[2064,256]{1,0:T(8,128)(2,1)S(1)} %get-tuple-element.30), channel_id=1, source_target_pairs={{0,24},{1,9},{2,26},{3,11},{4,28},{5,13},{6,30},{7,15},{8,16},{9,1... | collective-permute-start | bytes 3170312 | tf_op jit(solution)/shard_map/ppermute | solution.py:401
  36.5 18.1 %collective-permute-start.7 = (s16[2064,256]{1,0:T(8,128)(2,1)S(1)}, s16[2064,256]{1,0:T(8,128)(2,1)S(1)}, u32[]{:S(2)}, u32[]{:S(2)}) collective-permute-start(s16[2064,256]{1,0:T(8,128)(2,1)S(1)} %get-tuple-element.23.refs_0_), channel_id=1, source_target_pairs={{0,96},{1,33},{2,98},{3,35},{4,100},{5,37},{6,102},{7,39},{8,104},... | collective-permute-start | bytes 3170312 | tf_op jit(solution)/shard_map/ppermute | solution.py:401
  42.3 26.9 %collective-permute-start.12 = (s16[2064,256]{1,0:T(8,128)(2,1)S(1)}, s16[2064,256]{1,0:T(8,128)(2,1)S(1)}, u32[]{:S(2)}, u32[]{:S(2)}) collective-permute-start(s16[2064,256]{1,0:T(8,128)(2,1)S(1)} %get-tuple-element.35), channel_id=1, source_target_pairs={{0,8},{1,25},{2,10},{3,27},{4,12},{5,29},{6,14},{7,31},{8,0},{9,17... | collective-permute-start | bytes 3170312 | tf_op jit(solution)/shard_map/ppermute | solution.py:401
  45.3 23.2 %collective-permute-start.14 = (s16[2064,256]{1,0:T(8,128)(2,1)S(1)}, s16[2064,256]{1,0:T(8,128)(2,1)S(1)}, u32[]{:S(2)}, u32[]{:S(2)}) collective-permute-start(s16[2064,256]{1,0:T(8,128)(2,1)S(1)} %get-tuple-element.26.refs_0_), channel_id=1, source_target_pairs={{0,32},{1,97},{2,34},{3,99},{4,36},{5,101},{6,38},{7,103},{8,40},{... | collective-permute-start | bytes 3170312 | tf_op jit(solution)/shard_map/ppermute | solution.py:401
  49.7 24.7 %collective-permute-start.10 = (s16[2064,256]{1,0:T(8,128)(2,1)S(1)}, s16[2064,256]{1,0:T(8,128)(2,1)S(1)}, u32[]{:S(2)}, u32[]{:S(2)}) collective-permute-start(s16[2064,256]{1,0:T(8,128)(2,1)S(1)} %get-tuple-element.29.refs_0_), channel_id=1, source_target_pairs={{0,24},{1,9},{2,26},{3,11},{4,28},{5,13},{6,30},{7,15},{8,16},{9,1... | collective-permute-start | bytes 3170312 | tf_op jit(solution)/shard_map/ppermute | solution.py:401
  53.5 21.7 %collective-permute-start.8 = (s16[2064,256]{1,0:T(8,128)(2,1)S(1)}, s16[2064,256]{1,0:T(8,128)(2,1)S(1)}, u32[]{:S(2)}, u32[]{:S(2)}) collective-permute-start(s16[2064,256]{1,0:T(8,128)(2,1)S(1)} %get-tuple-element.32), channel_id=1, source_target_pairs={{0,96},{1,33},{2,98},{3,35},{4,100},{5,37},{6,102},{7,39},{8,104},... | collective-permute-start | bytes 3170312 | tf_op jit(solution)/shard_map/ppermute | solution.py:401
  69.0 11.0 %collective-permute-start.15 = (s16[1040,256]{1,0:T(8,128)(2,1)S(1)}, s16[1040,256]{1,0:T(8,128)(2,1)S(1)}, u32[]{:S(2)}, u32[]{:S(2)}) collective-permute-start(s16[1040,256]{1,0:T(8,128)(2,1)S(1)} %late_2_3.1), channel_id=1, source_target_pairs={{0,8},{1,25},{2,10},{3,27},{4,12},{5,29},{6,14},{7,31},{8,0},{9,17... | collective-permute-start | bytes 1597448 | tf_op jit(solution)/shard_map/ppermute | solution.py:401
  69.8 12.9 %collective-permute-start.13 = (s16[1040,256]{1,0:T(8,128)(2,1)S(1)}, s16[1040,256]{1,0:T(8,128)(2,1)S(1)}, u32[]{:S(2)}, u32[]{:S(2)}) collective-permute-start(s16[1040,256]{1,0:T(8,128)(2,1)S(1)} %late_2_2.1), channel_id=1, source_target_pairs={{0,32},{1,97},{2,34},{3,99},{4,36},{5,101},{6,38},{7,103},{8,40},{... | collective-permute-start | bytes 1597448 | tf_op jit(solution)/shard_map/ppermute | solution.py:401
  74.9 13.3 %collective-permute-start.11 = (s16[1040,256]{1,0:T(8,128)(2,1)S(1)}, s16[1040,256]{1,0:T(8,128)(2,1)S(1)}, u32[]{:S(2)}, u32[]{:S(2)}) collective-permute-start(s16[1040,256]{1,0:T(8,128)(2,1)S(1)} %late_2_1.1), channel_id=1, source_target_pairs={{0,96},{1,33},{2,98},{3,35},{4,100},{5,37},{6,102},{7,39},{8,104},... | collective-permute-start | bytes 1597448 | tf_op jit(solution)/shard_map/ppermute | solution.py:401
  75.7 15.0 %collective-permute-start.9 = (s16[1040,256]{1,0:T(8,128)(2,1)S(1)}, s16[1040,256]{1,0:T(8,128)(2,1)S(1)}, u32[]{:S(2)}, u32[]{:S(2)}) collective-permute-start(s16[1040,256]{1,0:T(8,128)(2,1)S(1)} %late_2_0.1), channel_id=1, source_target_pairs={{0,24},{1,9},{2,26},{3,11},{4,28},{5,13},{6,30},{7,15},{8,16},{9,1... | collective-permute-start | bytes 1597448 | tf_op jit(solution)/shard_map/ppermute | solution.py:401
  80.4 14.1 %collective-permute-start.19 = (s16[528,256]{1,0:T(8,128)(2,1)S(1)}, s16[528,256]{1,0:T(8,128)(2,1)S(1)}, u32[]{:S(2)}, u32[]{:S(2)}) collective-permute-start(s16[528,256]{1,0:T(8,128)(2,1)S(1)} %late_1_3.1), channel_id=1, source_target_pairs={{0,24},{1,9},{2,26},{3,11},{4,28},{5,13},{6,30},{7,15},{8,16},{9,1... | collective-permute-start | bytes 811016 | tf_op jit(solution)/shard_map/ppermute | solution.py:401
  83.1 11.4 %collective-permute-start.18 = (s16[528,256]{1,0:T(8,128)(2,1)S(1)}, s16[528,256]{1,0:T(8,128)(2,1)S(1)}, u32[]{:S(2)}, u32[]{:S(2)}) collective-permute-start(s16[528,256]{1,0:T(8,128)(2,1)S(1)} %late_1_2.1), channel_id=1, source_target_pairs={{0,96},{1,33},{2,98},{3,35},{4,100},{5,37},{6,102},{7,39},{8,104},... | collective-permute-start | bytes 811016 | tf_op jit(solution)/shard_map/ppermute | solution.py:401
  88.6 9.2 %collective-permute-start.17 = (s16[528,256]{1,0:T(8,128)(2,1)S(1)}, s16[528,256]{1,0:T(8,128)(2,1)S(1)}, u32[]{:S(2)}, u32[]{:S(2)}) collective-permute-start(s16[528,256]{1,0:T(8,128)(2,1)S(1)} %late_1_1.1), channel_id=1, source_target_pairs={{0,32},{1,97},{2,34},{3,99},{4,36},{5,101},{6,38},{7,103},{8,40},{... | collective-permute-start | bytes 811016 | tf_op jit(solution)/shard_map/ppermute | solution.py:401
  91.2 6.9 %collective-permute-start.16 = (s16[528,256]{1,0:T(8,128)(2,1)S(1)}, s16[528,256]{1,0:T(8,128)(2,1)S(1)}, u32[]{:S(2)}, u32[]{:S(2)}) collective-permute-start(s16[528,256]{1,0:T(8,128)(2,1)S(1)} %late_1_0.1), channel_id=1, source_target_pairs={{0,8},{1,25},{2,10},{3,27},{4,12},{5,29},{6,14},{7,31},{8,0},{9,17... | collective-permute-start | bytes 811016 | tf_op jit(solution)/shard_map/ppermute | solution.py:401

commit v4 on v3

v4 whole, which is shorter than its diff:
```python
import functools
import math

import jax
import jax.numpy as jnp
from jax import lax
from jax.experimental import pallas as pl
from jax.experimental.pallas import tpu as pltpu
from jax.sharding import PartitionSpec as P

D = 8192
KV = 1024
RANKS = 16
DEVICES = 128
FAR_ROWS = 12288
PIPE = 8
TOK = 512
OWN = 512
COLS = 256
VARIANTS = 2
ROWS = OWN // VARIANTS
BLOCK = ROWS * KV // COLS
GROUPS = KV // COLS
STEP = 512
KERNEL_VMEM = 18 << 20
UPDATE_VMEM = 60 << 20
TOP_POWER = 29.9985
SCALE_ROWS = 16

XA, XB, YA, YB = 4, 12, 1, 3
ORDERS = (
    ((XA, XB, YA, YB), (YA, YB, XA, XB)),
    ((XB, XA, YB, YA), (YB, YA, XB, XA)),
)
EVERY = range(VARIANTS)

TRANSPOSED = (((0,), (0,)), ((), ()))


def masks_of(v, step):
    masks = []
    for order in (orders[v] for orders in ORDERS):
        base = {0: order[0] ^ order[1], 1: order[0], 2: order[1], 3: 0}[step]
        masks.append([base, base ^ order[3], base ^ order[2], base ^ order[2] ^ order[3]])
    return list(zip(*masks))


def decode(codes, scale):
    wide = codes.astype(jnp.float32)
    return wide * jnp.abs(wide) * scale


def scale_of(step_code):
    power = step_code * (1.0 / 64.0) - TOP_POWER
    return jnp.exp2(power), jnp.exp2(-power)


def columns_of(me_ref, mask, v):
    block = jnp.bitwise_xor(me_ref[0], jnp.where(me_ref[1] == 0, *mask))
    return pl.ds(pl.multiple_of(block * OWN + v * ROWS, ROWS), ROWS)


def scales_of(received):
    return [
        scale_of(r[r.shape[0] - SCALE_ROWS :, :].astype(jnp.float32)[:1])[0]
        for r in received
    ]


def pieces(rows, body, start):
    def some(i, carry):
        return body(pl.multiple_of(i * STEP, STEP), carry)

    return lax.fori_loop(0, rows // STEP, some, start)


def largest_of(total):
    return jnp.max(jnp.abs(total), axis=0, keepdims=True)


def add_received(source, first, received, rows, sums):
    scales = scales_of([r for r, _ in received])

    def body(at, largest):
        total = source[pl.ds(first + at, STEP), :]
        for (r, begin), scale in zip(received, scales):
            total = total + decode(r[pl.ds(begin + at, STEP), :], scale)
        sums[pl.ds(at, STEP), :] = total
        return jnp.maximum(largest, largest_of(total))

    return pieces(rows, body, jnp.zeros((1, COLS), jnp.float32))


def encode(largest, sums, rows, out_ref):
    step_code = jnp.ceil(jnp.log2(jnp.maximum(largest, 1e-37)) * 64.0)
    step_code = jnp.clip(step_code, -90.0 * 64.0, 128.0 * 64.0)
    factor = scale_of(step_code)[1]
    out_ref[rows : rows + SCALE_ROWS, :] = (
        jnp.broadcast_to(step_code, (SCALE_ROWS, COLS)).astype(jnp.int32).astype(jnp.int16)
    )

    def body(at, _):
        scaled = sums[pl.ds(at, STEP), :] * factor
        rooted = scaled * lax.rsqrt(jnp.maximum(jnp.abs(scaled), 1e-12))
        out_ref[pl.ds(at, STEP), :] = jnp.round(rooted).astype(jnp.int32).astype(jnp.int16)
        return 0

    pieces(rows, body, 0)


def gather_kernel(me_ref, x_ref, *outs):
    outs = list(outs)
    for step in (0, 1):
        for v in EVERY:
            out = outs.pop(0)
            for slot, mask in enumerate(masks_of(v, step)):
                out[:, slot * ROWS : (slot + 1) * ROWS] = x_ref[0, :, columns_of(me_ref, mask, v)]


def multiply(v, masks, me_ref, x_ref, g_ref, x_there, g_there, into):
    x = [x_ref[0, :, columns_of(me_ref, mask, v)] for mask in masks]
    x = jnp.concatenate([jnp.concatenate(x, axis=1), x_there], axis=0)
    g = jnp.concatenate([g_ref[0], g_there[...]], axis=0)
    total = lax.dot_general(x, g, TRANSPOSED, preferred_element_type=jnp.float32)
    largest = jnp.zeros((1, COLS), jnp.float32)
    for group in range(GROUPS):
        part = total[:, group * COLS : (group + 1) * COLS]
        largest = jnp.maximum(largest, largest_of(part))
        for slot in range(len(masks)):
            at = slot * BLOCK + group * ROWS
            into[at : at + ROWS, :] = part[slot * ROWS : (slot + 1) * ROWS, :]
    return largest


def send_kernel(half, me_ref, x_ref, g_ref, after_ref, *refs):
    g_there, x_there, outs, sums = refs[:2], refs[2:4], refs[4:6], refs[6]
    for v in EVERY:
        masks = masks_of(v, 2)[2 * half : 2 * half + 2]
        x = x_there[v][:, 2 * half * ROWS : 2 * (half + 1) * ROWS]
        largest = multiply(v, masks, me_ref, x_ref, g_ref, x, g_there[v], sums)
        encode(largest, sums, 2 * BLOCK, outs[v])


def keep_kernel(me_ref, x_ref, g_ref, after_ref, *refs):
    g_there, x_there, outs = refs[:2], refs[2:4], refs[4:6]
    for v in EVERY:
        multiply(v, masks_of(v, 3), me_ref, x_ref, g_ref, x_there[v][...], g_there[v], outs[v])


def late_kernel(block, begins, p_ref, *refs):
    received, out, sums = refs[:-2], refs[-2], refs[-1]
    received = [(r, begin * BLOCK) for r, begin in zip(received, begins)]
    largest = add_received(p_ref, block * BLOCK, received, BLOCK, sums)
    encode(largest, sums, BLOCK, out)


def sum_kernel(*refs):
    outs = refs[3 * VARIANTS :]
    for v, out in enumerate(outs):
        p_ref, *received = refs[3 * v : 3 * v + 3]
        add_received(p_ref, 0, [(r, 0) for r in received], BLOCK, out)


def finish_kernel(*refs):
    flag_ref = refs[0]
    grad_hbm, report_hbm, grad_ref, report_ref, sems = refs[-5:]
    copies = []
    acc = jnp.zeros((8, 128), jnp.float32)
    for v in EVERY:
        p_ref, r = refs[1 + 2 * v : 3 + 2 * v]
        [scale] = scales_of([r])
        for group in range(GROUPS):
            at = slice(group * ROWS, (group + 1) * ROWS)
            total = p_ref[at, :] + decode(r[at, :], scale)
            grad_ref[v * ROWS : (v + 1) * ROWS, group * COLS : (group + 1) * COLS] = total
            squared = total * total
            squared = squared[:, :128] + squared[:, 128:]
            acc = acc + jnp.sum(squared.reshape(ROWS // 8, 8, 128), axis=0)
        at = slice(v * ROWS, (v + 1) * ROWS)
        copies.append(pltpu.make_async_copy(grad_ref.at[at], grad_hbm.at[at], sems.at[v]))
        copies[-1].start()
    marked = jnp.where(flag_ref[0, 0] != 0, 1.0, 0.0)
    acc = acc + pltpu.roll(acc, 64, axis=1)
    lane = lax.broadcasted_iota(jnp.int32, (8, 128), 1)
    acc = jnp.where(lane < 64, jnp.sum(acc, axis=0, keepdims=True), marked)
    report_ref[...] = jnp.broadcast_to(acc[:1][None], (DEVICES, 1, 128))
    copies.append(pltpu.make_async_copy(report_ref, report_hbm, sems.at[VARIANTS]))
    copies[-1].start()
    for copy in copies:
        copy.wait()


WHOLE = pl.BlockSpec(memory_space=pltpu.VMEM)
LEFT = pl.BlockSpec(memory_space=pl.ANY)
FAR = pl.BlockSpec(memory_space=pltpu.HBM)
SCALAR = pl.BlockSpec(memory_space=pltpu.SMEM)


def coded(blocks):
    return jax.ShapeDtypeStruct((blocks * BLOCK + SCALE_ROWS, COLS), jnp.int16)


def partial(blocks):
    return jax.ShapeDtypeStruct((blocks * BLOCK, COLS), jnp.float32)


def cost(blocks, dots, arrivals):
    values = blocks * BLOCK * COLS
    return pl.CostEstimate(
        flops=4 * TOK * values * dots,
        bytes_accessed=values * (4 + 2 * arrivals),
        transcendentals=values,
    )


def kernel_call(body, name, ins, outs, scratch, estimate, out_specs=None, vmem=KERNEL_VMEM):
    return pl.pallas_call(
        body,
        out_shape=outs,
        in_specs=ins,
        out_specs=out_specs or [WHOLE] * len(outs),
        scratch_shapes=scratch,
        compiler_params=pltpu.CompilerParams(vmem_limit_bytes=vmem),
        cost_estimate=estimate,
        name=name,
    )


def gather(me, x):
    return kernel_call(
        gather_kernel,
        "gather",
        [SCALAR, WHOLE],
        [jax.ShapeDtypeStruct((TOK, 4 * ROWS), jnp.bfloat16)] * (2 * VARIANTS),
        [],
        cost(4 * VARIANTS, 0, 1),
    )(me, x)


def send(half, me, x, g, after, there):
    return kernel_call(
        functools.partial(send_kernel, half),
        f"send_{half}",
        [SCALAR, WHOLE, WHOLE, LEFT] + [WHOLE] * len(there),
        [coded(2)] * VARIANTS,
        [pltpu.VMEM((2 * BLOCK, COLS), jnp.float32)],
        cost(2 * VARIANTS, 1, 1),
    )(me, x, g, after, *there)


def keep(me, x, g, after, there):
    return kernel_call(
        keep_kernel,
        "keep",
        [SCALAR, WHOLE, WHOLE, LEFT] + [WHOLE] * len(there),
        [partial(4)] * VARIANTS,
        [],
        cost(4 * VARIANTS, 1, 1),
    )(me, x, g, after, *there)


def late(block, v, p, received, begins):
    [code] = kernel_call(
        functools.partial(late_kernel, block, begins),
        f"late_{block}_{v}",
        [WHOLE] * (1 + len(received)),
        [coded(1)],
        [pltpu.VMEM((BLOCK, COLS), jnp.float32)],
        cost(1, 0, len(received)),
    )(p, *received)
    return code


def sum_own(held):
    return kernel_call(
        sum_kernel,
        "sum",
        [WHOLE] * len(held),
        [partial(1)] * VARIANTS,
        [],
        cost(VARIANTS, 0, 2),
    )(*held)


def finish(flag, held):
    grad = jax.ShapeDtypeStruct((OWN, KV), jnp.float32)
    report = jax.ShapeDtypeStruct((DEVICES, 1, 128), jnp.float32)
    far = jax.ShapeDtypeStruct((FAR_ROWS, KV), jnp.float32)
    return kernel_call(
        finish_kernel,
        "finish",
        [SCALAR] + [WHOLE] * len(held),
        [far, report],
        [pltpu.VMEM(o.shape, o.dtype) for o in (grad, report)]
        + [pltpu.SemaphoreType.DMA((VARIANTS + 1,))],
        cost(VARIANTS, 0, 1),
        [FAR] * 2,
    )(flag, *held)


UPDATE_ROWS = 256


def update_kernel(bound, pipe_ref, reports, w_ref, m1_ref, m2_ref, g_ref, *refs):
    new_w, new_m1, new_m2, clip_ref, own_ref = refs

    @pl.when(pl.program_id(0) == 0)
    def _():
        lane = lax.broadcasted_iota(jnp.int32, (1, 128), 1)
        total = jnp.zeros((1, 128), jnp.float32)
        own = jnp.zeros((1, 128), jnp.float32)
        for section in range(PIPE):
            report = functools.reduce(
                jnp.add, [reports[rank * PIPE + section] for rank in range(RANKS)]
            )
            marks = pltpu.roll(report, 64, axis=1)
            total = total + jnp.where((lane < 64) & (marks == 0.0), report, 0.0)
            own = jnp.where(pipe_ref[0] == section, marks, own)
        total = jnp.sum(total, keepdims=True)
        clip = jnp.minimum(1.0, bound / (jnp.sqrt(total) + 1e-06))
        clip_ref[...] = jnp.broadcast_to(clip, (8, 128))
        own_ref[...] = jnp.broadcast_to(own[:1, :1], (8, 128))

    clip = clip_ref[:1, :1]
    keep = own_ref[:1, :1] == 0.0
    w, first_old, second_old = w_ref[0], m1_ref[0], m2_ref[0]
    scaled = clip * g_ref[...]
    first = 0.9 * first_old + 0.1 * scaled
    second = 0.95 * second_old + 0.05 * scaled * scaled
    root = second * lax.rsqrt(second)
    updated = w - 0.02 * (first / (root + 1e-08) + 0.1 * w)
    new_w[0] = jnp.where(keep, updated, w)
    new_m1[0] = jnp.where(keep, first, first_old)
    new_m2[0] = jnp.where(keep, second, second_old)


def update(pipe, reports, w, m1, m2, grad, bound):
    block = pl.BlockSpec((1, UPDATE_ROWS, KV), lambda i: (0, i, 0))
    shape = jax.ShapeDtypeStruct((1, OWN, KV), jnp.float32)
    return pl.pallas_call(
        functools.partial(update_kernel, bound),
        grid=(OWN // UPDATE_ROWS,),
        out_shape=[shape] * 3,
        in_specs=[SCALAR, WHOLE, block, block, block]
        + [pl.BlockSpec((UPDATE_ROWS, KV), lambda i: (i, 0))],
        out_specs=[block] * 3,
        scratch_shapes=[pltpu.VMEM((8, 128), jnp.float32)] * 2,
        compiler_params=pltpu.CompilerParams(vmem_limit_bytes=UPDATE_VMEM),
        name="update",
    )(pipe, reports, w, m1, m2, grad)


def swap(value, masks):
    pairs = []
    for rank in range(RANKS):
        for pipe in range(PIPE):
            pairs.append((rank * PIPE + pipe, (rank ^ masks[pipe % 2]) * PIPE + pipe))
    return lax.ppermute(value, ("dp", "pipe"), pairs)


def per_device(layer_input, value_grad, master_weight, moment_one, moment_two, overflow_flags):
    rank, core = lax.axis_index("dp"), lax.axis_index("pipe") % 2
    me = jnp.stack([rank, core]).astype(jnp.int32)

    def cross(values, bit):
        return [swap(value, [orders[v][bit] for orders in ORDERS]) for v, value in enumerate(values)]

    x, g = layer_input, value_grad
    g_there = cross([g[0]] * VARIANTS, 0)
    sent = gather(me, x)
    on_there, kept_there = cross(sent[:VARIANTS], 0), cross(sent[VARIANTS:], 0)
    urgent = send(1, me, x, g, me, g_there + on_there)
    two_urgent = cross(urgent, 1)
    codes = send(0, me, x, g, urgent[-1], g_there + on_there)
    two = cross(codes, 1)
    kept = keep(me, x, g, codes[-1], g_there + kept_there)
    three_urgent = cross([late(3, v, kept[v], [two_urgent[v]], [1]) for v in EVERY], 2)
    three = cross([late(2, v, kept[v], [two_urgent[v]], [0]) for v in EVERY], 2)
    four = cross([late(1, v, kept[v], [two[v], three_urgent[v]], [1, 0]) for v in EVERY], 3)
    own = sum_own([a for v in EVERY for a in (kept[v], two[v], three[v])])
    held = [a for v in EVERY for a in (own[v], four[v])]
    grad, report = finish(overflow_flags, held)
    reports = lax.all_to_all(report, ("dp", "pipe"), 0, 0)
    bound = 0.5 * math.sqrt(D * KV * PIPE)
    pipe = lax.axis_index("pipe").astype(jnp.int32).reshape(1)
    return tuple(update(pipe, reports, master_weight, moment_one, moment_two, grad, bound))


def solution(mesh):
    placed = P("pipe", "dp", None)
    return jax.shard_map(
        per_device,
        mesh=mesh,
        in_specs=(placed,) * 5 + (P("pipe", "dp"),),
        out_specs=(placed,) * 3,
        check_vma=False,
    )
```

time: 126 us -> 112 us (0.89)
  Pallas kernels: 37.4 us -> 27.8 us
  waiting for transfers between devices: 40.8 us -> 33.1 us
  blocking collectives: 18.9 us -> 21.8 us
    pallas_call x13 -> x10, Pallas kernels: 27.5 us -> 18 us  [the longest x2 8.26 us: send(): kernel_call(functools.partial(send_kernel, half), f'send_{half}', [SCALAR...]
    ppermute x20 -> x16, waiting for transfers between devices: 40.8 us -> 33.1 us  [swap(): return lax.ppermute(value, ('dp', 'pipe'), pairs)]
    all_to_all x1, blocking collectives: 18.9 us -> 21.8 us  [per_device(): reports = lax.all_to_all(report, ('dp', 'pipe'), 0, 0)]
    ppermute x20 -> x16, starting transfers between devices: 23.5 us -> 24.1 us  [swap(): return lax.ppermute(value, ('dp', 'pipe'), pairs)]
    unnamed x6 -> x4, local copies, waits for them, and re-layouts: 3.39 us -> 3.38 us
  transfers between devices with their start and end apart: 20 -> 16, of which waited for: 13 -> 9; matrix products, arithmetic and copies ran while one was open for 0% -> 0% of each run, Pallas kernels for 22% -> 17%
where the time goes in v4:
time: 112 us
  waiting for transfers between devices  33.1 us (30%)
  Pallas kernels  27.8 us (25%)
  starting transfers between devices  24.1 us (22%)
  blocking collectives  21.8 us (19%)
  local copies, waits for them, and re-layouts  3.38 us (3%)
  between operations  1.4 us (1%)
    ppermute x16, waiting for transfers between devices, swap(): return lax.ppermute(value, ('dp', 'pipe'), pairs)  33.1 us
    ppermute x16, starting transfers between devices, swap(): return lax.ppermute(value, ('dp', 'pipe'), pairs)  24.1 us
    all_to_all x1, blocking collectives, per_device(): reports = lax.all_to_all(report, ('dp', 'pipe'), 0, 0)  21.8 us
    pallas_call x2, Pallas kernels, send(): kernel_call(functools.partial(send_kernel, half), f'send_{half}', [SCALAR...  8.26 us
    pallas_call x1, Pallas kernels, update(): pl.pallas_call(functools.partial(update_kernel, bound), grid=(OWN // UPDA...  7.22 us
    pallas_call x1, Pallas kernels, keep(): kernel_call(keep_kernel, 'keep', [SCALAR, WHOLE, WHOLE, LEFT] + [WHOLE] *...  5.07 us
    pallas_call x6, Pallas kernels, late(): kernel_call(functools.partial(late_kernel, block, begins), f'late_{block}...  3.48 us
    unnamed x4, local copies, waits for them, and re-layouts  3.38 us
  transfers between devices with their start and end apart: 16, of which 9 were waited for; matrix products, arithmetic and copies ran while one was open for 0% of the time, Pallas kernels for 17%

profile of v4, /device:TPU:1, one launch (start us, length us, event | category | flops | bytes accessed | tf_op | source)
XLA Modules:
  0.0 111.6 jit_solution(7563418859198702080)
XLA Ops:
  0.6 3.6 %collective-permute-start.1 = (bf16[512,1024]{1,0:T(8,128)(2,1)}, bf16[512,1024]{1,0:T(8,128)(2,1)S(1)}, u32[]{:S(2)}, u32[]{:S(2)}) collective-permute-start(bf16[512,1024]{1,0:T(8,128)(2,1)} %bitcast.4), channel_id=1, source_target_pairs={{0,8},{1,25},{2,10},{3,27},{4,12},{5,29},{6,14},{7,31},{8,0},{9,17... | collective-permute-start | bytes 3145736 | tf_op jit(solution)/shard_map/ppermute | solution.py:358
  4.3 2.5 %collective-permute-start = (bf16[512,1024]{1,0:T(8,128)(2,1)}, bf16[512,1024]{1,0:T(8,128)(2,1)S(1)}, u32[]{:S(2)}, u32[]{:S(2)}) collective-permute-start(bf16[512,1024]{1,0:T(8,128)(2,1)} %bitcast.5), channel_id=1, source_target_pairs={{0,32},{1,97},{2,34},{3,99},{4,36},{5,101},{6,38},{7,103},{8,40},{... | collective-permute-start | bytes 3145736 | tf_op jit(solution)/shard_map/ppermute | solution.py:358
  6.8 3.4 %copy-done = bf16[1,512,8192]{2,1,0:T(8,128)(2,1)S(1)} copy-done((bf16[1,512,8192]{2,1,0:T(8,128)(2,1)S(1)}, bf16[1,512,8192]{2,1,0:T(8,128)(2,1)}, u32[]{:S(2)}) %copy-start) | copy-done | bytes 8388632
  10.2 1.1 %gather.1 = (bf16[512,1024]{1,0:T(8,128)(2,1)S(1)}, bf16[512,1024]{1,0:T(8,128)(2,1)S(1)}, bf16[512,1024]{1,0:T(8,128)(2,1)S(1)}, bf16[512,1024]{1,0:T(8,128)(2,1)S(1)}) custom-call(s32[2]{0:T(128)S(1)} %pad_add_fusion.me_ref.after_ref, bf16[1,512,8192]{2,1,0:T(8,128)(2,1)S(1)} %copy-done), custom_call_target="tpu_custom_call" | custom-call | bytes 12582912 | tf_op jit(solution)/shard_map/gather/pallas_call | solution.py:230
  11.7 2.5 %collective-permute-start.4 = (bf16[512,1024]{1,0:T(8,128)(2,1)S(1)}, bf16[512,1024]{1,0:T(8,128)(2,1)S(1)}, u32[]{:S(2)}, u32[]{:S(2)}) collective-permute-start(bf16[512,1024]{1,0:T(8,128)(2,1)S(1)} %get-tuple-element.21), channel_id=1, source_target_pairs={{0,32},{1,97},{2,34},{3,99},{4,36},{5,101},{6,38},{7,103},{8,40},{... | collective-permute-start | bytes 3145736 | tf_op jit(solution)/shard_map/ppermute | solution.py:358
  14.2 2.5 %collective-permute-done.1.refs_1_ = bf16[512,1024]{1,0:T(8,128)(2,1)S(1)} collective-permute-done((bf16[512,1024]{1,0:T(8,128)(2,1)}, bf16[512,1024]{1,0:T(8,128)(2,1)S(1)}, u32[]{:S(2)}, u32[]{:S(2)}) %collective-permute-start.1) | collective-permute-done | bytes 1048608 | tf_op jit(solution)/shard_map/ppermute | solution.py:358
  16.7 2.7 %collective-permute-start.5 = (bf16[512,1024]{1,0:T(8,128)(2,1)S(1)}, bf16[512,1024]{1,0:T(8,128)(2,1)S(1)}, u32[]{:S(2)}, u32[]{:S(2)}) collective-permute-start(bf16[512,1024]{1,0:T(8,128)(2,1)S(1)} %get-tuple-element.22), channel_id=1, source_target_pairs={{0,8},{1,25},{2,10},{3,27},{4,12},{5,29},{6,14},{7,31},{8,0},{9,17... | collective-permute-start | bytes 3145736 | tf_op jit(solution)/shard_map/ppermute | solution.py:358
  19.3 11.2 %collective-permute-done.2.refs_2_ = bf16[512,1024]{1,0:T(8,128)(2,1)S(1)} collective-permute-done((bf16[512,1024]{1,0:T(8,128)(2,1)S(1)}, bf16[512,1024]{1,0:T(8,128)(2,1)S(1)}, u32[]{:S(2)}, u32[]{:S(2)}) %collective-permute-start.2) | collective-permute-done | bytes 1048608 | tf_op jit(solution)/shard_map/ppermute | solution.py:358
  30.6 4.1 %send_1.1 = (s16[2064,256]{1,0:T(8,128)(2,1)S(1)}, s16[2064,256]{1,0:T(8,128)(2,1)S(1)}) custom-call(s32[2]{0:T(128)S(1)} %pad_add_fusion.me_ref.after_ref, bf16[1,512,8192]{2,1,0:T(8,128)(2,1)S(1)} %copy-done, bf16[1,512,1024]{2,1,0:T(8,128)(2,1)S(1)} %copy-done.1, s32[2]{0:T(128)S(1)} %pad_add_fusion.me_ref.after_ref, ...), custom_call_target="tpu_custom_call" | custom-call | flops 2147483648 | bytes 6291456 | tf_op jit(solution)/shard_map/send_1/pallas_call | solution.py:241
  35.2 4.1 %send_0.1 = (s16[2064,256]{1,0:T(8,128)(2,1)S(1)}, s16[2064,256]{1,0:T(8,128)(2,1)S(1)}) custom-call(s32[2]{0:T(128)S(1)} %pad_add_fusion.me_ref.after_ref, bf16[1,512,8192]{2,1,0:T(8,128)(2,1)S(1)} %copy-done, bf16[1,512,1024]{2,1,0:T(8,128)(2,1)S(1)} %copy-done.1, s16[2064,256]{1,0:T(8,128)(2,1)S(1)} %get-tuple-element.19.after_ref, ...), custom_call_target="tpu_custom_call" | custom-call | flops 2147483648 | bytes 6291456 | tf_op jit(solution)/shard_map/send_0/pallas_call | solution.py:241
  39.3 1.4 %collective-permute-start.9 = (s16[2064,256]{1,0:T(8,128)(2,1)S(1)}, s16[2064,256]{1,0:T(8,128)(2,1)S(1)}, u32[]{:S(2)}, u32[]{:S(2)}) collective-permute-start(s16[2064,256]{1,0:T(8,128)(2,1)S(1)} %get-tuple-element.20.after_ref), channel_id=1, source_target_pairs={{0,24},{1,9},{2,26},{3,11},{4,28},{5,13},{6,30},{7,15},{8,16},{9,1... | collective-permute-start | bytes 3170312 | tf_op jit(solution)/shard_map/ppermute | solution.py:358
  40.8 2.5 %collective-permute-done.4.refs_2_ = bf16[512,1024]{1,0:T(8,128)(2,1)S(1)} collective-permute-done((bf16[512,1024]{1,0:T(8,128)(2,1)S(1)}, bf16[512,1024]{1,0:T(8,128)(2,1)S(1)}, u32[]{:S(2)}, u32[]{:S(2)}) %collective-permute-start.4) | collective-permute-done | bytes 1048608 | tf_op jit(solution)/shard_map/ppermute | solution.py:358
  43.3 5.1 %keep.1 = (f32[4096,256]{1,0:T(8,128)S(1)}, f32[4096,256]{1,0:T(8,128)S(1)}) custom-call(s32[2]{0:T(128)S(1)} %pad_add_fusion.me_ref.after_ref, bf16[1,512,8192]{2,1,0:T(8,128)(2,1)S(1)} %copy-done, bf16[1,512,1024]{2,1,0:T(8,128)(2,1)S(1)} %copy-done.1, s16[2064,256]{1,0:T(8,128)(2,1)S(1)} %get-tuple-element.20.after_ref, ...), custom_call_target="tpu_custom_call" | custom-call | flops 4294967296 | bytes 12582912 | tf_op jit(solution)/shard_map/keep/pallas_call | solution.py:252
  48.4 2.1 %collective-permute-done.10.refs_0_ = s16[2064,256]{1,0:T(8,128)(2,1)S(1)} collective-permute-done((s16[2064,256]{1,0:T(8,128)(2,1)S(1)}, s16[2064,256]{1,0:T(8,128)(2,1)S(1)}, u32[]{:S(2)}, u32[]{:S(2)}) %collective-permute-start.10) | collective-permute-done | bytes 1056800 | tf_op jit(solution)/shard_map/ppermute | solution.py:358
  50.5 0.5 late_3_1.1
  51.1 2.6 %collective-permute-start.14 = (s16[1040,256]{1,0:T(8,128)(2,1)S(1)}, s16[1040,256]{1,0:T(8,128)(2,1)S(1)}, u32[]{:S(2)}, u32[]{:S(2)}) collective-permute-start(s16[1040,256]{1,0:T(8,128)(2,1)S(1)} %late_3_1.1), channel_id=1, source_target_pairs={{0,32},{1,97},{2,34},{3,99},{4,36},{5,101},{6,38},{7,103},{8,40},{... | collective-permute-start | bytes 1597448 | tf_op jit(solution)/shard_map/ppermute | solution.py:358
  53.7 0.5 late_3_0.1
  54.2 2.8 %collective-permute-start.12 = (s16[1040,256]{1,0:T(8,128)(2,1)S(1)}, s16[1040,256]{1,0:T(8,128)(2,1)S(1)}, u32[]{:S(2)}, u32[]{:S(2)}) collective-permute-start(s16[1040,256]{1,0:T(8,128)(2,1)S(1)} %late_3_0.1), channel_id=1, source_target_pairs={{0,8},{1,25},{2,10},{3,27},{4,12},{5,29},{6,14},{7,31},{8,0},{9,17... | collective-permute-start | bytes 1597448 | tf_op jit(solution)/shard_map/ppermute | solution.py:358
  57.0 0.5 late_2_1.1
  58.0 0.5 late_2_0.1
  58.5 8.2 %collective-permute-done.9.refs_4_.refs_0_ = s16[2064,256]{1,0:T(8,128)(2,1)S(1)} collective-permute-done((s16[2064,256]{1,0:T(8,128)(2,1)S(1)}, s16[2064,256]{1,0:T(8,128)(2,1)S(1)}, u32[]{:S(2)}, u32[]{:S(2)}) %collective-permute-start.9) | collective-permute-done | bytes 1056800 | tf_op jit(solution)/shard_map/ppermute | solution.py:358
  66.8 1.8 %collective-permute-start.8 = (s16[1040,256]{1,0:T(8,128)(2,1)S(1)}, s16[1040,256]{1,0:T(8,128)(2,1)S(1)}, u32[]{:S(2)}, u32[]{:S(2)}) collective-permute-start(s16[1040,256]{1,0:T(8,128)(2,1)S(1)} %late_2_0.1), channel_id=1, source_target_pairs={{0,8},{1,25},{2,10},{3,27},{4,12},{5,29},{6,14},{7,31},{8,0},{9,17... | collective-permute-start | bytes 1597448 | tf_op jit(solution)/shard_map/ppermute | solution.py:358
  68.6 0.7 late_1_1.1
  69.3 1.5 %collective-permute-start.15 = (s16[1040,256]{1,0:T(8,128)(2,1)S(1)}, s16[1040,256]{1,0:T(8,128)(2,1)S(1)}, u32[]{:S(2)}, u32[]{:S(2)}) collective-permute-start(s16[1040,256]{1,0:T(8,128)(2,1)S(1)} %late_1_1.1), channel_id=1, source_target_pairs={{0,96},{1,33},{2,98},{3,35},{4,100},{5,37},{6,102},{7,39},{8,104},... | collective-permute-start | bytes 1597448 | tf_op jit(solution)/shard_map/ppermute | solution.py:358
  70.9 0.7 late_1_0.1
  71.6 1.3 %collective-permute-start.13 = (s16[1040,256]{1,0:T(8,128)(2,1)S(1)}, s16[1040,256]{1,0:T(8,128)(2,1)S(1)}, u32[]{:S(2)}, u32[]{:S(2)}) collective-permute-start(s16[1040,256]{1,0:T(8,128)(2,1)S(1)} %late_1_0.1), channel_id=1, source_target_pairs={{0,24},{1,9},{2,26},{3,11},{4,28},{5,13},{6,30},{7,15},{8,16},{9,1... | collective-permute-start | bytes 1597448 | tf_op jit(solution)/shard_map/ppermute | solution.py:358
  73.5 4.4 %collective-permute-done.11.refs_5_ = s16[1040,256]{1,0:T(8,128)(2,1)S(1)} collective-permute-done((s16[1040,256]{1,0:T(8,128)(2,1)S(1)}, s16[1040,256]{1,0:T(8,128)(2,1)S(1)}, u32[]{:S(2)}, u32[]{:S(2)}) %collective-permute-start.11) | collective-permute-done | bytes 532512 | tf_op jit(solution)/shard_map/ppermute | solution.py:358
  78.0 0.9 sum.1
  78.8 1.8 %collective-permute-done.15.refs_4_ = s16[1040,256]{1,0:T(8,128)(2,1)S(1)} collective-permute-done((s16[1040,256]{1,0:T(8,128)(2,1)S(1)}, s16[1040,256]{1,0:T(8,128)(2,1)S(1)}, u32[]{:S(2)}, u32[]{:S(2)}) %collective-permute-start.15) | collective-permute-done | bytes 532512 | tf_op jit(solution)/shard_map/ppermute | solution.py:358
  80.8 1.8 %finish.1 = (f32[12288,1024]{1,0:T(8,128)}, f32[128,1,128]{2,1,0:T(1,128)S(1)}) custom-call(s32[1,1]{1,0:T(1,128)S(6)} %copy.9.refs_0_, f32[1024,256]{1,0:T(8,128)S(1)} %get-tuple-element.27.refs_1_, s16[1040,256]{1,0:T(8,128)(2,1)S(1)} %collective-permute-done.13.refs_2_, f32[1024,256]{1,0:T(8,128)S(1)} %get-tuple-element.28.refs_3_, ...), custom_call_target="tpu_custom_call" | custom-call | bytes 3145728 | tf_op jit(solution)/shard_map/finish/pallas_call | solution.py:289
  82.6 21.8 %all_to_all.5.reports = f32[128,1,128]{2,1,0:T(1,128)} all-to-all(f32[128,1,128]{2,1,0:T(1,128)S(1)} %get-tuple-element.29), channel_id=1, replica_groups=mesh['dp'=16,'pipe'=8] {'dp','pipe'}, dimensions={0} | all-to-all | bytes 131072 | tf_op jit(solution)/shard_map/all_to_all | solution.py:383
  104.4 7.2 %update.1 = (f32[1,512,1024]{2,1,0:T(8,128)}, f32[1,512,1024]{2,1,0:T(8,128)}, f32[1,512,1024]{2,1,0:T(8,128)}) custom-call(s32[1]{0:T(128)} %bitcast.pipe_ref, f32[128,1,128]{2,1,0:T(1,128)} %all_to_all.5.reports, f32[1,512,1024]{2,1,0:T(8,128)} %w_ref.1, f32[1,512,1024]{2,1,0:T(8,128)} %m1_ref.1, f32[1,512,1024]{2,1,0:T(8,128)} %m2_ref.1, ...), custom_call_target="tpu_custom_call" | custom-call | tf_op jit(solution)/shard_map/update/pallas_call | solution.py:340
  (19 shorter events, 1.6 us)
Async XLA Ops:
  0.6 16.0 %collective-permute-start.1 = (bf16[512,1024]{1,0:T(8,128)(2,1)}, bf16[512,1024]{1,0:T(8,128)(2,1)S(1)}, u32[]{:S(2)}, u32[]{:S(2)}) collective-permute-start(bf16[512,1024]{1,0:T(8,128)(2,1)} %bitcast.4), channel_id=1, source_target_pairs={{0,8},{1,25},{2,10},{3,27},{4,12},{5,29},{6,14},{7,31},{8,0},{9,17... | collective-permute-start | bytes 3145736 | tf_op jit(solution)/shard_map/ppermute | solution.py:358
  4.3 15.1 %collective-permute-start = (bf16[512,1024]{1,0:T(8,128)(2,1)}, bf16[512,1024]{1,0:T(8,128)(2,1)S(1)}, u32[]{:S(2)}, u32[]{:S(2)}) collective-permute-start(bf16[512,1024]{1,0:T(8,128)(2,1)} %bitcast.5), channel_id=1, source_target_pairs={{0,32},{1,97},{2,34},{3,99},{4,36},{5,101},{6,38},{7,103},{8,40},{... | collective-permute-start | bytes 3145736 | tf_op jit(solution)/shard_map/ppermute | solution.py:358
  6.8 3.4 %copy-start = (bf16[1,512,8192]{2,1,0:T(8,128)(2,1)S(1)}, bf16[1,512,8192]{2,1,0:T(8,128)(2,1)}, u32[]{:S(2)}) copy-start(bf16[1,512,8192]{2,1,0:T(8,128)(2,1)} %x_ref.7) | copy-start | bytes 25165828
  10.2 20.4 %copy-start.1 = (bf16[1,512,1024]{2,1,0:T(8,128)(2,1)S(1)}, bf16[1,512,1024]{2,1,0:T(8,128)(2,1)}, u32[]{:S(2)}) copy-start(bf16[1,512,1024]{2,1,0:T(8,128)(2,1)} %g_ref.5) | copy-start | bytes 3145732
  11.4 19.2 %collective-permute-start.2 = (bf16[512,1024]{1,0:T(8,128)(2,1)S(1)}, bf16[512,1024]{1,0:T(8,128)(2,1)S(1)}, u32[]{:S(2)}, u32[]{:S(2)}) collective-permute-start(bf16[512,1024]{1,0:T(8,128)(2,1)S(1)} %get-tuple-element.17), channel_id=1, source_target_pairs={{0,32},{1,97},{2,34},{3,99},{4,36},{5,101},{6,38},{7,103},{8,40},{... | collective-permute-start | bytes 3145736 | tf_op jit(solution)/shard_map/ppermute | solution.py:358
  11.6 18.9 %collective-permute-start.3 = (bf16[512,1024]{1,0:T(8,128)(2,1)S(1)}, bf16[512,1024]{1,0:T(8,128)(2,1)S(1)}, u32[]{:S(2)}, u32[]{:S(2)}) collective-permute-start(bf16[512,1024]{1,0:T(8,128)(2,1)S(1)} %get-tuple-element.18), channel_id=1, source_target_pairs={{0,8},{1,25},{2,10},{3,27},{4,12},{5,29},{6,14},{7,31},{8,0},{9,17... | collective-permute-start | bytes 3145736 | tf_op jit(solution)/shard_map/ppermute | solution.py:358
  11.7 31.6 %collective-permute-start.4 = (bf16[512,1024]{1,0:T(8,128)(2,1)S(1)}, bf16[512,1024]{1,0:T(8,128)(2,1)S(1)}, u32[]{:S(2)}, u32[]{:S(2)}) collective-permute-start(bf16[512,1024]{1,0:T(8,128)(2,1)S(1)} %get-tuple-element.21), channel_id=1, source_target_pairs={{0,32},{1,97},{2,34},{3,99},{4,36},{5,101},{6,38},{7,103},{8,40},{... | collective-permute-start | bytes 3145736 | tf_op jit(solution)/shard_map/ppermute | solution.py:358
  16.7 26.7 %collective-permute-start.5 = (bf16[512,1024]{1,0:T(8,128)(2,1)S(1)}, bf16[512,1024]{1,0:T(8,128)(2,1)S(1)}, u32[]{:S(2)}, u32[]{:S(2)}) collective-permute-start(bf16[512,1024]{1,0:T(8,128)(2,1)S(1)} %get-tuple-element.22), channel_id=1, source_target_pairs={{0,8},{1,25},{2,10},{3,27},{4,12},{5,29},{6,14},{7,31},{8,0},{9,17... | collective-permute-start | bytes 3145736 | tf_op jit(solution)/shard_map/ppermute | solution.py:358
  34.7 15.8 %collective-permute-start.10 = (s16[2064,256]{1,0:T(8,128)(2,1)S(1)}, s16[2064,256]{1,0:T(8,128)(2,1)S(1)}, u32[]{:S(2)}, u32[]{:S(2)}) collective-permute-start(s16[2064,256]{1,0:T(8,128)(2,1)S(1)} %get-tuple-element.19.after_ref), channel_id=1, source_target_pairs={{0,24},{1,9},{2,26},{3,11},{4,28},{5,13},{6,30},{7,15},{8,16},{9,1... | collective-permute-start | bytes 3170312 | tf_op jit(solution)/shard_map/ppermute | solution.py:358
  34.8 18.9 %collective-permute-start.7 = (s16[2064,256]{1,0:T(8,128)(2,1)S(1)}, s16[2064,256]{1,0:T(8,128)(2,1)S(1)}, u32[]{:S(2)}, u32[]{:S(2)}) collective-permute-start(s16[2064,256]{1,0:T(8,128)(2,1)S(1)} %get-tuple-element.25), channel_id=1, source_target_pairs={{0,96},{1,33},{2,98},{3,35},{4,100},{5,37},{6,102},{7,39},{8,104},... | collective-permute-start | bytes 3170312 | tf_op jit(solution)/shard_map/ppermute | solution.py:358
  39.3 27.4 %collective-permute-start.9 = (s16[2064,256]{1,0:T(8,128)(2,1)S(1)}, s16[2064,256]{1,0:T(8,128)(2,1)S(1)}, u32[]{:S(2)}, u32[]{:S(2)}) collective-permute-start(s16[2064,256]{1,0:T(8,128)(2,1)S(1)} %get-tuple-element.20.after_ref), channel_id=1, source_target_pairs={{0,24},{1,9},{2,26},{3,11},{4,28},{5,13},{6,30},{7,15},{8,16},{9,1... | collective-permute-start | bytes 3170312 | tf_op jit(solution)/shard_map/ppermute | solution.py:358
  43.3 27.5 %collective-permute-start.6 = (s16[2064,256]{1,0:T(8,128)(2,1)S(1)}, s16[2064,256]{1,0:T(8,128)(2,1)S(1)}, u32[]{:S(2)}, u32[]{:S(2)}) collective-permute-start(s16[2064,256]{1,0:T(8,128)(2,1)S(1)} %get-tuple-element.24), channel_id=1, source_target_pairs={{0,96},{1,33},{2,98},{3,35},{4,100},{5,37},{6,102},{7,39},{8,104},... | collective-permute-start | bytes 3170312 | tf_op jit(solution)/shard_map/ppermute | solution.py:358
  51.1 17.5 %collective-permute-start.14 = (s16[1040,256]{1,0:T(8,128)(2,1)S(1)}, s16[1040,256]{1,0:T(8,128)(2,1)S(1)}, u32[]{:S(2)}, u32[]{:S(2)}) collective-permute-start(s16[1040,256]{1,0:T(8,128)(2,1)S(1)} %late_3_1.1), channel_id=1, source_target_pairs={{0,32},{1,97},{2,34},{3,99},{4,36},{5,101},{6,38},{7,103},{8,40},{... | collective-permute-start | bytes 1597448 | tf_op jit(solution)/shard_map/ppermute | solution.py:358
  54.2 16.6 %collective-permute-start.12 = (s16[1040,256]{1,0:T(8,128)(2,1)S(1)}, s16[1040,256]{1,0:T(8,128)(2,1)S(1)}, u32[]{:S(2)}, u32[]{:S(2)}) collective-permute-start(s16[1040,256]{1,0:T(8,128)(2,1)S(1)} %late_3_0.1), channel_id=1, source_target_pairs={{0,8},{1,25},{2,10},{3,27},{4,12},{5,29},{6,14},{7,31},{8,0},{9,17... | collective-permute-start | bytes 1597448 | tf_op jit(solution)/shard_map/ppermute | solution.py:358
  57.6 20.4 %collective-permute-start.11 = (s16[1040,256]{1,0:T(8,128)(2,1)S(1)}, s16[1040,256]{1,0:T(8,128)(2,1)S(1)}, u32[]{:S(2)}, u32[]{:S(2)}) collective-permute-start(s16[1040,256]{1,0:T(8,128)(2,1)S(1)} %late_2_1.1), channel_id=1, source_target_pairs={{0,32},{1,97},{2,34},{3,99},{4,36},{5,101},{6,38},{7,103},{8,40},{... | collective-permute-start | bytes 1597448 | tf_op jit(solution)/shard_map/ppermute | solution.py:358
  66.8 11.2 %collective-permute-start.8 = (s16[1040,256]{1,0:T(8,128)(2,1)S(1)}, s16[1040,256]{1,0:T(8,128)(2,1)S(1)}, u32[]{:S(2)}, u32[]{:S(2)}) collective-permute-start(s16[1040,256]{1,0:T(8,128)(2,1)S(1)} %late_2_0.1), channel_id=1, source_target_pairs={{0,8},{1,25},{2,10},{3,27},{4,12},{5,29},{6,14},{7,31},{8,0},{9,17... | collective-permute-start | bytes 1597448 | tf_op jit(solution)/shard_map/ppermute | solution.py:358
  69.3 11.4 %collective-permute-start.15 = (s16[1040,256]{1,0:T(8,128)(2,1)S(1)}, s16[1040,256]{1,0:T(8,128)(2,1)S(1)}, u32[]{:S(2)}, u32[]{:S(2)}) collective-permute-start(s16[1040,256]{1,0:T(8,128)(2,1)S(1)} %late_1_1.1), channel_id=1, source_target_pairs={{0,96},{1,33},{2,98},{3,35},{4,100},{5,37},{6,102},{7,39},{8,104},... | collective-permute-start | bytes 1597448 | tf_op jit(solution)/shard_map/ppermute | solution.py:358
  71.6 9.2 %collective-permute-start.13 = (s16[1040,256]{1,0:T(8,128)(2,1)S(1)}, s16[1040,256]{1,0:T(8,128)(2,1)S(1)}, u32[]{:S(2)}, u32[]{:S(2)}) collective-permute-start(s16[1040,256]{1,0:T(8,128)(2,1)S(1)} %late_1_0.1), channel_id=1, source_target_pairs={{0,24},{1,9},{2,26},{3,11},{4,28},{5,13},{6,30},{7,15},{8,16},{9,1... | collective-permute-start | bytes 1597448 | tf_op jit(solution)/shard_map/ppermute | solution.py:358

commit v5 on v4

--- a/solution.py
+++ b/solution.py
@@ -161,31 +161,31 @@
         add_received(p_ref, 0, [(r, 0) for r in received], BLOCK, out)
 
 
-def finish_kernel(*refs):
-    flag_ref = refs[0]
-    grad_hbm, report_hbm, grad_ref, report_ref, sems = refs[-5:]
-    copies = []
-    acc = jnp.zeros((8, 128), jnp.float32)
-    for v in EVERY:
-        p_ref, r = refs[1 + 2 * v : 3 + 2 * v]
-        [scale] = scales_of([r])
-        for group in range(GROUPS):
-            at = slice(group * ROWS, (group + 1) * ROWS)
-            total = p_ref[at, :] + decode(r[at, :], scale)
-            grad_ref[v * ROWS : (v + 1) * ROWS, group * COLS : (group + 1) * COLS] = total
-            squared = total * total
-            squared = squared[:, :128] + squared[:, 128:]
-            acc = acc + jnp.sum(squared.reshape(ROWS // 8, 8, 128), axis=0)
-        at = slice(v * ROWS, (v + 1) * ROWS)
-        copies.append(pltpu.make_async_copy(grad_ref.at[at], grad_hbm.at[at], sems.at[v]))
-        copies[-1].start()
-    marked = jnp.where(flag_ref[0, 0] != 0, 1.0, 0.0)
-    acc = acc + pltpu.roll(acc, 64, axis=1)
-    lane = lax.broadcasted_iota(jnp.int32, (8, 128), 1)
-    acc = jnp.where(lane < 64, jnp.sum(acc, axis=0, keepdims=True), marked)
-    report_ref[...] = jnp.broadcast_to(acc[:1][None], (DEVICES, 1, 128))
-    copies.append(pltpu.make_async_copy(report_ref, report_hbm, sems.at[VARIANTS]))
-    copies[-1].start()
+def finish_kernel(v, *refs):
+    last = v == 0
+    grad_hbm, sum_out, grad_ref, sum_ref, sems = refs[-5:]
+    p_ref, r = refs[-7:-5]
+    acc = refs[0][...] if last else jnp.zeros((8, 128), jnp.float32)
+    [scale] = scales_of([r])
+    for group in range(GROUPS):
+        at = slice(group * ROWS, (group + 1) * ROWS)
+        total = p_ref[at, :] + decode(r[at, :], scale)
+        grad_ref[:, group * COLS : (group + 1) * COLS] = total
+        squared = total * total
+        squared = squared[:, :128] + squared[:, 128:]
+        acc = acc + jnp.sum(squared.reshape(ROWS // 8, 8, 128), axis=0)
+    copies = [pltpu.make_async_copy(grad_ref, grad_hbm.at[pl.ds(v * ROWS, ROWS)], sems.at[0])]
+    copies[0].start()
+    if last:
+        marked = jnp.where(refs[1][0, 0] != 0, 1.0, 0.0)
+        acc = acc + pltpu.roll(acc, 64, axis=1)
+        lane = lax.broadcasted_iota(jnp.int32, (8, 128), 1)
+        acc = jnp.where(lane < 64, jnp.sum(acc, axis=0, keepdims=True), marked)
+        sum_ref[...] = jnp.broadcast_to(acc[:1][None], (DEVICES, 1, 128))
+        copies.append(pltpu.make_async_copy(sum_ref, sum_out, sems.at[1]))
+        copies[1].start()
+    else:
+        sum_out[...] = acc
     for copy in copies:
         copy.wait()
 
@@ -213,12 +213,13 @@
     )
 
 
-def kernel_call(body, name, ins, outs, scratch, estimate, out_specs=None, vmem=KERNEL_VMEM):
+def kernel_call(body, name, ins, outs, scratch, estimate, out_specs=None, vmem=KERNEL_VMEM, aliases=None):
     return pl.pallas_call(
         body,
         out_shape=outs,
         in_specs=ins,
         out_specs=out_specs or [WHOLE] * len(outs),
+        input_output_aliases=aliases or {},
         scratch_shapes=scratch,
         compiler_params=pltpu.CompilerParams(vmem_limit_bytes=vmem),
         cost_estimate=estimate,
@@ -282,71 +283,90 @@
     )(*held)
 
 
-def finish(flag, held):
-    grad = jax.ShapeDtypeStruct((OWN, KV), jnp.float32)
-    report = jax.ShapeDtypeStruct((DEVICES, 1, 128), jnp.float32)
+def finish(v, before, own, code):
+    last = v == 0
     far = jax.ShapeDtypeStruct((FAR_ROWS, KV), jnp.float32)
-    return kernel_call(
-        finish_kernel,
-        "finish",
-        [SCALAR] + [WHOLE] * len(held),
-        [far, report],
-        [pltpu.VMEM(o.shape, o.dtype) for o in (grad, report)]
-        + [pltpu.SemaphoreType.DMA((VARIANTS + 1,))],
-        cost(VARIANTS, 0, 1),
-        [FAR] * 2,
-    )(flag, *held)
-
-
-UPDATE_ROWS = 256
-
-
-def update_kernel(bound, pipe_ref, reports, w_ref, m1_ref, m2_ref, g_ref, *refs):
-    new_w, new_m1, new_m2, clip_ref, own_ref = refs
-
-    @pl.when(pl.program_id(0) == 0)
-    def _():
-        lane = lax.broadcasted_iota(jnp.int32, (1, 128), 1)
-        total = jnp.zeros((1, 128), jnp.float32)
-        own = jnp.zeros((1, 128), jnp.float32)
-        for section in range(PIPE):
-            report = functools.reduce(
-                jnp.add, [reports[rank * PIPE + section] for rank in range(RANKS)]
-            )
-            marks = pltpu.roll(report, 64, axis=1)
-            total = total + jnp.where((lane < 64) & (marks == 0.0), report, 0.0)
-            own = jnp.where(pipe_ref[0] == section, marks, own)
-        total = jnp.sum(total, keepdims=True)
-        clip = jnp.minimum(1.0, bound / (jnp.sqrt(total) + 1e-06))
-        clip_ref[...] = jnp.broadcast_to(clip, (8, 128))
-        own_ref[...] = jnp.broadcast_to(own[:1, :1], (8, 128))
-
-    clip = clip_ref[:1, :1]
-    keep = own_ref[:1, :1] == 0.0
-    w, first_old, second_old = w_ref[0], m1_ref[0], m2_ref[0]
-    scaled = clip * g_ref[...]
-    first = 0.9 * first_old + 0.1 * scaled
-    second = 0.95 * second_old + 0.05 * scaled * scaled
-    root = second * lax.rsqrt(second)
-    updated = w - 0.02 * (first / (root + 1e-08) + 0.1 * w)
-    new_w[0] = jnp.where(keep, updated, w)
-    new_m1[0] = jnp.where(keep, first, first_old)
-    new_m2[0] = jnp.where(keep, second, second_old)
+    sums = jax.ShapeDtypeStruct((DEVICES, 1, 128) if last else (8, 128), jnp.float32)
+    return kernel_call(
+        functools.partial(finish_kernel, v),
+        f"finish_{v}",
+        [WHOLE, SCALAR, LEFT][: len(before)] + [WHOLE] * 2,
+        [far, sums],
+        [
+            pltpu.VMEM((ROWS, KV), jnp.float32),
+            pltpu.VMEM(sums.shape, sums.dtype),
+            pltpu.SemaphoreType.DMA((2,)),
+        ],
+        cost(1, 0, 1),
+        [FAR, FAR if last else WHOLE],
+        aliases={2: 0} if last else {},
+    )(*before, own, code)
+
+
+UPDATE_ROWS = 128
+
+
+def update_kernel(bound, pipe_ref, reports, *refs):
+    sources, results = refs[:4], refs[4:7]
+    buffers, (in_sems, out_sems) = refs[7:11], refs[11:]
+    w_ref, m1_ref, m2_ref, g_ref = buffers
+    arriving, leaving = [], []
+    for part in range(OWN // UPDATE_ROWS):
+        at = pl.ds(part * UPDATE_ROWS, UPDATE_ROWS)
+        arriving.append([])
+        for i, (source, buffer) in enumerate(zip(sources, buffers)):
+            source = source.at[0, at] if i < 3 else source.at[at]
+            copy = pltpu.make_async_copy(source, buffer.at[at], in_sems.at[part, i])
+            copy.start()
+            arriving[-1].append(copy)
+
+    lane = lax.broadcasted_iota(jnp.int32, (1, 128), 1)
+    total = jnp.zeros((1, 128), jnp.float32)
+    own = jnp.zeros((1, 128), jnp.float32)
+    for section in range(PIPE):
+        report = functools.reduce(
+            jnp.add, [reports[rank * PIPE + section] for rank in range(RANKS)]
+        )
+        marks = pltpu.roll(report, 64, axis=1)
+        total = total + jnp.where((lane < 64) & (marks == 0.0), report, 0.0)
+        own = jnp.where(pipe_ref[0] == section, marks, own)
+    total = jnp.sum(total, keepdims=True)
+    clip = jnp.minimum(1.0, bound / (jnp.sqrt(total) + 1e-06))
+    keep = own[:1, :1] == 0.0
+
+    for part, copies in enumerate(arriving):
+        for copy in copies:
+            copy.wait()
+        at = slice(part * UPDATE_ROWS, (part + 1) * UPDATE_ROWS)
+        w, first_old, second_old = w_ref[at], m1_ref[at], m2_ref[at]
+        scaled = clip * g_ref[at]
+        first = 0.9 * first_old + 0.1 * scaled
+        second = 0.95 * second_old + 0.05 * scaled * scaled
+        root = second * lax.rsqrt(second)
+        updated = w - 0.02 * (first / (root + 1e-08) + 0.1 * w)
+        w_ref[at] = jnp.where(keep, updated, w)
+        m1_ref[at] = jnp.where(keep, first, first_old)
+        m2_ref[at] = jnp.where(keep, second, second_old)
+        for i, (buffer, result) in enumerate(zip(buffers, results)):
+            copy = pltpu.make_async_copy(buffer.at[at], result.at[0, at], out_sems.at[part, i])
+            copy.start()
+            leaving.append(copy)
+    for copy in leaving:
+        copy.wait()
 
 
 def update(pipe, reports, w, m1, m2, grad, bound):
-    block = pl.BlockSpec((1, UPDATE_ROWS, KV), lambda i: (0, i, 0))
-    shape = jax.ShapeDtypeStruct((1, OWN, KV), jnp.float32)
-    return pl.pallas_call(
+    parts = OWN // UPDATE_ROWS
+    return kernel_call(
         functools.partial(update_kernel, bound),
-        grid=(OWN // UPDATE_ROWS,),
-        out_shape=[shape] * 3,
-        in_specs=[SCALAR, WHOLE, block, block, block]
-        + [pl.BlockSpec((UPDATE_ROWS, KV), lambda i: (i, 0))],
-        out_specs=[block] * 3,
-        scratch_shapes=[pltpu.VMEM((8, 128), jnp.float32)] * 2,
-        compiler_params=pltpu.CompilerParams(vmem_limit_bytes=UPDATE_VMEM),
-        name="update",
+        "update",
+        [SCALAR, WHOLE] + [FAR] * 4,
+        [jax.ShapeDtypeStruct((1, OWN, KV), jnp.float32)] * 3,
+        [pltpu.VMEM((OWN, KV), jnp.float32)] * 4
+        + [pltpu.SemaphoreType.DMA((parts, 4)), pltpu.SemaphoreType.DMA((parts, 3))],
+        cost(4, 0, 1),
+        [FAR] * 3,
+        UPDATE_VMEM,
     )(pipe, reports, w, m1, m2, grad)
 
 
@@ -378,8 +398,8 @@
     three = cross([late(2, v, kept[v], [two_urgent[v]], [0]) for v in EVERY], 2)
     four = cross([late(1, v, kept[v], [two[v], three_urgent[v]], [1, 0]) for v in EVERY], 3)
     own = sum_own([a for v in EVERY for a in (kept[v], two[v], three[v])])
-    held = [a for v in EVERY for a in (own[v], four[v])]
-    grad, report = finish(overflow_flags, held)
+    grad, squares = finish(1, [], own[1], four[1])
+    grad, report = finish(0, [squares, overflow_flags, grad], own[0], four[0])
     reports = lax.all_to_all(report, ("dp", "pipe"), 0, 0)
     bound = 0.5 * math.sqrt(D * KV * PIPE)
     pipe = lax.axis_index("pipe").astype(jnp.int32).reshape(1)

time: 112 us -> 111 us (level)
    pallas_call x2 -> x3, Pallas kernels: 8.99 us -> 9.51 us  [the longest x1 6.86 us: update(): kernel_call(functools.partial(update_kernel, bound), 'update', [SCALAR, W...]
  transfers between devices with their start and end apart: 16 -> 16, of which waited for: 9 -> 8; matrix products, arithmetic and copies ran while one was open for 0% -> 0% of each run, Pallas kernels for 17% -> 18%
where the time goes in v5:
time: 111 us
  waiting for transfers between devices  32.9 us (30%)
  Pallas kernels  28.3 us (25%)
  starting transfers between devices  24 us (22%)
  blocking collectives  20.7 us (19%)
  local copies, waits for them, and re-layouts  3.38 us (3%)
  between operations  1.57 us (1%)
    ppermute x16, waiting for transfers between devices, swap(): return lax.ppermute(value, ('dp', 'pipe'), pairs)  32.9 us
    ppermute x16, starting transfers between devices, swap(): return lax.ppermute(value, ('dp', 'pipe'), pairs)  24 us
    all_to_all x1, blocking collectives, per_device(): reports = lax.all_to_all(report, ('dp', 'pipe'), 0, 0)  20.7 us
    pallas_call x2, Pallas kernels, send(): kernel_call(functools.partial(send_kernel, half), f'send_{half}', [SCALAR...  8.27 us
    pallas_call x1, Pallas kernels, update(): kernel_call(functools.partial(update_kernel, bound), 'update', [SCALAR, W...  6.86 us
    pallas_call x1, Pallas kernels, keep(): kernel_call(keep_kernel, 'keep', [SCALAR, WHOLE, WHOLE, LEFT] + [WHOLE] *...  5.07 us
    pallas_call x6, Pallas kernels, late(): kernel_call(functools.partial(late_kernel, block, begins), f'late_{block}...  3.48 us
    unnamed x4, local copies, waits for them, and re-layouts  3.38 us
  transfers between devices with their start and end apart: 16, of which 8 were waited for; matrix products, arithmetic and copies ran while one was open for 0% of the time, Pallas kernels for 18%

profile of v5, /device:TPU:1, one launch (start us, length us, event | category | flops | bytes accessed | tf_op | source)
XLA Modules:
  0.0 111.1 jit_solution(4747235518463926097)
XLA Ops:
  0.6 3.6 %collective-permute-start.1 = (bf16[512,1024]{1,0:T(8,128)(2,1)}, bf16[512,1024]{1,0:T(8,128)(2,1)S(1)}, u32[]{:S(2)}, u32[]{:S(2)}) collective-permute-start(bf16[512,1024]{1,0:T(8,128)(2,1)} %bitcast.4), channel_id=1, source_target_pairs={{0,8},{1,25},{2,10},{3,27},{4,12},{5,29},{6,14},{7,31},{8,0},{9,17... | collective-permute-start | bytes 3145736 | tf_op jit(solution)/shard_map/ppermute | solution.py:378
  4.3 2.5 %collective-permute-start = (bf16[512,1024]{1,0:T(8,128)(2,1)}, bf16[512,1024]{1,0:T(8,128)(2,1)S(1)}, u32[]{:S(2)}, u32[]{:S(2)}) collective-permute-start(bf16[512,1024]{1,0:T(8,128)(2,1)} %bitcast.5), channel_id=1, source_target_pairs={{0,32},{1,97},{2,34},{3,99},{4,36},{5,101},{6,38},{7,103},{8,40},{... | collective-permute-start | bytes 3145736 | tf_op jit(solution)/shard_map/ppermute | solution.py:378
  6.8 3.4 %copy-done = bf16[1,512,8192]{2,1,0:T(8,128)(2,1)S(1)} copy-done((bf16[1,512,8192]{2,1,0:T(8,128)(2,1)S(1)}, bf16[1,512,8192]{2,1,0:T(8,128)(2,1)}, u32[]{:S(2)}) %copy-start) | copy-done | bytes 8388632
  10.2 1.2 %gather.1 = (bf16[512,1024]{1,0:T(8,128)(2,1)S(1)}, bf16[512,1024]{1,0:T(8,128)(2,1)S(1)}, bf16[512,1024]{1,0:T(8,128)(2,1)S(1)}, bf16[512,1024]{1,0:T(8,128)(2,1)S(1)}) custom-call(s32[2]{0:T(128)S(1)} %pad_add_fusion.me_ref.after_ref, bf16[1,512,8192]{2,1,0:T(8,128)(2,1)S(1)} %copy-done), custom_call_target="tpu_custom_call" | custom-call | bytes 12582912 | tf_op jit(solution)/shard_map/gather/pallas_call | solution.py:231
  11.7 2.5 %collective-permute-start.4 = (bf16[512,1024]{1,0:T(8,128)(2,1)S(1)}, bf16[512,1024]{1,0:T(8,128)(2,1)S(1)}, u32[]{:S(2)}, u32[]{:S(2)}) collective-permute-start(bf16[512,1024]{1,0:T(8,128)(2,1)S(1)} %get-tuple-element.23), channel_id=1, source_target_pairs={{0,32},{1,97},{2,34},{3,99},{4,36},{5,101},{6,38},{7,103},{8,40},{... | collective-permute-start | bytes 3145736 | tf_op jit(solution)/shard_map/ppermute | solution.py:378
  14.2 2.5 %collective-permute-done.1.refs_1_ = bf16[512,1024]{1,0:T(8,128)(2,1)S(1)} collective-permute-done((bf16[512,1024]{1,0:T(8,128)(2,1)}, bf16[512,1024]{1,0:T(8,128)(2,1)S(1)}, u32[]{:S(2)}, u32[]{:S(2)}) %collective-permute-start.1) | collective-permute-done | bytes 1048608 | tf_op jit(solution)/shard_map/ppermute | solution.py:378
  16.7 2.7 %collective-permute-start.5 = (bf16[512,1024]{1,0:T(8,128)(2,1)S(1)}, bf16[512,1024]{1,0:T(8,128)(2,1)S(1)}, u32[]{:S(2)}, u32[]{:S(2)}) collective-permute-start(bf16[512,1024]{1,0:T(8,128)(2,1)S(1)} %get-tuple-element.24), channel_id=1, source_target_pairs={{0,8},{1,25},{2,10},{3,27},{4,12},{5,29},{6,14},{7,31},{8,0},{9,17... | collective-permute-start | bytes 3145736 | tf_op jit(solution)/shard_map/ppermute | solution.py:378
  19.3 11.2 %collective-permute-done.2.refs_2_ = bf16[512,1024]{1,0:T(8,128)(2,1)S(1)} collective-permute-done((bf16[512,1024]{1,0:T(8,128)(2,1)S(1)}, bf16[512,1024]{1,0:T(8,128)(2,1)S(1)}, u32[]{:S(2)}, u32[]{:S(2)}) %collective-permute-start.2) | collective-permute-done | bytes 1048608 | tf_op jit(solution)/shard_map/ppermute | solution.py:378
  30.6 4.1 %send_1.1 = (s16[2064,256]{1,0:T(8,128)(2,1)S(1)}, s16[2064,256]{1,0:T(8,128)(2,1)S(1)}) custom-call(s32[2]{0:T(128)S(1)} %pad_add_fusion.me_ref.after_ref, bf16[1,512,8192]{2,1,0:T(8,128)(2,1)S(1)} %copy-done, bf16[1,512,1024]{2,1,0:T(8,128)(2,1)S(1)} %copy-done.1, s32[2]{0:T(128)S(1)} %pad_add_fusion.me_ref.after_ref, ...), custom_call_target="tpu_custom_call" | custom-call | flops 2147483648 | bytes 6291456 | tf_op jit(solution)/shard_map/send_1/pallas_call | solution.py:242
  35.2 4.1 %send_0.1 = (s16[2064,256]{1,0:T(8,128)(2,1)S(1)}, s16[2064,256]{1,0:T(8,128)(2,1)S(1)}) custom-call(s32[2]{0:T(128)S(1)} %pad_add_fusion.me_ref.after_ref, bf16[1,512,8192]{2,1,0:T(8,128)(2,1)S(1)} %copy-done, bf16[1,512,1024]{2,1,0:T(8,128)(2,1)S(1)} %copy-done.1, s16[2064,256]{1,0:T(8,128)(2,1)S(1)} %get-tuple-element.21.after_ref, ...), custom_call_target="tpu_custom_call" | custom-call | flops 2147483648 | bytes 6291456 | tf_op jit(solution)/shard_map/send_0/pallas_call | solution.py:242
  39.4 1.4 %collective-permute-start.9 = (s16[2064,256]{1,0:T(8,128)(2,1)S(1)}, s16[2064,256]{1,0:T(8,128)(2,1)S(1)}, u32[]{:S(2)}, u32[]{:S(2)}) collective-permute-start(s16[2064,256]{1,0:T(8,128)(2,1)S(1)} %get-tuple-element.22.after_ref), channel_id=1, source_target_pairs={{0,24},{1,9},{2,26},{3,11},{4,28},{5,13},{6,30},{7,15},{8,16},{9,1... | collective-permute-start | bytes 3170312 | tf_op jit(solution)/shard_map/ppermute | solution.py:378
  40.8 2.5 %collective-permute-done.4.refs_2_ = bf16[512,1024]{1,0:T(8,128)(2,1)S(1)} collective-permute-done((bf16[512,1024]{1,0:T(8,128)(2,1)S(1)}, bf16[512,1024]{1,0:T(8,128)(2,1)S(1)}, u32[]{:S(2)}, u32[]{:S(2)}) %collective-permute-start.4) | collective-permute-done | bytes 1048608 | tf_op jit(solution)/shard_map/ppermute | solution.py:378
  43.3 5.1 %keep.1 = (f32[4096,256]{1,0:T(8,128)S(1)}, f32[4096,256]{1,0:T(8,128)S(1)}) custom-call(s32[2]{0:T(128)S(1)} %pad_add_fusion.me_ref.after_ref, bf16[1,512,8192]{2,1,0:T(8,128)(2,1)S(1)} %copy-done, bf16[1,512,1024]{2,1,0:T(8,128)(2,1)S(1)} %copy-done.1, s16[2064,256]{1,0:T(8,128)(2,1)S(1)} %get-tuple-element.22.after_ref, ...), custom_call_target="tpu_custom_call" | custom-call | flops 4294967296 | bytes 12582912 | tf_op jit(solution)/shard_map/keep/pallas_call | solution.py:253
  48.4 2.1 %collective-permute-done.10.refs_0_ = s16[2064,256]{1,0:T(8,128)(2,1)S(1)} collective-permute-done((s16[2064,256]{1,0:T(8,128)(2,1)S(1)}, s16[2064,256]{1,0:T(8,128)(2,1)S(1)}, u32[]{:S(2)}, u32[]{:S(2)}) %collective-permute-start.10) | collective-permute-done | bytes 1056800 | tf_op jit(solution)/shard_map/ppermute | solution.py:378
  50.5 0.5 late_3_1.1
  51.1 2.6 %collective-permute-start.12 = (s16[1040,256]{1,0:T(8,128)(2,1)S(1)}, s16[1040,256]{1,0:T(8,128)(2,1)S(1)}, u32[]{:S(2)}, u32[]{:S(2)}) collective-permute-start(s16[1040,256]{1,0:T(8,128)(2,1)S(1)} %late_3_1.1), channel_id=1, source_target_pairs={{0,32},{1,97},{2,34},{3,99},{4,36},{5,101},{6,38},{7,103},{8,40},{... | collective-permute-start | bytes 1597448 | tf_op jit(solution)/shard_map/ppermute | solution.py:378
  53.7 0.5 late_3_0.1
  54.2 2.8 %collective-permute-start.14 = (s16[1040,256]{1,0:T(8,128)(2,1)S(1)}, s16[1040,256]{1,0:T(8,128)(2,1)S(1)}, u32[]{:S(2)}, u32[]{:S(2)}) collective-permute-start(s16[1040,256]{1,0:T(8,128)(2,1)S(1)} %late_3_0.1), channel_id=1, source_target_pairs={{0,8},{1,25},{2,10},{3,27},{4,12},{5,29},{6,14},{7,31},{8,0},{9,17... | collective-permute-start | bytes 1597448 | tf_op jit(solution)/shard_map/ppermute | solution.py:378
  57.0 0.5 late_2_1.1
  58.5 8.2 %collective-permute-done.9.refs_4_.refs_0_ = s16[2064,256]{1,0:T(8,128)(2,1)S(1)} collective-permute-done((s16[2064,256]{1,0:T(8,128)(2,1)S(1)}, s16[2064,256]{1,0:T(8,128)(2,1)S(1)}, u32[]{:S(2)}, u32[]{:S(2)}) %collective-permute-start.9) | collective-permute-done | bytes 1056800 | tf_op jit(solution)/shard_map/ppermute | solution.py:378
  66.8 1.8 %collective-permute-start.8 = (s16[1040,256]{1,0:T(8,128)(2,1)S(1)}, s16[1040,256]{1,0:T(8,128)(2,1)S(1)}, u32[]{:S(2)}, u32[]{:S(2)}) collective-permute-start(s16[1040,256]{1,0:T(8,128)(2,1)S(1)} %late_2_0.1), channel_id=1, source_target_pairs={{0,8},{1,25},{2,10},{3,27},{4,12},{5,29},{6,14},{7,31},{8,0},{9,17... | collective-permute-start | bytes 1597448 | tf_op jit(solution)/shard_map/ppermute | solution.py:378
  68.6 0.7 late_1_1.1
  69.3 1.5 %collective-permute-start.13 = (s16[1040,256]{1,0:T(8,128)(2,1)S(1)}, s16[1040,256]{1,0:T(8,128)(2,1)S(1)}, u32[]{:S(2)}, u32[]{:S(2)}) collective-permute-start(s16[1040,256]{1,0:T(8,128)(2,1)S(1)} %late_1_1.1), channel_id=1, source_target_pairs={{0,96},{1,33},{2,98},{3,35},{4,100},{5,37},{6,102},{7,39},{8,104},... | collective-permute-start | bytes 1597448 | tf_op jit(solution)/shard_map/ppermute | solution.py:378
  70.9 0.7 late_1_0.1
  71.6 1.3 %collective-permute-start.15 = (s16[1040,256]{1,0:T(8,128)(2,1)S(1)}, s16[1040,256]{1,0:T(8,128)(2,1)S(1)}, u32[]{:S(2)}, u32[]{:S(2)}) collective-permute-start(s16[1040,256]{1,0:T(8,128)(2,1)S(1)} %late_1_0.1), channel_id=1, source_target_pairs={{0,24},{1,9},{2,26},{3,11},{4,28},{5,13},{6,30},{7,15},{8,16},{9,1... | collective-permute-start | bytes 1597448 | tf_op jit(solution)/shard_map/ppermute | solution.py:378
  73.5 4.4 %collective-permute-done.11.refs_5_ = s16[1040,256]{1,0:T(8,128)(2,1)S(1)} collective-permute-done((s16[1040,256]{1,0:T(8,128)(2,1)S(1)}, s16[1040,256]{1,0:T(8,128)(2,1)S(1)}, u32[]{:S(2)}, u32[]{:S(2)}) %collective-permute-start.11) | collective-permute-done | bytes 532512 | tf_op jit(solution)/shard_map/ppermute | solution.py:378
  78.0 0.9 sum.1
  78.8 1.8 %collective-permute-done.13.refs_1_ = s16[1040,256]{1,0:T(8,128)(2,1)S(1)} collective-permute-done((s16[1040,256]{1,0:T(8,128)(2,1)S(1)}, s16[1040,256]{1,0:T(8,128)(2,1)S(1)}, u32[]{:S(2)}, u32[]{:S(2)}) %collective-permute-start.13) | collective-permute-done | bytes 532512 | tf_op jit(solution)/shard_map/ppermute | solution.py:378
  80.6 1.3 %finish_1.1 = (f32[12288,1024]{1,0:T(8,128)}, f32[8,128]{1,0:T(8,128)S(1)}) custom-call(f32[1024,256]{1,0:T(8,128)S(1)} %get-tuple-element.29.refs_0_, s16[1040,256]{1,0:T(8,128)(2,1)S(1)} %collective-permute-done.13.refs_1_), custom_call_target="tpu_custom_call" | custom-call | bytes 1572864 | tf_op jit(solution)/shard_map/finish_1/pallas_call | solution.py:290
  81.9 1.4 %finish_0.1 = (f32[12288,1024]{1,0:T(8,128)}, f32[128,1,128]{2,1,0:T(1,128)S(1)}) custom-call(f32[8,128]{1,0:T(8,128)S(1)} %get-tuple-element.30.refs_0_, s32[1,1]{1,0:T(1,128)S(6)} %copy.11.refs_1_, f32[12288,1024]{1,0:T(8,128)} %get-tuple-element.31.refs_2_, f32[1024,256]{1,0:T(8,128)S(1)} %get-tuple-element.32.refs_3_, ...), custom_call_target="tpu_custom_call", output_to_operand_aliasing={{0}: (2, {})} | custom-call | bytes 1572864 | tf_op jit(solution)/shard_map/finish_0/pallas_call | solution.py:290
  83.3 20.7 %all_to_all.5.reports = f32[128,1,128]{2,1,0:T(1,128)} all-to-all(f32[128,1,128]{2,1,0:T(1,128)S(1)} %get-tuple-element.33), channel_id=1, replica_groups=mesh['dp'=16,'pipe'=8] {'dp','pipe'}, dimensions={0} | all-to-all | bytes 131072 | tf_op jit(solution)/shard_map/all_to_all | solution.py:403
  104.1 6.9 %update.1 = (f32[1,512,1024]{2,1,0:T(8,128)}, f32[1,512,1024]{2,1,0:T(8,128)}, f32[1,512,1024]{2,1,0:T(8,128)}) custom-call(s32[1]{0:T(128)} %bitcast.pipe_ref, f32[128,1,128]{2,1,0:T(1,128)} %all_to_all.5.reports, f32[1,512,1024]{2,1,0:T(8,128)} %refs_0_.1, f32[1,512,1024]{2,1,0:T(8,128)} %refs_1_.2, f32[1,512,1024]{2,1,0:T(8,128)} %refs_2_.1, ...), custom_call_target="tpu_custom_call" | custom-call | bytes 6291456 | tf_op jit(solution)/shard_map/update/pallas_call | solution.py:360
  (20 shorter events, 1.9 us)
Async XLA Ops:
  0.6 16.0 %collective-permute-start.1 = (bf16[512,1024]{1,0:T(8,128)(2,1)}, bf16[512,1024]{1,0:T(8,128)(2,1)S(1)}, u32[]{:S(2)}, u32[]{:S(2)}) collective-permute-start(bf16[512,1024]{1,0:T(8,128)(2,1)} %bitcast.4), channel_id=1, source_target_pairs={{0,8},{1,25},{2,10},{3,27},{4,12},{5,29},{6,14},{7,31},{8,0},{9,17... | collective-permute-start | bytes 3145736 | tf_op jit(solution)/shard_map/ppermute | solution.py:378
  4.3 15.1 %collective-permute-start = (bf16[512,1024]{1,0:T(8,128)(2,1)}, bf16[512,1024]{1,0:T(8,128)(2,1)S(1)}, u32[]{:S(2)}, u32[]{:S(2)}) collective-permute-start(bf16[512,1024]{1,0:T(8,128)(2,1)} %bitcast.5), channel_id=1, source_target_pairs={{0,32},{1,97},{2,34},{3,99},{4,36},{5,101},{6,38},{7,103},{8,40},{... | collective-permute-start | bytes 3145736 | tf_op jit(solution)/shard_map/ppermute | solution.py:378
  6.8 3.4 %copy-start = (bf16[1,512,8192]{2,1,0:T(8,128)(2,1)S(1)}, bf16[1,512,8192]{2,1,0:T(8,128)(2,1)}, u32[]{:S(2)}) copy-start(bf16[1,512,8192]{2,1,0:T(8,128)(2,1)} %x_ref.7) | copy-start | bytes 25165828
  10.2 20.4 %copy-start.1 = (bf16[1,512,1024]{2,1,0:T(8,128)(2,1)S(1)}, bf16[1,512,1024]{2,1,0:T(8,128)(2,1)}, u32[]{:S(2)}) copy-start(bf16[1,512,1024]{2,1,0:T(8,128)(2,1)} %g_ref.5) | copy-start | bytes 3145732
  11.4 19.2 %collective-permute-start.2 = (bf16[512,1024]{1,0:T(8,128)(2,1)S(1)}, bf16[512,1024]{1,0:T(8,128)(2,1)S(1)}, u32[]{:S(2)}, u32[]{:S(2)}) collective-permute-start(bf16[512,1024]{1,0:T(8,128)(2,1)S(1)} %get-tuple-element.19), channel_id=1, source_target_pairs={{0,32},{1,97},{2,34},{3,99},{4,36},{5,101},{6,38},{7,103},{8,40},{... | collective-permute-start | bytes 3145736 | tf_op jit(solution)/shard_map/ppermute | solution.py:378
  11.7 18.9 %collective-permute-start.3 = (bf16[512,1024]{1,0:T(8,128)(2,1)S(1)}, bf16[512,1024]{1,0:T(8,128)(2,1)S(1)}, u32[]{:S(2)}, u32[]{:S(2)}) collective-permute-start(bf16[512,1024]{1,0:T(8,128)(2,1)S(1)} %get-tuple-element.20), channel_id=1, source_target_pairs={{0,8},{1,25},{2,10},{3,27},{4,12},{5,29},{6,14},{7,31},{8,0},{9,17... | collective-permute-start | bytes 3145736 | tf_op jit(solution)/shard_map/ppermute | solution.py:378
  11.7 31.6 %collective-permute-start.4 = (bf16[512,1024]{1,0:T(8,128)(2,1)S(1)}, bf16[512,1024]{1,0:T(8,128)(2,1)S(1)}, u32[]{:S(2)}, u32[]{:S(2)}) collective-permute-start(bf16[512,1024]{1,0:T(8,128)(2,1)S(1)} %get-tuple-element.23), channel_id=1, source_target_pairs={{0,32},{1,97},{2,34},{3,99},{4,36},{5,101},{6,38},{7,103},{8,40},{... | collective-permute-start | bytes 3145736 | tf_op jit(solution)/shard_map/ppermute | solution.py:378
  16.7 26.7 %collective-permute-start.5 = (bf16[512,1024]{1,0:T(8,128)(2,1)S(1)}, bf16[512,1024]{1,0:T(8,128)(2,1)S(1)}, u32[]{:S(2)}, u32[]{:S(2)}) collective-permute-start(bf16[512,1024]{1,0:T(8,128)(2,1)S(1)} %get-tuple-element.24), channel_id=1, source_target_pairs={{0,8},{1,25},{2,10},{3,27},{4,12},{5,29},{6,14},{7,31},{8,0},{9,17... | collective-permute-start | bytes 3145736 | tf_op jit(solution)/shard_map/ppermute | solution.py:378
  34.7 15.8 %collective-permute-start.10 = (s16[2064,256]{1,0:T(8,128)(2,1)S(1)}, s16[2064,256]{1,0:T(8,128)(2,1)S(1)}, u32[]{:S(2)}, u32[]{:S(2)}) collective-permute-start(s16[2064,256]{1,0:T(8,128)(2,1)S(1)} %get-tuple-element.21.after_ref), channel_id=1, source_target_pairs={{0,24},{1,9},{2,26},{3,11},{4,28},{5,13},{6,30},{7,15},{8,16},{9,1... | collective-permute-start | bytes 3170312 | tf_op jit(solution)/shard_map/ppermute | solution.py:378
  34.8 18.9 %collective-permute-start.7 = (s16[2064,256]{1,0:T(8,128)(2,1)S(1)}, s16[2064,256]{1,0:T(8,128)(2,1)S(1)}, u32[]{:S(2)}, u32[]{:S(2)}) collective-permute-start(s16[2064,256]{1,0:T(8,128)(2,1)S(1)} %get-tuple-element.27), channel_id=1, source_target_pairs={{0,96},{1,33},{2,98},{3,35},{4,100},{5,37},{6,102},{7,39},{8,104},... | collective-permute-start | bytes 3170312 | tf_op jit(solution)/shard_map/ppermute | solution.py:378
  39.4 27.4 %collective-permute-start.9 = (s16[2064,256]{1,0:T(8,128)(2,1)S(1)}, s16[2064,256]{1,0:T(8,128)(2,1)S(1)}, u32[]{:S(2)}, u32[]{:S(2)}) collective-permute-start(s16[2064,256]{1,0:T(8,128)(2,1)S(1)} %get-tuple-element.22.after_ref), channel_id=1, source_target_pairs={{0,24},{1,9},{2,26},{3,11},{4,28},{5,13},{6,30},{7,15},{8,16},{9,1... | collective-permute-start | bytes 3170312 | tf_op jit(solution)/shard_map/ppermute | solution.py:378
  43.3 27.5 %collective-permute-start.6 = (s16[2064,256]{1,0:T(8,128)(2,1)S(1)}, s16[2064,256]{1,0:T(8,128)(2,1)S(1)}, u32[]{:S(2)}, u32[]{:S(2)}) collective-permute-start(s16[2064,256]{1,0:T(8,128)(2,1)S(1)} %get-tuple-element.26), channel_id=1, source_target_pairs={{0,96},{1,33},{2,98},{3,35},{4,100},{5,37},{6,102},{7,39},{8,104},... | collective-permute-start | bytes 3170312 | tf_op jit(solution)/shard_map/ppermute | solution.py:378
  51.1 17.5 %collective-permute-start.12 = (s16[1040,256]{1,0:T(8,128)(2,1)S(1)}, s16[1040,256]{1,0:T(8,128)(2,1)S(1)}, u32[]{:S(2)}, u32[]{:S(2)}) collective-permute-start(s16[1040,256]{1,0:T(8,128)(2,1)S(1)} %late_3_1.1), channel_id=1, source_target_pairs={{0,32},{1,97},{2,34},{3,99},{4,36},{5,101},{6,38},{7,103},{8,40},{... | collective-permute-start | bytes 1597448 | tf_op jit(solution)/shard_map/ppermute | solution.py:378
  54.2 16.6 %collective-permute-start.14 = (s16[1040,256]{1,0:T(8,128)(2,1)S(1)}, s16[1040,256]{1,0:T(8,128)(2,1)S(1)}, u32[]{:S(2)}, u32[]{:S(2)}) collective-permute-start(s16[1040,256]{1,0:T(8,128)(2,1)S(1)} %late_3_0.1), channel_id=1, source_target_pairs={{0,8},{1,25},{2,10},{3,27},{4,12},{5,29},{6,14},{7,31},{8,0},{9,17... | collective-permute-start | bytes 1597448 | tf_op jit(solution)/shard_map/ppermute | solution.py:378
  57.6 20.4 %collective-permute-start.11 = (s16[1040,256]{1,0:T(8,128)(2,1)S(1)}, s16[1040,256]{1,0:T(8,128)(2,1)S(1)}, u32[]{:S(2)}, u32[]{:S(2)}) collective-permute-start(s16[1040,256]{1,0:T(8,128)(2,1)S(1)} %late_2_1.1), channel_id=1, source_target_pairs={{0,32},{1,97},{2,34},{3,99},{4,36},{5,101},{6,38},{7,103},{8,40},{... | collective-permute-start | bytes 1597448 | tf_op jit(solution)/shard_map/ppermute | solution.py:378
  66.8 11.2 %collective-permute-start.8 = (s16[1040,256]{1,0:T(8,128)(2,1)S(1)}, s16[1040,256]{1,0:T(8,128)(2,1)S(1)}, u32[]{:S(2)}, u32[]{:S(2)}) collective-permute-start(s16[1040,256]{1,0:T(8,128)(2,1)S(1)} %late_2_0.1), channel_id=1, source_target_pairs={{0,8},{1,25},{2,10},{3,27},{4,12},{5,29},{6,14},{7,31},{8,0},{9,17... | collective-permute-start | bytes 1597448 | tf_op jit(solution)/shard_map/ppermute | solution.py:378
  69.3 11.4 %collective-permute-start.13 = (s16[1040,256]{1,0:T(8,128)(2,1)S(1)}, s16[1040,256]{1,0:T(8,128)(2,1)S(1)}, u32[]{:S(2)}, u32[]{:S(2)}) collective-permute-start(s16[1040,256]{1,0:T(8,128)(2,1)S(1)} %late_1_1.1), channel_id=1, source_target_pairs={{0,96},{1,33},{2,98},{3,35},{4,100},{5,37},{6,102},{7,39},{8,104},... | collective-permute-start | bytes 1597448 | tf_op jit(solution)/shard_map/ppermute | solution.py:378
  71.6 10.3 %collective-permute-start.15 = (s16[1040,256]{1,0:T(8,128)(2,1)S(1)}, s16[1040,256]{1,0:T(8,128)(2,1)S(1)}, u32[]{:S(2)}, u32[]{:S(2)}) collective-permute-start(s16[1040,256]{1,0:T(8,128)(2,1)S(1)} %late_1_0.1), channel_id=1, source_target_pairs={{0,24},{1,9},{2,26},{3,11},{4,28},{5,13},{6,30},{7,15},{8,16},{9,1... | collective-permute-start | bytes 1597448 | tf_op jit(solution)/shard_map/ppermute | solution.py:378

commit v6 on v5

--- a/solution.py
+++ b/solution.py
@@ -29,8 +29,8 @@
 
 XA, XB, YA, YB = 4, 12, 1, 3
 ORDERS = (
-    ((XA, XB, YA, YB), (YA, YB, XA, XB)),
-    ((XB, XA, YB, YA), (YB, YA, XB, XA)),
+    ((XA, XB, YB, YA), (YA, YB, XA, XB)),
+    ((XB, XA, YA, YB), (YB, YA, XB, XA)),
 )
 EVERY = range(VARIANTS)
 

time: 111 us -> 110 us (level)
  waiting for transfers between devices: 32.9 us -> 36.8 us
  starting transfers between devices: 24 us -> 20.2 us
  blocking collectives: 20.7 us -> 19.5 us
    ppermute x16, waiting for transfers between devices: 32.9 us -> 36.8 us  [swap(): return lax.ppermute(value, ('dp', 'pipe'), pairs)]
    ppermute x16, starting transfers between devices: 24 us -> 20.2 us  [swap(): return lax.ppermute(value, ('dp', 'pipe'), pairs)]
    all_to_all x1, blocking collectives: 20.7 us -> 19.5 us  [per_device(): reports = lax.all_to_all(report, ('dp', 'pipe'), 0, 0)]
  transfers between devices with their start and end apart: 16 -> 16, of which waited for: 8 -> 9; matrix products, arithmetic and copies ran while one was open for 0% -> 0% of each run, Pallas kernels for 18% -> 18%
where the time goes in v6:
time: 110 us
  waiting for transfers between devices  36.8 us (33%)
  Pallas kernels  28.3 us (26%)
  starting transfers between devices  20.2 us (18%)
  blocking collectives  19.5 us (18%)
  local copies, waits for them, and re-layouts  3.38 us (3%)
  between operations  1.57 us (1%)
    ppermute x16, waiting for transfers between devices, swap(): return lax.ppermute(value, ('dp', 'pipe'), pairs)  36.8 us
    ppermute x16, starting transfers between devices, swap(): return lax.ppermute(value, ('dp', 'pipe'), pairs)  20.2 us
    all_to_all x1, blocking collectives, per_device(): reports = lax.all_to_all(report, ('dp', 'pipe'), 0, 0)  19.5 us
    pallas_call x2, Pallas kernels, send(): kernel_call(functools.partial(send_kernel, half), f'send_{half}', [SCALAR...  8.27 us
    pallas_call x1, Pallas kernels, update(): kernel_call(functools.partial(update_kernel, bound), 'update', [SCALAR, W...  6.86 us
    pallas_call x1, Pallas kernels, keep(): kernel_call(keep_kernel, 'keep', [SCALAR, WHOLE, WHOLE, LEFT] + [WHOLE] *...  5.07 us
    pallas_call x6, Pallas kernels, late(): kernel_call(functools.partial(late_kernel, block, begins), f'late_{block}...  3.48 us
    unnamed x4, local copies, waits for them, and re-layouts  3.38 us
  transfers between devices with their start and end apart: 16, of which 9 were waited for; matrix products, arithmetic and copies ran while one was open for 0% of the time, Pallas kernels for 18%

profile of v6, /device:TPU:1, one launch (start us, length us, event | category | flops | bytes accessed | tf_op | source)
XLA Modules:
  0.0 109.9 jit_solution(7990233660148327025)
XLA Ops:
  0.6 3.6 %collective-permute-start.1 = (bf16[512,1024]{1,0:T(8,128)(2,1)}, bf16[512,1024]{1,0:T(8,128)(2,1)S(1)}, u32[]{:S(2)}, u32[]{:S(2)}) collective-permute-start(bf16[512,1024]{1,0:T(8,128)(2,1)} %bitcast.4), channel_id=1, source_target_pairs={{0,8},{1,25},{2,10},{3,27},{4,12},{5,29},{6,14},{7,31},{8,0},{9,17... | collective-permute-start | bytes 3145736 | tf_op jit(solution)/shard_map/ppermute | solution.py:378
  4.3 2.5 %collective-permute-start = (bf16[512,1024]{1,0:T(8,128)(2,1)}, bf16[512,1024]{1,0:T(8,128)(2,1)S(1)}, u32[]{:S(2)}, u32[]{:S(2)}) collective-permute-start(bf16[512,1024]{1,0:T(8,128)(2,1)} %bitcast.5), channel_id=1, source_target_pairs={{0,32},{1,97},{2,34},{3,99},{4,36},{5,101},{6,38},{7,103},{8,40},{... | collective-permute-start | bytes 3145736 | tf_op jit(solution)/shard_map/ppermute | solution.py:378
  6.8 3.4 %copy-done = bf16[1,512,8192]{2,1,0:T(8,128)(2,1)S(1)} copy-done((bf16[1,512,8192]{2,1,0:T(8,128)(2,1)S(1)}, bf16[1,512,8192]{2,1,0:T(8,128)(2,1)}, u32[]{:S(2)}) %copy-start) | copy-done | bytes 8388632
  10.2 1.2 %gather.1 = (bf16[512,1024]{1,0:T(8,128)(2,1)S(1)}, bf16[512,1024]{1,0:T(8,128)(2,1)S(1)}, bf16[512,1024]{1,0:T(8,128)(2,1)S(1)}, bf16[512,1024]{1,0:T(8,128)(2,1)S(1)}) custom-call(s32[2]{0:T(128)S(1)} %pad_add_fusion.me_ref.after_ref, bf16[1,512,8192]{2,1,0:T(8,128)(2,1)S(1)} %copy-done), custom_call_target="tpu_custom_call" | custom-call | bytes 12582912 | tf_op jit(solution)/shard_map/gather/pallas_call | solution.py:231
  11.7 2.5 %collective-permute-start.4 = (bf16[512,1024]{1,0:T(8,128)(2,1)S(1)}, bf16[512,1024]{1,0:T(8,128)(2,1)S(1)}, u32[]{:S(2)}, u32[]{:S(2)}) collective-permute-start(bf16[512,1024]{1,0:T(8,128)(2,1)S(1)} %get-tuple-element.23), channel_id=1, source_target_pairs={{0,32},{1,97},{2,34},{3,99},{4,36},{5,101},{6,38},{7,103},{8,40},{... | collective-permute-start | bytes 3145736 | tf_op jit(solution)/shard_map/ppermute | solution.py:378
  14.2 2.5 %collective-permute-done.1.refs_1_ = bf16[512,1024]{1,0:T(8,128)(2,1)S(1)} collective-permute-done((bf16[512,1024]{1,0:T(8,128)(2,1)}, bf16[512,1024]{1,0:T(8,128)(2,1)S(1)}, u32[]{:S(2)}, u32[]{:S(2)}) %collective-permute-start.1) | collective-permute-done | bytes 1048608 | tf_op jit(solution)/shard_map/ppermute | solution.py:378
  16.7 2.7 %collective-permute-start.5 = (bf16[512,1024]{1,0:T(8,128)(2,1)S(1)}, bf16[512,1024]{1,0:T(8,128)(2,1)S(1)}, u32[]{:S(2)}, u32[]{:S(2)}) collective-permute-start(bf16[512,1024]{1,0:T(8,128)(2,1)S(1)} %get-tuple-element.24), channel_id=1, source_target_pairs={{0,8},{1,25},{2,10},{3,27},{4,12},{5,29},{6,14},{7,31},{8,0},{9,17... | collective-permute-start | bytes 3145736 | tf_op jit(solution)/shard_map/ppermute | solution.py:378
  19.3 11.2 %collective-permute-done.2.refs_2_ = bf16[512,1024]{1,0:T(8,128)(2,1)S(1)} collective-permute-done((bf16[512,1024]{1,0:T(8,128)(2,1)S(1)}, bf16[512,1024]{1,0:T(8,128)(2,1)S(1)}, u32[]{:S(2)}, u32[]{:S(2)}) %collective-permute-start.2) | collective-permute-done | bytes 1048608 | tf_op jit(solution)/shard_map/ppermute | solution.py:378
  30.6 4.1 %send_1.1 = (s16[2064,256]{1,0:T(8,128)(2,1)S(1)}, s16[2064,256]{1,0:T(8,128)(2,1)S(1)}) custom-call(s32[2]{0:T(128)S(1)} %pad_add_fusion.me_ref.after_ref, bf16[1,512,8192]{2,1,0:T(8,128)(2,1)S(1)} %copy-done, bf16[1,512,1024]{2,1,0:T(8,128)(2,1)S(1)} %copy-done.1, s32[2]{0:T(128)S(1)} %pad_add_fusion.me_ref.after_ref, ...), custom_call_target="tpu_custom_call" | custom-call | flops 2147483648 | bytes 6291456 | tf_op jit(solution)/shard_map/send_1/pallas_call | solution.py:242
  35.2 4.1 %send_0.1 = (s16[2064,256]{1,0:T(8,128)(2,1)S(1)}, s16[2064,256]{1,0:T(8,128)(2,1)S(1)}) custom-call(s32[2]{0:T(128)S(1)} %pad_add_fusion.me_ref.after_ref, bf16[1,512,8192]{2,1,0:T(8,128)(2,1)S(1)} %copy-done, bf16[1,512,1024]{2,1,0:T(8,128)(2,1)S(1)} %copy-done.1, s16[2064,256]{1,0:T(8,128)(2,1)S(1)} %get-tuple-element.21.after_ref, ...), custom_call_target="tpu_custom_call" | custom-call | flops 2147483648 | bytes 6291456 | tf_op jit(solution)/shard_map/send_0/pallas_call | solution.py:242
  39.4 1.4 %collective-permute-start.9 = (s16[2064,256]{1,0:T(8,128)(2,1)S(1)}, s16[2064,256]{1,0:T(8,128)(2,1)S(1)}, u32[]{:S(2)}, u32[]{:S(2)}) collective-permute-start(s16[2064,256]{1,0:T(8,128)(2,1)S(1)} %get-tuple-element.22.after_ref), channel_id=1, source_target_pairs={{0,24},{1,9},{2,26},{3,11},{4,28},{5,13},{6,30},{7,15},{8,16},{9,1... | collective-permute-start | bytes 3170312 | tf_op jit(solution)/shard_map/ppermute | solution.py:378
  40.8 2.5 %collective-permute-done.4.refs_2_ = bf16[512,1024]{1,0:T(8,128)(2,1)S(1)} collective-permute-done((bf16[512,1024]{1,0:T(8,128)(2,1)S(1)}, bf16[512,1024]{1,0:T(8,128)(2,1)S(1)}, u32[]{:S(2)}, u32[]{:S(2)}) %collective-permute-start.4) | collective-permute-done | bytes 1048608 | tf_op jit(solution)/shard_map/ppermute | solution.py:378
  43.3 5.1 %keep.1 = (f32[4096,256]{1,0:T(8,128)S(1)}, f32[4096,256]{1,0:T(8,128)S(1)}) custom-call(s32[2]{0:T(128)S(1)} %pad_add_fusion.me_ref.after_ref, bf16[1,512,8192]{2,1,0:T(8,128)(2,1)S(1)} %copy-done, bf16[1,512,1024]{2,1,0:T(8,128)(2,1)S(1)} %copy-done.1, s16[2064,256]{1,0:T(8,128)(2,1)S(1)} %get-tuple-element.22.after_ref, ...), custom_call_target="tpu_custom_call" | custom-call | flops 4294967296 | bytes 12582912 | tf_op jit(solution)/shard_map/keep/pallas_call | solution.py:253
  48.4 2.1 %collective-permute-done.10.refs_0_ = s16[2064,256]{1,0:T(8,128)(2,1)S(1)} collective-permute-done((s16[2064,256]{1,0:T(8,128)(2,1)S(1)}, s16[2064,256]{1,0:T(8,128)(2,1)S(1)}, u32[]{:S(2)}, u32[]{:S(2)}) %collective-permute-start.10) | collective-permute-done | bytes 1056800 | tf_op jit(solution)/shard_map/ppermute | solution.py:378
  50.5 0.5 late_3_1.1
  51.1 2.6 %collective-permute-start.12 = (s16[1040,256]{1,0:T(8,128)(2,1)S(1)}, s16[1040,256]{1,0:T(8,128)(2,1)S(1)}, u32[]{:S(2)}, u32[]{:S(2)}) collective-permute-start(s16[1040,256]{1,0:T(8,128)(2,1)S(1)} %late_3_1.1), channel_id=1, source_target_pairs={{0,32},{1,97},{2,34},{3,99},{4,36},{5,101},{6,38},{7,103},{8,40},{... | collective-permute-start | bytes 1597448 | tf_op jit(solution)/shard_map/ppermute | solution.py:378
  54.2 1.4 %collective-permute-start.14 = (s16[1040,256]{1,0:T(8,128)(2,1)S(1)}, s16[1040,256]{1,0:T(8,128)(2,1)S(1)}, u32[]{:S(2)}, u32[]{:S(2)}) collective-permute-start(s16[1040,256]{1,0:T(8,128)(2,1)S(1)} %late_3_0.1), channel_id=1, source_target_pairs={{0,24},{1,9},{2,26},{3,11},{4,28},{5,13},{6,30},{7,15},{8,16},{9,1... | collective-permute-start | bytes 1597448 | tf_op jit(solution)/shard_map/ppermute | solution.py:378
  55.6 0.5 late_2_1.1
  57.1 4.8 %collective-permute-done.9.refs_4_.refs_0_ = s16[2064,256]{1,0:T(8,128)(2,1)S(1)} collective-permute-done((s16[2064,256]{1,0:T(8,128)(2,1)S(1)}, s16[2064,256]{1,0:T(8,128)(2,1)S(1)}, u32[]{:S(2)}, u32[]{:S(2)}) %collective-permute-start.9) | collective-permute-done | bytes 1056800 | tf_op jit(solution)/shard_map/ppermute | solution.py:378
  61.9 1.4 %collective-permute-start.8 = (s16[1040,256]{1,0:T(8,128)(2,1)S(1)}, s16[1040,256]{1,0:T(8,128)(2,1)S(1)}, u32[]{:S(2)}, u32[]{:S(2)}) collective-permute-start(s16[1040,256]{1,0:T(8,128)(2,1)S(1)} %late_2_0.1), channel_id=1, source_target_pairs={{0,24},{1,9},{2,26},{3,11},{4,28},{5,13},{6,30},{7,15},{8,16},{9,1... | collective-permute-start | bytes 1597448 | tf_op jit(solution)/shard_map/ppermute | solution.py:378
  63.2 3.3 %collective-permute-done.12.refs_1_ = s16[1040,256]{1,0:T(8,128)(2,1)S(1)} collective-permute-done((s16[1040,256]{1,0:T(8,128)(2,1)S(1)}, s16[1040,256]{1,0:T(8,128)(2,1)S(1)}, u32[]{:S(2)}, u32[]{:S(2)}) %collective-permute-start.12) | collective-permute-done | bytes 532512 | tf_op jit(solution)/shard_map/ppermute | solution.py:378
  66.5 0.7 late_1_1.1
  67.4 3.4 %collective-permute-done.6.refs_1_.refs_0_ = s16[2064,256]{1,0:T(8,128)(2,1)S(1)} collective-permute-done((s16[2064,256]{1,0:T(8,128)(2,1)S(1)}, s16[2064,256]{1,0:T(8,128)(2,1)S(1)}, u32[]{:S(2)}, u32[]{:S(2)}) %collective-permute-start.6) | collective-permute-done | bytes 1056800 | tf_op jit(solution)/shard_map/ppermute | solution.py:378
  70.9 0.7 late_1_0.1
  71.6 0.6 collective-permute-start.15
  72.9 5.1 %collective-permute-done.11.refs_5_ = s16[1040,256]{1,0:T(8,128)(2,1)S(1)} collective-permute-done((s16[1040,256]{1,0:T(8,128)(2,1)S(1)}, s16[1040,256]{1,0:T(8,128)(2,1)S(1)}, u32[]{:S(2)}, u32[]{:S(2)}) %collective-permute-start.11) | collective-permute-done | bytes 532512 | tf_op jit(solution)/shard_map/ppermute | solution.py:378
  78.0 0.9 sum.1
  78.8 1.8 %collective-permute-done.13.refs_1_ = s16[1040,256]{1,0:T(8,128)(2,1)S(1)} collective-permute-done((s16[1040,256]{1,0:T(8,128)(2,1)S(1)}, s16[1040,256]{1,0:T(8,128)(2,1)S(1)}, u32[]{:S(2)}, u32[]{:S(2)}) %collective-permute-start.13) | collective-permute-done | bytes 532512 | tf_op jit(solution)/shard_map/ppermute | solution.py:378
  80.6 1.3 %finish_1.1 = (f32[12288,1024]{1,0:T(8,128)}, f32[8,128]{1,0:T(8,128)S(1)}) custom-call(f32[1024,256]{1,0:T(8,128)S(1)} %get-tuple-element.29.refs_0_, s16[1040,256]{1,0:T(8,128)(2,1)S(1)} %collective-permute-done.13.refs_1_), custom_call_target="tpu_custom_call" | custom-call | bytes 1572864 | tf_op jit(solution)/shard_map/finish_1/pallas_call | solution.py:290
  81.9 1.4 %finish_0.1 = (f32[12288,1024]{1,0:T(8,128)}, f32[128,1,128]{2,1,0:T(1,128)S(1)}) custom-call(f32[8,128]{1,0:T(8,128)S(1)} %get-tuple-element.30.refs_0_, s32[1,1]{1,0:T(1,128)S(6)} %copy.11.refs_1_, f32[12288,1024]{1,0:T(8,128)} %get-tuple-element.31.refs_2_, f32[1024,256]{1,0:T(8,128)S(1)} %get-tuple-element.32.refs_3_, ...), custom_call_target="tpu_custom_call", output_to_operand_aliasing={{0}: (2, {})} | custom-call | bytes 1572864 | tf_op jit(solution)/shard_map/finish_0/pallas_call | solution.py:290
  83.3 19.5 %all_to_all.5.reports = f32[128,1,128]{2,1,0:T(1,128)} all-to-all(f32[128,1,128]{2,1,0:T(1,128)S(1)} %get-tuple-element.33), channel_id=1, replica_groups=mesh['dp'=16,'pipe'=8] {'dp','pipe'}, dimensions={0} | all-to-all | bytes 131072 | tf_op jit(solution)/shard_map/all_to_all | solution.py:403
  102.8 6.9 %update.1 = (f32[1,512,1024]{2,1,0:T(8,128)}, f32[1,512,1024]{2,1,0:T(8,128)}, f32[1,512,1024]{2,1,0:T(8,128)}) custom-call(s32[1]{0:T(128)} %bitcast.pipe_ref, f32[128,1,128]{2,1,0:T(1,128)} %all_to_all.5.reports, f32[1,512,1024]{2,1,0:T(8,128)} %refs_0_.1, f32[1,512,1024]{2,1,0:T(8,128)} %refs_1_.2, f32[1,512,1024]{2,1,0:T(8,128)} %refs_2_.1, ...), custom_call_target="tpu_custom_call" | custom-call | bytes 6291456 | tf_op jit(solution)/shard_map/update/pallas_call | solution.py:360
  (20 shorter events, 2.5 us)
Async XLA Ops:
  0.6 16.0 %collective-permute-start.1 = (bf16[512,1024]{1,0:T(8,128)(2,1)}, bf16[512,1024]{1,0:T(8,128)(2,1)S(1)}, u32[]{:S(2)}, u32[]{:S(2)}) collective-permute-start(bf16[512,1024]{1,0:T(8,128)(2,1)} %bitcast.4), channel_id=1, source_target_pairs={{0,8},{1,25},{2,10},{3,27},{4,12},{5,29},{6,14},{7,31},{8,0},{9,17... | collective-permute-start | bytes 3145736 | tf_op jit(solution)/shard_map/ppermute | solution.py:378
  4.3 15.1 %collective-permute-start = (bf16[512,1024]{1,0:T(8,128)(2,1)}, bf16[512,1024]{1,0:T(8,128)(2,1)S(1)}, u32[]{:S(2)}, u32[]{:S(2)}) collective-permute-start(bf16[512,1024]{1,0:T(8,128)(2,1)} %bitcast.5), channel_id=1, source_target_pairs={{0,32},{1,97},{2,34},{3,99},{4,36},{5,101},{6,38},{7,103},{8,40},{... | collective-permute-start | bytes 3145736 | tf_op jit(solution)/shard_map/ppermute | solution.py:378
  6.8 3.4 %copy-start = (bf16[1,512,8192]{2,1,0:T(8,128)(2,1)S(1)}, bf16[1,512,8192]{2,1,0:T(8,128)(2,1)}, u32[]{:S(2)}) copy-start(bf16[1,512,8192]{2,1,0:T(8,128)(2,1)} %x_ref.7) | copy-start | bytes 25165828
  10.2 20.4 %copy-start.1 = (bf16[1,512,1024]{2,1,0:T(8,128)(2,1)S(1)}, bf16[1,512,1024]{2,1,0:T(8,128)(2,1)}, u32[]{:S(2)}) copy-start(bf16[1,512,1024]{2,1,0:T(8,128)(2,1)} %g_ref.5) | copy-start | bytes 3145732
  11.4 19.2 %collective-permute-start.2 = (bf16[512,1024]{1,0:T(8,128)(2,1)S(1)}, bf16[512,1024]{1,0:T(8,128)(2,1)S(1)}, u32[]{:S(2)}, u32[]{:S(2)}) collective-permute-start(bf16[512,1024]{1,0:T(8,128)(2,1)S(1)} %get-tuple-element.19), channel_id=1, source_target_pairs={{0,32},{1,97},{2,34},{3,99},{4,36},{5,101},{6,38},{7,103},{8,40},{... | collective-permute-start | bytes 3145736 | tf_op jit(solution)/shard_map/ppermute | solution.py:378
  11.7 18.9 %collective-permute-start.3 = (bf16[512,1024]{1,0:T(8,128)(2,1)S(1)}, bf16[512,1024]{1,0:T(8,128)(2,1)S(1)}, u32[]{:S(2)}, u32[]{:S(2)}) collective-permute-start(bf16[512,1024]{1,0:T(8,128)(2,1)S(1)} %get-tuple-element.20), channel_id=1, source_target_pairs={{0,8},{1,25},{2,10},{3,27},{4,12},{5,29},{6,14},{7,31},{8,0},{9,17... | collective-permute-start | bytes 3145736 | tf_op jit(solution)/shard_map/ppermute | solution.py:378
  11.7 31.6 %collective-permute-start.4 = (bf16[512,1024]{1,0:T(8,128)(2,1)S(1)}, bf16[512,1024]{1,0:T(8,128)(2,1)S(1)}, u32[]{:S(2)}, u32[]{:S(2)}) collective-permute-start(bf16[512,1024]{1,0:T(8,128)(2,1)S(1)} %get-tuple-element.23), channel_id=1, source_target_pairs={{0,32},{1,97},{2,34},{3,99},{4,36},{5,101},{6,38},{7,103},{8,40},{... | collective-permute-start | bytes 3145736 | tf_op jit(solution)/shard_map/ppermute | solution.py:378
  16.7 26.7 %collective-permute-start.5 = (bf16[512,1024]{1,0:T(8,128)(2,1)S(1)}, bf16[512,1024]{1,0:T(8,128)(2,1)S(1)}, u32[]{:S(2)}, u32[]{:S(2)}) collective-permute-start(bf16[512,1024]{1,0:T(8,128)(2,1)S(1)} %get-tuple-element.24), channel_id=1, source_target_pairs={{0,8},{1,25},{2,10},{3,27},{4,12},{5,29},{6,14},{7,31},{8,0},{9,17... | collective-permute-start | bytes 3145736 | tf_op jit(solution)/shard_map/ppermute | solution.py:378
  34.7 15.8 %collective-permute-start.10 = (s16[2064,256]{1,0:T(8,128)(2,1)S(1)}, s16[2064,256]{1,0:T(8,128)(2,1)S(1)}, u32[]{:S(2)}, u32[]{:S(2)}) collective-permute-start(s16[2064,256]{1,0:T(8,128)(2,1)S(1)} %get-tuple-element.21.after_ref), channel_id=1, source_target_pairs={{0,24},{1,9},{2,26},{3,11},{4,28},{5,13},{6,30},{7,15},{8,16},{9,1... | collective-permute-start | bytes 3170312 | tf_op jit(solution)/shard_map/ppermute | solution.py:378
  34.8 18.9 %collective-permute-start.7 = (s16[2064,256]{1,0:T(8,128)(2,1)S(1)}, s16[2064,256]{1,0:T(8,128)(2,1)S(1)}, u32[]{:S(2)}, u32[]{:S(2)}) collective-permute-start(s16[2064,256]{1,0:T(8,128)(2,1)S(1)} %get-tuple-element.27), channel_id=1, source_target_pairs={{0,96},{1,33},{2,98},{3,35},{4,100},{5,37},{6,102},{7,39},{8,104},... | collective-permute-start | bytes 3170312 | tf_op jit(solution)/shard_map/ppermute | solution.py:378
  39.4 22.5 %collective-permute-start.9 = (s16[2064,256]{1,0:T(8,128)(2,1)S(1)}, s16[2064,256]{1,0:T(8,128)(2,1)S(1)}, u32[]{:S(2)}, u32[]{:S(2)}) collective-permute-start(s16[2064,256]{1,0:T(8,128)(2,1)S(1)} %get-tuple-element.22.after_ref), channel_id=1, source_target_pairs={{0,24},{1,9},{2,26},{3,11},{4,28},{5,13},{6,30},{7,15},{8,16},{9,1... | collective-permute-start | bytes 3170312 | tf_op jit(solution)/shard_map/ppermute | solution.py:378
  43.3 27.5 %collective-permute-start.6 = (s16[2064,256]{1,0:T(8,128)(2,1)S(1)}, s16[2064,256]{1,0:T(8,128)(2,1)S(1)}, u32[]{:S(2)}, u32[]{:S(2)}) collective-permute-start(s16[2064,256]{1,0:T(8,128)(2,1)S(1)} %get-tuple-element.26), channel_id=1, source_target_pairs={{0,96},{1,33},{2,98},{3,35},{4,100},{5,37},{6,102},{7,39},{8,104},... | collective-permute-start | bytes 3170312 | tf_op jit(solution)/shard_map/ppermute | solution.py:378
  51.1 15.5 %collective-permute-start.12 = (s16[1040,256]{1,0:T(8,128)(2,1)S(1)}, s16[1040,256]{1,0:T(8,128)(2,1)S(1)}, u32[]{:S(2)}, u32[]{:S(2)}) collective-permute-start(s16[1040,256]{1,0:T(8,128)(2,1)S(1)} %late_3_1.1), channel_id=1, source_target_pairs={{0,32},{1,97},{2,34},{3,99},{4,36},{5,101},{6,38},{7,103},{8,40},{... | collective-permute-start | bytes 1597448 | tf_op jit(solution)/shard_map/ppermute | solution.py:378
  54.2 16.6 %collective-permute-start.14 = (s16[1040,256]{1,0:T(8,128)(2,1)S(1)}, s16[1040,256]{1,0:T(8,128)(2,1)S(1)}, u32[]{:S(2)}, u32[]{:S(2)}) collective-permute-start(s16[1040,256]{1,0:T(8,128)(2,1)S(1)} %late_3_0.1), channel_id=1, source_target_pairs={{0,24},{1,9},{2,26},{3,11},{4,28},{5,13},{6,30},{7,15},{8,16},{9,1... | collective-permute-start | bytes 1597448 | tf_op jit(solution)/shard_map/ppermute | solution.py:378
  56.1 21.8 %collective-permute-start.11 = (s16[1040,256]{1,0:T(8,128)(2,1)S(1)}, s16[1040,256]{1,0:T(8,128)(2,1)S(1)}, u32[]{:S(2)}, u32[]{:S(2)}) collective-permute-start(s16[1040,256]{1,0:T(8,128)(2,1)S(1)} %late_2_1.1), channel_id=1, source_target_pairs={{0,32},{1,97},{2,34},{3,99},{4,36},{5,101},{6,38},{7,103},{8,40},{... | collective-permute-start | bytes 1597448 | tf_op jit(solution)/shard_map/ppermute | solution.py:378
  61.9 16.1 %collective-permute-start.8 = (s16[1040,256]{1,0:T(8,128)(2,1)S(1)}, s16[1040,256]{1,0:T(8,128)(2,1)S(1)}, u32[]{:S(2)}, u32[]{:S(2)}) collective-permute-start(s16[1040,256]{1,0:T(8,128)(2,1)S(1)} %late_2_0.1), channel_id=1, source_target_pairs={{0,24},{1,9},{2,26},{3,11},{4,28},{5,13},{6,30},{7,15},{8,16},{9,1... | collective-permute-start | bytes 1597448 | tf_op jit(solution)/shard_map/ppermute | solution.py:378
  67.3 13.4 %collective-permute-start.13 = (s16[1040,256]{1,0:T(8,128)(2,1)S(1)}, s16[1040,256]{1,0:T(8,128)(2,1)S(1)}, u32[]{:S(2)}, u32[]{:S(2)}) collective-permute-start(s16[1040,256]{1,0:T(8,128)(2,1)S(1)} %late_1_1.1), channel_id=1, source_target_pairs={{0,96},{1,33},{2,98},{3,35},{4,100},{5,37},{6,102},{7,39},{8,104},... | collective-permute-start | bytes 1597448 | tf_op jit(solution)/shard_map/ppermute | solution.py:378
  71.6 10.3 %collective-permute-start.15 = (s16[1040,256]{1,0:T(8,128)(2,1)S(1)}, s16[1040,256]{1,0:T(8,128)(2,1)S(1)}, u32[]{:S(2)}, u32[]{:S(2)}) collective-permute-start(s16[1040,256]{1,0:T(8,128)(2,1)S(1)} %late_1_0.1), channel_id=1, source_target_pairs={{0,8},{1,25},{2,10},{3,27},{4,12},{5,29},{6,14},{7,31},{8,0},{9,17... | collective-permute-start | bytes 1597448 | tf_op jit(solution)/shard_map/ppermute | solution.py:378

commit v7 on v6

--- a/solution.py
+++ b/solution.py
@@ -167,23 +167,26 @@
     p_ref, r = refs[-7:-5]
     acc = refs[0][...] if last else jnp.zeros((8, 128), jnp.float32)
     [scale] = scales_of([r])
+    copies = []
     for group in range(GROUPS):
         at = slice(group * ROWS, (group + 1) * ROWS)
         total = p_ref[at, :] + decode(r[at, :], scale)
-        grad_ref[:, group * COLS : (group + 1) * COLS] = total
+        cols = slice(group * COLS, (group + 1) * COLS)
+        grad_ref[:, cols] = total
+        there = grad_hbm.at[pl.ds(v * ROWS, ROWS), cols]
+        copies.append(pltpu.make_async_copy(grad_ref.at[:, cols], there, sems.at[group]))
+        copies[-1].start()
         squared = total * total
         squared = squared[:, :128] + squared[:, 128:]
         acc = acc + jnp.sum(squared.reshape(ROWS // 8, 8, 128), axis=0)
-    copies = [pltpu.make_async_copy(grad_ref, grad_hbm.at[pl.ds(v * ROWS, ROWS)], sems.at[0])]
-    copies[0].start()
     if last:
         marked = jnp.where(refs[1][0, 0] != 0, 1.0, 0.0)
         acc = acc + pltpu.roll(acc, 64, axis=1)
         lane = lax.broadcasted_iota(jnp.int32, (8, 128), 1)
         acc = jnp.where(lane < 64, jnp.sum(acc, axis=0, keepdims=True), marked)
         sum_ref[...] = jnp.broadcast_to(acc[:1][None], (DEVICES, 1, 128))
-        copies.append(pltpu.make_async_copy(sum_ref, sum_out, sems.at[1]))
-        copies[1].start()
+        copies.append(pltpu.make_async_copy(sum_ref, sum_out, sems.at[GROUPS]))
+        copies[-1].start()
     else:
         sum_out[...] = acc
     for copy in copies:
@@ -295,7 +298,7 @@
         [
             pltpu.VMEM((ROWS, KV), jnp.float32),
             pltpu.VMEM(sums.shape, sums.dtype),
-            pltpu.SemaphoreType.DMA((2,)),
+            pltpu.SemaphoreType.DMA((GROUPS + 1,)),
         ],
         cost(1, 0, 1),
         [FAR, FAR if last else WHOLE],

time: 110 us -> 110 us (level)
  no operation moved by 1% of the time
where the time goes in v7:
time: 110 us
  waiting for transfers between devices  36.8 us (33%)
  Pallas kernels  28.1 us (26%)
  starting transfers between devices  20.2 us (18%)
  blocking collectives  19.7 us (18%)
  local copies, waits for them, and re-layouts  3.38 us (3%)
  between operations  1.57 us (1%)
    ppermute x16, waiting for transfers between devices, swap(): return lax.ppermute(value, ('dp', 'pipe'), pairs)  36.8 us
    ppermute x16, starting transfers between devices, swap(): return lax.ppermute(value, ('dp', 'pipe'), pairs)  20.2 us
    all_to_all x1, blocking collectives, per_device(): reports = lax.all_to_all(report, ('dp', 'pipe'), 0, 0)  19.7 us
    pallas_call x2, Pallas kernels, send(): kernel_call(functools.partial(send_kernel, half), f'send_{half}', [SCALAR...  8.27 us
    pallas_call x1, Pallas kernels, update(): kernel_call(functools.partial(update_kernel, bound), 'update', [SCALAR, W...  6.86 us
    pallas_call x1, Pallas kernels, keep(): kernel_call(keep_kernel, 'keep', [SCALAR, WHOLE, WHOLE, LEFT] + [WHOLE] *...  5.07 us
    pallas_call x6, Pallas kernels, late(): kernel_call(functools.partial(late_kernel, block, begins), f'late_{block}...  3.48 us
    unnamed x4, local copies, waits for them, and re-layouts  3.38 us
  transfers between devices with their start and end apart: 16, of which 9 were waited for; matrix products, arithmetic and copies ran while one was open for 0% of the time, Pallas kernels for 18%

profile of v7, /device:TPU:1, one launch (start us, length us, event | category | flops | bytes accessed | tf_op | source)
XLA Modules:
  0.0 109.8 jit_solution(17549696042728019287)
XLA Ops:
  0.6 3.6 %collective-permute-start.1 = (bf16[512,1024]{1,0:T(8,128)(2,1)}, bf16[512,1024]{1,0:T(8,128)(2,1)S(1)}, u32[]{:S(2)}, u32[]{:S(2)}) collective-permute-start(bf16[512,1024]{1,0:T(8,128)(2,1)} %bitcast.4), channel_id=1, source_target_pairs={{0,8},{1,25},{2,10},{3,27},{4,12},{5,29},{6,14},{7,31},{8,0},{9,17... | collective-permute-start | bytes 3145736 | tf_op jit(solution)/shard_map/ppermute | solution.py:381
  4.3 2.5 %collective-permute-start = (bf16[512,1024]{1,0:T(8,128)(2,1)}, bf16[512,1024]{1,0:T(8,128)(2,1)S(1)}, u32[]{:S(2)}, u32[]{:S(2)}) collective-permute-start(bf16[512,1024]{1,0:T(8,128)(2,1)} %bitcast.5), channel_id=1, source_target_pairs={{0,32},{1,97},{2,34},{3,99},{4,36},{5,101},{6,38},{7,103},{8,40},{... | collective-permute-start | bytes 3145736 | tf_op jit(solution)/shard_map/ppermute | solution.py:381
  6.8 3.4 %copy-done = bf16[1,512,8192]{2,1,0:T(8,128)(2,1)S(1)} copy-done((bf16[1,512,8192]{2,1,0:T(8,128)(2,1)S(1)}, bf16[1,512,8192]{2,1,0:T(8,128)(2,1)}, u32[]{:S(2)}) %copy-start) | copy-done | bytes 8388632
  10.2 1.2 %gather.1 = (bf16[512,1024]{1,0:T(8,128)(2,1)S(1)}, bf16[512,1024]{1,0:T(8,128)(2,1)S(1)}, bf16[512,1024]{1,0:T(8,128)(2,1)S(1)}, bf16[512,1024]{1,0:T(8,128)(2,1)S(1)}) custom-call(s32[2]{0:T(128)S(1)} %pad_add_fusion.me_ref.after_ref, bf16[1,512,8192]{2,1,0:T(8,128)(2,1)S(1)} %copy-done), custom_call_target="tpu_custom_call" | custom-call | bytes 12582912 | tf_op jit(solution)/shard_map/gather/pallas_call | solution.py:234
  11.7 2.5 %collective-permute-start.4 = (bf16[512,1024]{1,0:T(8,128)(2,1)S(1)}, bf16[512,1024]{1,0:T(8,128)(2,1)S(1)}, u32[]{:S(2)}, u32[]{:S(2)}) collective-permute-start(bf16[512,1024]{1,0:T(8,128)(2,1)S(1)} %get-tuple-element.23), channel_id=1, source_target_pairs={{0,32},{1,97},{2,34},{3,99},{4,36},{5,101},{6,38},{7,103},{8,40},{... | collective-permute-start | bytes 3145736 | tf_op jit(solution)/shard_map/ppermute | solution.py:381
  14.2 2.5 %collective-permute-done.1.refs_1_ = bf16[512,1024]{1,0:T(8,128)(2,1)S(1)} collective-permute-done((bf16[512,1024]{1,0:T(8,128)(2,1)}, bf16[512,1024]{1,0:T(8,128)(2,1)S(1)}, u32[]{:S(2)}, u32[]{:S(2)}) %collective-permute-start.1) | collective-permute-done | bytes 1048608 | tf_op jit(solution)/shard_map/ppermute | solution.py:381
  16.7 2.7 %collective-permute-start.5 = (bf16[512,1024]{1,0:T(8,128)(2,1)S(1)}, bf16[512,1024]{1,0:T(8,128)(2,1)S(1)}, u32[]{:S(2)}, u32[]{:S(2)}) collective-permute-start(bf16[512,1024]{1,0:T(8,128)(2,1)S(1)} %get-tuple-element.24), channel_id=1, source_target_pairs={{0,8},{1,25},{2,10},{3,27},{4,12},{5,29},{6,14},{7,31},{8,0},{9,17... | collective-permute-start | bytes 3145736 | tf_op jit(solution)/shard_map/ppermute | solution.py:381
  19.3 11.2 %collective-permute-done.2.refs_2_ = bf16[512,1024]{1,0:T(8,128)(2,1)S(1)} collective-permute-done((bf16[512,1024]{1,0:T(8,128)(2,1)S(1)}, bf16[512,1024]{1,0:T(8,128)(2,1)S(1)}, u32[]{:S(2)}, u32[]{:S(2)}) %collective-permute-start.2) | collective-permute-done | bytes 1048608 | tf_op jit(solution)/shard_map/ppermute | solution.py:381
  30.6 4.1 %send_1.1 = (s16[2064,256]{1,0:T(8,128)(2,1)S(1)}, s16[2064,256]{1,0:T(8,128)(2,1)S(1)}) custom-call(s32[2]{0:T(128)S(1)} %pad_add_fusion.me_ref.after_ref, bf16[1,512,8192]{2,1,0:T(8,128)(2,1)S(1)} %copy-done, bf16[1,512,1024]{2,1,0:T(8,128)(2,1)S(1)} %copy-done.1, s32[2]{0:T(128)S(1)} %pad_add_fusion.me_ref.after_ref, ...), custom_call_target="tpu_custom_call" | custom-call | flops 2147483648 | bytes 6291456 | tf_op jit(solution)/shard_map/send_1/pallas_call | solution.py:245
  35.2 4.1 %send_0.1 = (s16[2064,256]{1,0:T(8,128)(2,1)S(1)}, s16[2064,256]{1,0:T(8,128)(2,1)S(1)}) custom-call(s32[2]{0:T(128)S(1)} %pad_add_fusion.me_ref.after_ref, bf16[1,512,8192]{2,1,0:T(8,128)(2,1)S(1)} %copy-done, bf16[1,512,1024]{2,1,0:T(8,128)(2,1)S(1)} %copy-done.1, s16[2064,256]{1,0:T(8,128)(2,1)S(1)} %get-tuple-element.21.after_ref, ...), custom_call_target="tpu_custom_call" | custom-call | flops 2147483648 | bytes 6291456 | tf_op jit(solution)/shard_map/send_0/pallas_call | solution.py:245
  39.4 1.4 %collective-permute-start.9 = (s16[2064,256]{1,0:T(8,128)(2,1)S(1)}, s16[2064,256]{1,0:T(8,128)(2,1)S(1)}, u32[]{:S(2)}, u32[]{:S(2)}) collective-permute-start(s16[2064,256]{1,0:T(8,128)(2,1)S(1)} %get-tuple-element.22.after_ref), channel_id=1, source_target_pairs={{0,24},{1,9},{2,26},{3,11},{4,28},{5,13},{6,30},{7,15},{8,16},{9,1... | collective-permute-start | bytes 3170312 | tf_op jit(solution)/shard_map/ppermute | solution.py:381
  40.8 2.5 %collective-permute-done.4.refs_2_ = bf16[512,1024]{1,0:T(8,128)(2,1)S(1)} collective-permute-done((bf16[512,1024]{1,0:T(8,128)(2,1)S(1)}, bf16[512,1024]{1,0:T(8,128)(2,1)S(1)}, u32[]{:S(2)}, u32[]{:S(2)}) %collective-permute-start.4) | collective-permute-done | bytes 1048608 | tf_op jit(solution)/shard_map/ppermute | solution.py:381
  43.3 5.1 %keep.1 = (f32[4096,256]{1,0:T(8,128)S(1)}, f32[4096,256]{1,0:T(8,128)S(1)}) custom-call(s32[2]{0:T(128)S(1)} %pad_add_fusion.me_ref.after_ref, bf16[1,512,8192]{2,1,0:T(8,128)(2,1)S(1)} %copy-done, bf16[1,512,1024]{2,1,0:T(8,128)(2,1)S(1)} %copy-done.1, s16[2064,256]{1,0:T(8,128)(2,1)S(1)} %get-tuple-element.22.after_ref, ...), custom_call_target="tpu_custom_call" | custom-call | flops 4294967296 | bytes 12582912 | tf_op jit(solution)/shard_map/keep/pallas_call | solution.py:256
  48.4 2.1 %collective-permute-done.10.refs_0_ = s16[2064,256]{1,0:T(8,128)(2,1)S(1)} collective-permute-done((s16[2064,256]{1,0:T(8,128)(2,1)S(1)}, s16[2064,256]{1,0:T(8,128)(2,1)S(1)}, u32[]{:S(2)}, u32[]{:S(2)}) %collective-permute-start.10) | collective-permute-done | bytes 1056800 | tf_op jit(solution)/shard_map/ppermute | solution.py:381
  50.5 0.5 late_3_1.1
  51.1 2.6 %collective-permute-start.12 = (s16[1040,256]{1,0:T(8,128)(2,1)S(1)}, s16[1040,256]{1,0:T(8,128)(2,1)S(1)}, u32[]{:S(2)}, u32[]{:S(2)}) collective-permute-start(s16[1040,256]{1,0:T(8,128)(2,1)S(1)} %late_3_1.1), channel_id=1, source_target_pairs={{0,32},{1,97},{2,34},{3,99},{4,36},{5,101},{6,38},{7,103},{8,40},{... | collective-permute-start | bytes 1597448 | tf_op jit(solution)/shard_map/ppermute | solution.py:381
  54.2 1.4 %collective-permute-start.14 = (s16[1040,256]{1,0:T(8,128)(2,1)S(1)}, s16[1040,256]{1,0:T(8,128)(2,1)S(1)}, u32[]{:S(2)}, u32[]{:S(2)}) collective-permute-start(s16[1040,256]{1,0:T(8,128)(2,1)S(1)} %late_3_0.1), channel_id=1, source_target_pairs={{0,24},{1,9},{2,26},{3,11},{4,28},{5,13},{6,30},{7,15},{8,16},{9,1... | collective-permute-start | bytes 1597448 | tf_op jit(solution)/shard_map/ppermute | solution.py:381
  55.6 0.5 late_2_1.1
  57.1 4.8 %collective-permute-done.9.refs_4_.refs_0_ = s16[2064,256]{1,0:T(8,128)(2,1)S(1)} collective-permute-done((s16[2064,256]{1,0:T(8,128)(2,1)S(1)}, s16[2064,256]{1,0:T(8,128)(2,1)S(1)}, u32[]{:S(2)}, u32[]{:S(2)}) %collective-permute-start.9) | collective-permute-done | bytes 1056800 | tf_op jit(solution)/shard_map/ppermute | solution.py:381
  61.9 1.4 %collective-permute-start.8 = (s16[1040,256]{1,0:T(8,128)(2,1)S(1)}, s16[1040,256]{1,0:T(8,128)(2,1)S(1)}, u32[]{:S(2)}, u32[]{:S(2)}) collective-permute-start(s16[1040,256]{1,0:T(8,128)(2,1)S(1)} %late_2_0.1), channel_id=1, source_target_pairs={{0,24},{1,9},{2,26},{3,11},{4,28},{5,13},{6,30},{7,15},{8,16},{9,1... | collective-permute-start | bytes 1597448 | tf_op jit(solution)/shard_map/ppermute | solution.py:381
  63.2 3.3 %collective-permute-done.12.refs_1_ = s16[1040,256]{1,0:T(8,128)(2,1)S(1)} collective-permute-done((s16[1040,256]{1,0:T(8,128)(2,1)S(1)}, s16[1040,256]{1,0:T(8,128)(2,1)S(1)}, u32[]{:S(2)}, u32[]{:S(2)}) %collective-permute-start.12) | collective-permute-done | bytes 532512 | tf_op jit(solution)/shard_map/ppermute | solution.py:381
  66.5 0.7 late_1_1.1
  67.4 3.4 %collective-permute-done.6.refs_1_.refs_0_ = s16[2064,256]{1,0:T(8,128)(2,1)S(1)} collective-permute-done((s16[2064,256]{1,0:T(8,128)(2,1)S(1)}, s16[2064,256]{1,0:T(8,128)(2,1)S(1)}, u32[]{:S(2)}, u32[]{:S(2)}) %collective-permute-start.6) | collective-permute-done | bytes 1056800 | tf_op jit(solution)/shard_map/ppermute | solution.py:381
  70.9 0.7 late_1_0.1
  71.6 0.6 collective-permute-start.15
  72.9 5.1 %collective-permute-done.11.refs_5_ = s16[1040,256]{1,0:T(8,128)(2,1)S(1)} collective-permute-done((s16[1040,256]{1,0:T(8,128)(2,1)S(1)}, s16[1040,256]{1,0:T(8,128)(2,1)S(1)}, u32[]{:S(2)}, u32[]{:S(2)}) %collective-permute-start.11) | collective-permute-done | bytes 532512 | tf_op jit(solution)/shard_map/ppermute | solution.py:381
  78.0 0.9 sum.1
  78.8 1.8 %collective-permute-done.13.refs_1_ = s16[1040,256]{1,0:T(8,128)(2,1)S(1)} collective-permute-done((s16[1040,256]{1,0:T(8,128)(2,1)S(1)}, s16[1040,256]{1,0:T(8,128)(2,1)S(1)}, u32[]{:S(2)}, u32[]{:S(2)}) %collective-permute-start.13) | collective-permute-done | bytes 532512 | tf_op jit(solution)/shard_map/ppermute | solution.py:381
  80.6 1.1 %finish_1.1 = (f32[12288,1024]{1,0:T(8,128)}, f32[8,128]{1,0:T(8,128)S(1)}) custom-call(f32[1024,256]{1,0:T(8,128)S(1)} %get-tuple-element.29.refs_0_, s16[1040,256]{1,0:T(8,128)(2,1)S(1)} %collective-permute-done.13.refs_1_), custom_call_target="tpu_custom_call" | custom-call | bytes 1572864 | tf_op jit(solution)/shard_map/finish_1/pallas_call | solution.py:293
  81.8 1.3 %finish_0.1 = (f32[12288,1024]{1,0:T(8,128)}, f32[128,1,128]{2,1,0:T(1,128)S(1)}) custom-call(f32[8,128]{1,0:T(8,128)S(1)} %get-tuple-element.30.refs_0_, s32[1,1]{1,0:T(1,128)S(6)} %copy.11.refs_1_, f32[12288,1024]{1,0:T(8,128)} %get-tuple-element.31.refs_2_, f32[1024,256]{1,0:T(8,128)S(1)} %get-tuple-element.32.refs_3_, ...), custom_call_target="tpu_custom_call", output_to_operand_aliasing={{0}: (2, {})} | custom-call | bytes 1572864 | tf_op jit(solution)/shard_map/finish_0/pallas_call | solution.py:293
  83.1 19.7 %all_to_all.5.reports = f32[128,1,128]{2,1,0:T(1,128)} all-to-all(f32[128,1,128]{2,1,0:T(1,128)S(1)} %get-tuple-element.33), channel_id=1, replica_groups=mesh['dp'=16,'pipe'=8] {'dp','pipe'}, dimensions={0} | all-to-all | bytes 131072 | tf_op jit(solution)/shard_map/all_to_all | solution.py:406
  102.8 6.9 %update.1 = (f32[1,512,1024]{2,1,0:T(8,128)}, f32[1,512,1024]{2,1,0:T(8,128)}, f32[1,512,1024]{2,1,0:T(8,128)}) custom-call(s32[1]{0:T(128)} %bitcast.pipe_ref, f32[128,1,128]{2,1,0:T(1,128)} %all_to_all.5.reports, f32[1,512,1024]{2,1,0:T(8,128)} %refs_0_.1, f32[1,512,1024]{2,1,0:T(8,128)} %refs_1_.2, f32[1,512,1024]{2,1,0:T(8,128)} %refs_2_.1, ...), custom_call_target="tpu_custom_call" | custom-call | bytes 6291456 | tf_op jit(solution)/shard_map/update/pallas_call | solution.py:363
  (20 shorter events, 2.5 us)
Async XLA Ops:
  0.6 16.0 %collective-permute-start.1 = (bf16[512,1024]{1,0:T(8,128)(2,1)}, bf16[512,1024]{1,0:T(8,128)(2,1)S(1)}, u32[]{:S(2)}, u32[]{:S(2)}) collective-permute-start(bf16[512,1024]{1,0:T(8,128)(2,1)} %bitcast.4), channel_id=1, source_target_pairs={{0,8},{1,25},{2,10},{3,27},{4,12},{5,29},{6,14},{7,31},{8,0},{9,17... | collective-permute-start | bytes 3145736 | tf_op jit(solution)/shard_map/ppermute | solution.py:381
  4.3 15.1 %collective-permute-start = (bf16[512,1024]{1,0:T(8,128)(2,1)}, bf16[512,1024]{1,0:T(8,128)(2,1)S(1)}, u32[]{:S(2)}, u32[]{:S(2)}) collective-permute-start(bf16[512,1024]{1,0:T(8,128)(2,1)} %bitcast.5), channel_id=1, source_target_pairs={{0,32},{1,97},{2,34},{3,99},{4,36},{5,101},{6,38},{7,103},{8,40},{... | collective-permute-start | bytes 3145736 | tf_op jit(solution)/shard_map/ppermute | solution.py:381
  6.8 3.4 %copy-start = (bf16[1,512,8192]{2,1,0:T(8,128)(2,1)S(1)}, bf16[1,512,8192]{2,1,0:T(8,128)(2,1)}, u32[]{:S(2)}) copy-start(bf16[1,512,8192]{2,1,0:T(8,128)(2,1)} %x_ref.7) | copy-start | bytes 25165828
  10.2 20.4 %copy-start.1 = (bf16[1,512,1024]{2,1,0:T(8,128)(2,1)S(1)}, bf16[1,512,1024]{2,1,0:T(8,128)(2,1)}, u32[]{:S(2)}) copy-start(bf16[1,512,1024]{2,1,0:T(8,128)(2,1)} %g_ref.5) | copy-start | bytes 3145732
  11.4 19.2 %collective-permute-start.2 = (bf16[512,1024]{1,0:T(8,128)(2,1)S(1)}, bf16[512,1024]{1,0:T(8,128)(2,1)S(1)}, u32[]{:S(2)}, u32[]{:S(2)}) collective-permute-start(bf16[512,1024]{1,0:T(8,128)(2,1)S(1)} %get-tuple-element.19), channel_id=1, source_target_pairs={{0,32},{1,97},{2,34},{3,99},{4,36},{5,101},{6,38},{7,103},{8,40},{... | collective-permute-start | bytes 3145736 | tf_op jit(solution)/shard_map/ppermute | solution.py:381
  11.7 18.9 %collective-permute-start.3 = (bf16[512,1024]{1,0:T(8,128)(2,1)S(1)}, bf16[512,1024]{1,0:T(8,128)(2,1)S(1)}, u32[]{:S(2)}, u32[]{:S(2)}) collective-permute-start(bf16[512,1024]{1,0:T(8,128)(2,1)S(1)} %get-tuple-element.20), channel_id=1, source_target_pairs={{0,8},{1,25},{2,10},{3,27},{4,12},{5,29},{6,14},{7,31},{8,0},{9,17... | collective-permute-start | bytes 3145736 | tf_op jit(solution)/shard_map/ppermute | solution.py:381
  11.7 31.6 %collective-permute-start.4 = (bf16[512,1024]{1,0:T(8,128)(2,1)S(1)}, bf16[512,1024]{1,0:T(8,128)(2,1)S(1)}, u32[]{:S(2)}, u32[]{:S(2)}) collective-permute-start(bf16[512,1024]{1,0:T(8,128)(2,1)S(1)} %get-tuple-element.23), channel_id=1, source_target_pairs={{0,32},{1,97},{2,34},{3,99},{4,36},{5,101},{6,38},{7,103},{8,40},{... | collective-permute-start | bytes 3145736 | tf_op jit(solution)/shard_map/ppermute | solution.py:381
  16.7 26.7 %collective-permute-start.5 = (bf16[512,1024]{1,0:T(8,128)(2,1)S(1)}, bf16[512,1024]{1,0:T(8,128)(2,1)S(1)}, u32[]{:S(2)}, u32[]{:S(2)}) collective-permute-start(bf16[512,1024]{1,0:T(8,128)(2,1)S(1)} %get-tuple-element.24), channel_id=1, source_target_pairs={{0,8},{1,25},{2,10},{3,27},{4,12},{5,29},{6,14},{7,31},{8,0},{9,17... | collective-permute-start | bytes 3145736 | tf_op jit(solution)/shard_map/ppermute | solution.py:381
  34.7 15.8 %collective-permute-start.10 = (s16[2064,256]{1,0:T(8,128)(2,1)S(1)}, s16[2064,256]{1,0:T(8,128)(2,1)S(1)}, u32[]{:S(2)}, u32[]{:S(2)}) collective-permute-start(s16[2064,256]{1,0:T(8,128)(2,1)S(1)} %get-tuple-element.21.after_ref), channel_id=1, source_target_pairs={{0,24},{1,9},{2,26},{3,11},{4,28},{5,13},{6,30},{7,15},{8,16},{9,1... | collective-permute-start | bytes 3170312 | tf_op jit(solution)/shard_map/ppermute | solution.py:381
  34.8 18.9 %collective-permute-start.7 = (s16[2064,256]{1,0:T(8,128)(2,1)S(1)}, s16[2064,256]{1,0:T(8,128)(2,1)S(1)}, u32[]{:S(2)}, u32[]{:S(2)}) collective-permute-start(s16[2064,256]{1,0:T(8,128)(2,1)S(1)} %get-tuple-element.27), channel_id=1, source_target_pairs={{0,96},{1,33},{2,98},{3,35},{4,100},{5,37},{6,102},{7,39},{8,104},... | collective-permute-start | bytes 3170312 | tf_op jit(solution)/shard_map/ppermute | solution.py:381
  39.4 22.5 %collective-permute-start.9 = (s16[2064,256]{1,0:T(8,128)(2,1)S(1)}, s16[2064,256]{1,0:T(8,128)(2,1)S(1)}, u32[]{:S(2)}, u32[]{:S(2)}) collective-permute-start(s16[2064,256]{1,0:T(8,128)(2,1)S(1)} %get-tuple-element.22.after_ref), channel_id=1, source_target_pairs={{0,24},{1,9},{2,26},{3,11},{4,28},{5,13},{6,30},{7,15},{8,16},{9,1... | collective-permute-start | bytes 3170312 | tf_op jit(solution)/shard_map/ppermute | solution.py:381
  43.3 27.5 %collective-permute-start.6 = (s16[2064,256]{1,0:T(8,128)(2,1)S(1)}, s16[2064,256]{1,0:T(8,128)(2,1)S(1)}, u32[]{:S(2)}, u32[]{:S(2)}) collective-permute-start(s16[2064,256]{1,0:T(8,128)(2,1)S(1)} %get-tuple-element.26), channel_id=1, source_target_pairs={{0,96},{1,33},{2,98},{3,35},{4,100},{5,37},{6,102},{7,39},{8,104},... | collective-permute-start | bytes 3170312 | tf_op jit(solution)/shard_map/ppermute | solution.py:381
  51.1 15.5 %collective-permute-start.12 = (s16[1040,256]{1,0:T(8,128)(2,1)S(1)}, s16[1040,256]{1,0:T(8,128)(2,1)S(1)}, u32[]{:S(2)}, u32[]{:S(2)}) collective-permute-start(s16[1040,256]{1,0:T(8,128)(2,1)S(1)} %late_3_1.1), channel_id=1, source_target_pairs={{0,32},{1,97},{2,34},{3,99},{4,36},{5,101},{6,38},{7,103},{8,40},{... | collective-permute-start | bytes 1597448 | tf_op jit(solution)/shard_map/ppermute | solution.py:381
  54.2 16.6 %collective-permute-start.14 = (s16[1040,256]{1,0:T(8,128)(2,1)S(1)}, s16[1040,256]{1,0:T(8,128)(2,1)S(1)}, u32[]{:S(2)}, u32[]{:S(2)}) collective-permute-start(s16[1040,256]{1,0:T(8,128)(2,1)S(1)} %late_3_0.1), channel_id=1, source_target_pairs={{0,24},{1,9},{2,26},{3,11},{4,28},{5,13},{6,30},{7,15},{8,16},{9,1... | collective-permute-start | bytes 1597448 | tf_op jit(solution)/shard_map/ppermute | solution.py:381
  56.1 21.8 %collective-permute-start.11 = (s16[1040,256]{1,0:T(8,128)(2,1)S(1)}, s16[1040,256]{1,0:T(8,128)(2,1)S(1)}, u32[]{:S(2)}, u32[]{:S(2)}) collective-permute-start(s16[1040,256]{1,0:T(8,128)(2,1)S(1)} %late_2_1.1), channel_id=1, source_target_pairs={{0,32},{1,97},{2,34},{3,99},{4,36},{5,101},{6,38},{7,103},{8,40},{... | collective-permute-start | bytes 1597448 | tf_op jit(solution)/shard_map/ppermute | solution.py:381
  61.9 16.1 %collective-permute-start.8 = (s16[1040,256]{1,0:T(8,128)(2,1)S(1)}, s16[1040,256]{1,0:T(8,128)(2,1)S(1)}, u32[]{:S(2)}, u32[]{:S(2)}) collective-permute-start(s16[1040,256]{1,0:T(8,128)(2,1)S(1)} %late_2_0.1), channel_id=1, source_target_pairs={{0,24},{1,9},{2,26},{3,11},{4,28},{5,13},{6,30},{7,15},{8,16},{9,1... | collective-permute-start | bytes 1597448 | tf_op jit(solution)/shard_map/ppermute | solution.py:381
  67.3 13.4 %collective-permute-start.13 = (s16[1040,256]{1,0:T(8,128)(2,1)S(1)}, s16[1040,256]{1,0:T(8,128)(2,1)S(1)}, u32[]{:S(2)}, u32[]{:S(2)}) collective-permute-start(s16[1040,256]{1,0:T(8,128)(2,1)S(1)} %late_1_1.1), channel_id=1, source_target_pairs={{0,96},{1,33},{2,98},{3,35},{4,100},{5,37},{6,102},{7,39},{8,104},... | collective-permute-start | bytes 1597448 | tf_op jit(solution)/shard_map/ppermute | solution.py:381
  71.6 10.2 %collective-permute-start.15 = (s16[1040,256]{1,0:T(8,128)(2,1)S(1)}, s16[1040,256]{1,0:T(8,128)(2,1)S(1)}, u32[]{:S(2)}, u32[]{:S(2)}) collective-permute-start(s16[1040,256]{1,0:T(8,128)(2,1)S(1)} %late_1_0.1), channel_id=1, source_target_pairs={{0,8},{1,25},{2,10},{3,27},{4,12},{5,29},{6,14},{7,31},{8,0},{9,17... | collective-permute-start | bytes 1597448 | tf_op jit(solution)/shard_map/ppermute | solution.py:381
